TPU v7x, 32 devices: a whole 2x2x4 slice. The times are simulated.
32 devices in a mesh: req: 8 (over y, x, core), exp: 4 (over z).
Axes of the slice: x: 2, y: 2, z: 4, core: 2. Of those that a mesh axis runs over, the one named last changes fastest.
Arguments:
- resid_in: bfloat16 [256, 3584], P(('req', 'exp')), may hold values from -6 to 6
- queries: bfloat16 [256, 3584], P(('req', 'exp')), may hold values from -40 to 40
- fresh_kv: bfloat16 [256, 1024], P(('req', 'exp')), may hold values from -6 to 6
- kv_pool: bfloat16 [8, 4, 32, 16, 1024], P('req', 'exp'), may hold values from -6 to 6
- block_table: int32 [128, 8], P(('req', 'exp')), may hold values from 0 to 31, as said below
- lengths: int32 [128], P(('req', 'exp')), may hold values from 1 to 128, as said below
- mig_source: int32 [8, 4, 2, 4], P('req', 'exp'), may hold values from 0 to 31, as said below
- mig_target: int32 [8, 4, 2, 4], P('req', 'exp'), may hold values from 0 to 31, as said below
- expert_ids: int32 [256, 8], P('req'), may hold values from 0 to 15, all different within a row; in each aligned block of 32 rows (0 to 31, 32 to 63, ...) at most 24 rows name the same one
- gate_values: float32 [256, 8], P('req'), may hold values from 0.2 to 1
- norm_gain: bfloat16 [3584], replicated, may hold values from 0.5 to 1.5
- w_in: bfloat16 [4, 8, 3584, 1024], P('exp', 'req'), may hold values from -0.09375 to 0.09375
- w_out: bfloat16 [4, 8, 1024, 3584], P('exp', 'req'), may hold values from -0.125 to 0.125
Outputs:
- mixed: bfloat16 [256, 3584], P(('req', 'exp'))
Inputs may be any that keep to these rules, and one draw needn't show every extreme that they name: `block_table`: the entries of the 4 rows of one device are distinct pages of that device's pool. `lengths`: A request that arrives by migration has more than (3) * 16 cached positions. `mig_target`: on every device exactly one request arrives from req index - 1 and one from index + 1 (around the loop); [r, e, 0, i] is the page that takes page i of the request from index - 1, [r, e, 1, i] of the one from index + 1; they are the first 4 entries of that request's block-table row. `mig_source`: [r, e, 0, i] is the pool page sent as page i to index + 1, [r, e, 1, i] to index - 1; the 8 pages of a device are distinct and belong to no request that stays on it. `expert_ids`: each row names 8 different experts; among the 32 tokens of one index of req no expert is named by more than 24 rows.
All inputs are finite; a program needn't handle non-finite values.
Results may differ from a plain program's by a relative error of at most 0.012.
Values may be sent and summed in bfloat16 or wider, within the bound.
No kernel may reach another device: no remote copies, remote signals or barrier semaphores. Data moves between devices by JAX's collectives and lax.ppermute only.
A program may use at most 64 MiB of HBM per device.

v0:
```python
import jax
import jax.numpy as jnp
from jax import lax
from jax.sharding import PartitionSpec as P

HEADS = 28
KV_HEADS = 4
HEAD_DIM = 128
EXP_DEV = 4
CAP = 24


neg_big = -1e30
norm_eps = 1e-06


def with_halo(block, sides, width):
    for axis, dim in sides:
        count = lax.axis_size(axis)
        forward = [(i, i + 1) for i in range(count - 1)]
        forward.append((count - 1, 0))
        backward = [(target, source) for source, target in forward]
        low = lax.ppermute(
            lax.slice_in_dim(block, block.shape[dim] - width, None, axis=dim), axis, forward
        )
        high = lax.ppermute(lax.slice_in_dim(block, 0, width, axis=dim), axis, backward)
        block = jnp.concatenate([low, block, high], axis=dim)
    return block


def partial_attention(query_grid, key_rows, visible):
    request_count = key_rows.shape[0]
    span = key_rows.shape[1]
    key_width = KV_HEADS * HEAD_DIM
    key_part = key_rows[:, :, :key_width].reshape(request_count, span, KV_HEADS, HEAD_DIM)
    value_part = (
        key_rows[:, :, key_width:]
        .reshape(request_count, span, KV_HEADS, HEAD_DIM)
        .astype(jnp.float32)
    )
    scores = jnp.einsum(
        "rdkgh,rpkh->rdkgp", query_grid, key_part, preferred_element_type=jnp.float32
    ) * HEAD_DIM ** (-0.5)
    live = visible[:, :, None, None, :]
    scores = jnp.where(live, scores, neg_big)
    highest = jnp.max(scores, axis=-1)
    weights = jnp.where(live, jnp.exp(scores - highest[..., None]), 0.0)
    weight_sum = jnp.sum(weights, axis=-1)
    summed = jnp.einsum("rdkgp,rpkh->rdkgh", weights, value_part, precision=lax.Precision.HIGHEST)
    return (highest, weight_sum, summed)


def body(
    resid_in,
    queries,
    fresh_kv,
    kv_pool,
    block_table,
    lengths,
    mig_source,
    mig_target,
    expert_ids,
    gate_values,
    norm_gain,
    w_in,
    w_out,
):
    request_count = block_table.shape[0]
    table_width = block_table.shape[1]
    page_tokens = kv_pool.shape[3]
    kv_width = kv_pool.shape[4]
    cache_span = table_width * page_tokens
    token_count = resid_in.shape[0]
    draft_count = token_count // request_count
    model_width = resid_in.shape[1]
    moved = mig_source.shape[3]
    pool_pages = kv_pool[0, 0]
    sources = mig_source[0, 0]
    target_pairs = mig_target[0, 0]
    outgoing = jnp.concatenate([pool_pages[sources[1]], pool_pages[sources[0]]], axis=0)
    targets = jnp.concatenate([target_pairs[0], target_pairs[1]], axis=0)
    extended = with_halo(outgoing, (("req", 0),), moved)
    arrivals = jnp.concatenate([extended[:moved], extended[-moved:]], axis=0)
    query_grid = queries.reshape(request_count, draft_count, KV_HEADS, HEADS // KV_HEADS, HEAD_DIM)
    fresh_rows = fresh_kv.reshape(request_count, draft_count, kv_width)
    position = jnp.arange(cache_span)
    cache_visible = jnp.broadcast_to(
        position[None, None, :] < lengths[:, None, None], (request_count, draft_count, cache_span)
    )
    draft_index = jnp.arange(draft_count)
    draft_visible = jnp.broadcast_to(
        draft_index[None, :] <= draft_index[:, None], (request_count, draft_count, draft_count)
    )
    pool_after = pool_pages.at[targets].set(arrivals)
    cache_rows = pool_after[block_table].reshape(request_count, cache_span, kv_width)
    parts = partial_attention(
        query_grid,
        jnp.concatenate([cache_rows, fresh_rows], axis=1),
        jnp.concatenate([cache_visible, draft_visible], axis=2),
    )
    attention = (parts[2] / parts[1][..., None]).reshape(token_count, model_width)
    residual = resid_in.astype(jnp.float32) + attention
    inv_rms = lax.rsqrt(jnp.mean(residual * residual, axis=1, keepdims=True) + norm_eps)
    normed = (residual * inv_rms * norm_gain.astype(jnp.float32)).astype(jnp.bfloat16)
    local_ids = lax.axis_index("exp") * EXP_DEV + jnp.arange(EXP_DEV)
    matches = expert_ids[None, :, :] == local_ids[:, None, None]
    is_named = jnp.any(matches, axis=2)
    gate_local = jnp.sum(jnp.where(matches, gate_values[None, :, :], 0.0), axis=2)
    slot_index = jnp.cumsum(is_named.astype(jnp.int32), axis=1) - 1
    placement = is_named[:, None, :] & (slot_index[:, None, :] == jnp.arange(CAP)[None, :, None])
    slot_gate = jnp.sum(jnp.where(placement, gate_local[:, None, :], 0.0), axis=2)
    slot_select = placement.astype(jnp.bfloat16)
    columns = slot_select
    packed = jnp.einsum(
        "kct,td->kcd",
        columns,
        lax.all_gather(normed, "exp", axis=0, tiled=True),
        preferred_element_type=jnp.float32,
    )
    packed = packed.astype(jnp.bfloat16)
    group_size = lax.axis_size("req") // EXP_DEV
    outbound = jnp.repeat(packed, group_size, axis=0)
    inner_weights = w_in[0, 0]
    outer_weights = w_out[0, 0]
    inbound = lax.all_to_all(outbound, "req", split_axis=0, concat_axis=0, tiled=True)
    hidden = jnp.einsum("scd,df->scf", inbound, inner_weights, preferred_element_type=jnp.float32)
    activated = jax.nn.silu(hidden).astype(jnp.bfloat16)
    returned = lax.all_to_all(
        jnp.einsum(
            "scf,fd->scd", activated, outer_weights, preferred_element_type=jnp.float32
        ).astype(jnp.bfloat16),
        "req",
        split_axis=0,
        concat_axis=0,
        tiled=True,
    )
    expert_out = jnp.sum(
        returned.reshape(EXP_DEV, group_size, CAP, model_width).astype(jnp.float32), axis=1
    )
    weighted = expert_out * slot_gate[:, :, None]
    slot_select_wide = placement.astype(jnp.float32)
    columns = slot_select_wide
    expert_mix = lax.psum_scatter(
        jnp.einsum("kct,kcd->td", columns, weighted, precision=lax.Precision.HIGHEST).astype(
            jnp.bfloat16
        ),
        "exp",
        scatter_dimension=0,
        tiled=True,
    ).astype(jnp.float32)
    return (residual + expert_mix).astype(jnp.bfloat16)


def solution(mesh):
    placed = (
        P(("req", "exp"), None),
        P(("req", "exp"), None),
        P(("req", "exp"), None),
        P("req", "exp", None, None, None),
        P(("req", "exp"), None),
        P(("req", "exp")),
        P("req", "exp", None, None),
        P("req", "exp", None, None),
        P("req", None),
        P("req", None),
        P(),
        P("exp", "req", None, None),
        P("exp", "req", None, None),
    )
    return jax.shard_map(
        body, mesh=mesh, in_specs=placed, out_specs=P(("req", "exp"), None), check_vma=False
    )
```

profile of v0, /device:TPU:0, one launch (start us, length us, event | category | flops | bytes accessed | tf_op | source)
XLA Modules:
  0.0 116.6 jit_solution(11707276706037209845)
XLA Ops:
  6.6 1.3 %copy.45 = bf16[1,1,32,16,1024]{4,3,2,1,0:T(8,128)(2,1)S(1)} copy(bf16[1,1,32,16,1024]{4,3,2,1,0:T(8,128)(2,1)} %param.16) | data formatting | bytes 2097152
  7.9 0.6 gather_fusion
  8.5 0.5 collective-permute-start
  9.0 0.6 gather_fusion.1
  9.5 3.0 %collective-permute-start.1 = (bf16[4,16,1024]{2,1,0:T(8,128)(2,1)S(1)}, bf16[4,16,1024]{2,1,0:T(8,128)(2,1)S(1)}, u32[]{:S(2)}, u32[]{:S(2)}) collective-permute-start(bf16[4,16,1024]{2,1,0:T(8,128)(2,1)S(1)} %gather_fusion.1), channel_id=1, source_target_pairs={{4,0},{8,4},{12,8},{16,12},{20,16},{24,20},{28,24},{0,28},{5,1},{9... | collective-permute-start | bytes 393224 | tf_op jit(solution)/shard_map/ppermute | solution.py:26
  12.7 0.1 compare_reduce_fusion
  12.8 0.2 reduce_window_sum.11
  13.1 0.1 reshape.228
  13.3 1.2 %collective-permute-done = bf16[4,16,1024]{2,1,0:T(8,128)(2,1)S(1)} collective-permute-done((bf16[4,16,1024]{2,1,0:T(8,128)(2,1)S(1)}, bf16[4,16,1024]{2,1,0:T(8,128)(2,1)S(1)}, u32[]{:S(2)}, u32[]{:S(2)}) %collective-permute-start) | collective-permute-done | bytes 131104 | tf_op jit(solution)/shard_map/ppermute | solution.py:23
  14.5 0.5 collective-permute-done.1
  15.1 0.8 scatter_fusion
  15.8 0.6 gather_fusion.2
  16.5 0.2 reshape.227
  16.7 0.2 reshape.226
  16.9 0.5 fusion.40
  17.4 0.2 fusion.22
  17.6 0.6 fusion.11
  18.3 0.1 multiply_reduce_fusion
  18.4 0.1 multiply_convert_fusion.1
  18.5 15.1 %all_gather.3 = bf16[32,3584]{1,0:T(8,128)(2,1)S(1)} all-gather(bf16[8,3584]{1,0:T(8,128)(2,1)S(1)} %multiply_convert_fusion.1), channel_id=1, replica_groups=mesh['req'=8,'exp'=4] {'exp'}, dimensions={0}, use_global_device_ids=true | all-gather | bytes 286720 | tf_op jit(solution)/shard_map/all_gather | solution.py:117
  33.7 0.3 convolution_convert_fusion
  34.0 0.1 broadcast_in_dim.82
  34.1 21.5 %all_to_all.10 = bf16[8,24,3584]{2,1,0:T(8,128)(2,1)S(1)} all-to-all(bf16[8,24,3584]{2,1,0:T(8,128)(2,1)S(1)} %bitcast.57), channel_id=1, replica_groups=mesh['req'=8,'exp'=4] {'req'}, dimensions={0} | all-to-all | bytes 2752512 | tf_op jit(solution)/shard_map/all_to_all | solution.py:125
  55.6 9.3 %fusion.4 = bf16[8,24,3584]{2,1,0:T(8,128)(2,1)} fusion(bf16[1,1,1024,3584]{3,2,1,0:T(8,128)(2,1)} %param.25, bf16[8,24,3584]{2,1,0:T(8,128)(2,1)S(1)} %all_to_all.10, bf16[1,1,3584,1024]{3,2,1,0:T(8,128)(2,1)} %param.24), kind=kOutput, calls=%fused_computation.8 | convolution fusion | flops 2820243456 | bytes 17432576 | tf_op jit(solution)/shard_map/scf,fd->scd/dot_general | solution.py:129
  65.0 3.7 %all-to-all-start.1 = ((bf16[8,24,3584]{2,1,0:T(8,128)(2,1)}), bf16[8,24,3584]{2,1,0:T(8,128)(2,1)S(1)}, u32[]{:S(2)}, u32[]{:S(2)}) async-start(bf16[8,24,3584]{2,1,0:T(8,128)(2,1)} %fusion.4), calls=%async_computation.1 | async-start | bytes 2752512 | tf_op jit(solution)/shard_map/all_to_all | solution.py:128
  68.7 0.1 fusion.34
  68.8 0.1 select_reduce_fusion
  68.9 18.6 %all-to-all-done.1 = bf16[8,24,3584]{2,1,0:T(8,128)(2,1)S(1)} async-done(((bf16[8,24,3584]{2,1,0:T(8,128)(2,1)}), bf16[8,24,3584]{2,1,0:T(8,128)(2,1)S(1)}, u32[]{:S(2)}, u32[]{:S(2)}) %all-to-all-start.1) | async-done | bytes 1376288 | tf_op jit(solution)/shard_map/all_to_all | solution.py:128
  87.5 0.2 convert_reduce_fusion
  87.7 1.4 %fusion.7 = bf16[32,3584]{1,0:T(8,128)(2,1)} fusion(f32[4,24,3584]{2,1,0:T(8,128)S(1)} %convert_reduce_fusion, f32[4,24]{1,0:T(4,128)S(1)} %select_reduce_fusion, s32[4,32]{1,0:T(4,128)S(1)} %broadcast_add_fusion, pred[4,32]{1,0:T(4,128)(4,1)S(1)} %compare_reduce_fusion), kind=kOutput, calls=%fused_computation.11 | convolution fusion | flops 132585472 | bytes 1606656 | tf_op jit(solution)/shard_map/kct,kcd->td/dot_general | solution.py:144
  89.2 19.1 %reduce-scatter.2.cloned.1.call-done = bf16[8,3584]{1,0:T(8,128)(2,1)} async-done(((bf16[32,3584]{1,0:T(8,128)(2,1)}), bf16[8,3584]{1,0:T(8,128)(2,1)}) %reduce-scatter.2.cloned.1.call-update) | async-done | bytes 57360 | tf_op jit(solution)/shard_map/reduce_scatter | solution.py:143
  108.3 1.5 %add_convert_fusion = bf16[8,3584]{1,0:T(8,128)(2,1)} fusion(bf16[8,3584]{1,0:T(8,128)(2,1)} %reduce-scatter.2.cloned.1.call-done, f32[8,3584]{1,0:T(8,128)S(1)} %reshape.229, bf16[8,3584]{1,0:T(8,128)(2,1)S(1)} %copy-done), kind=kLoop, calls=%fused_computation.35 | loop fusion | flops 143360 | bytes 286720 | tf_op jit(solution)/shard_map/convert_element_type | solution.py:151
  (45 shorter events, 0.6 us)
Async XLA Ops:
  6.5 6.6 %copy-start.1 = (bf16[8,3584]{1,0:T(8,128)(2,1)S(1)}, bf16[8,3584]{1,0:T(8,128)(2,1)}, u32[]{:S(2)}) copy-start(bf16[8,3584]{1,0:T(8,128)(2,1)} %param.14) | copy-start | bytes 172036
  6.5 6.6 %copy-start.3 = (bf16[8,1024]{1,0:T(8,128)(2,1)S(1)}, bf16[8,1024]{1,0:T(8,128)(2,1)}, u32[]{:S(2)}) copy-start(bf16[8,1024]{1,0:T(8,128)(2,1)} %param.15) | copy-start | bytes 49156
  6.5 6.0 %copy-start.6 = (s32[4,8]{1,0:T(4,128)S(1)}, s32[4,8]{1,0:T(4,128)}, u32[]{:S(2)}) copy-start(s32[4,8]{1,0:T(4,128)} %param.17) | copy-start | bytes 388
  6.5 6.1 %copy-start.9 = (s32[4]{0:T(128)S(1)}, s32[4]{0:T(128)}, u32[]{:S(2)}) copy-start(s32[4]{0:T(128)} %param.18) | copy-start | bytes 52
  6.5 1.4 %copy-start.7 = (s32[1,1,2,4]{3,2,1,0:T(2,128)S(1)}, s32[1,1,2,4]{3,2,1,0:T(2,128)}, u32[]{:S(2)}) copy-start(s32[1,1,2,4]{3,2,1,0:T(2,128)} %param.19) | copy-start | bytes 100
  6.5 6.0 %copy-start.8 = (s32[1,1,2,4]{3,2,1,0:T(2,128)S(1)}, s32[1,1,2,4]{3,2,1,0:T(2,128)}, u32[]{:S(2)}) copy-start(s32[1,1,2,4]{3,2,1,0:T(2,128)} %param.20) | copy-start | bytes 100
  6.6 6.2 %copy-start.2 = (s32[32,8]{0,1:T(8,128)S(1)}, s32[32,8]{0,1:T(8,128)}, u32[]{:S(2)}) copy-start(s32[32,8]{0,1:T(8,128)} %param.21) | copy-start | bytes 3076
  6.6 6.7 %copy-start.4 = (bf16[3584]{0:T(1024)(128)(2,1)S(1)}, bf16[3584]{0:T(1024)(128)(2,1)}, u32[]{:S(2)}) copy-start(bf16[3584]{0:T(1024)(128)(2,1)} %param.23) | copy-start | bytes 21508
  8.5 6.0 %collective-permute-start = (bf16[4,16,1024]{2,1,0:T(8,128)(2,1)S(1)}, bf16[4,16,1024]{2,1,0:T(8,128)(2,1)S(1)}, u32[]{:S(2)}, u32[]{:S(2)}) collective-permute-start(bf16[4,16,1024]{2,1,0:T(8,128)(2,1)S(1)} %gather_fusion), channel_id=1, source_target_pairs={{0,4},{4,8},{8,12},{12,16},{16,20},{20,24},{24,28},{28,0},{1,5},{5... | collective-permute-start | bytes 393224 | tf_op jit(solution)/shard_map/ppermute | solution.py:23
  9.5 5.5 %collective-permute-start.1 = (bf16[4,16,1024]{2,1,0:T(8,128)(2,1)S(1)}, bf16[4,16,1024]{2,1,0:T(8,128)(2,1)S(1)}, u32[]{:S(2)}, u32[]{:S(2)}) collective-permute-start(bf16[4,16,1024]{2,1,0:T(8,128)(2,1)S(1)} %gather_fusion.1), channel_id=1, source_target_pairs={{4,0},{8,4},{12,8},{16,12},{20,16},{24,20},{28,24},{0,28},{5,1},{9... | collective-permute-start | bytes 393224 | tf_op jit(solution)/shard_map/ppermute | solution.py:26
  17.4 0.9 copy-start
  65.0 3.8 %copy-start.5 = (f32[32,8]{0,1:T(8,128)S(1)}, f32[32,8]{0,1:T(8,128)}, u32[]{:S(2)}) copy-start(f32[32,8]{0,1:T(8,128)} %param.22) | copy-start | bytes 3076
  65.0 22.6 %all-to-all-start.1 = ((bf16[8,24,3584]{2,1,0:T(8,128)(2,1)}), bf16[8,24,3584]{2,1,0:T(8,128)(2,1)S(1)}, u32[]{:S(2)}, u32[]{:S(2)}) async-start(bf16[8,24,3584]{2,1,0:T(8,128)(2,1)} %fusion.4), calls=%async_computation.1 | async-start | bytes 2752512 | tf_op jit(solution)/shard_map/all_to_all | solution.py:128
  68.7 39.6 %reduce-scatter.2.cloned.1.call-start = ((), (), s32[]{:S(2)}) async-start(), calls=%async_computation.3 | async-start | bytes 286720 | tf_op jit(solution)/shard_map/reduce_scatter | solution.py:143
Sparse Core Ops, SparseCore 0:
  89.3 18.9 reduce-scatter.1
where the time goes:
time: 117 us
  waiting for transfers between devices  39.4 us (34%)
  blocking collectives  36.7 us (31%)
  between operations  13.6 us (12%)
  matrix products  12.2 us (10%)
  starting transfers between devices  7.21 us (6%)
  local copies, waits for them, and re-layouts  4.5 us (4%)
  other arithmetic  2.96 us (3%)
    all_to_all x1, blocking collectives, body(): lax.all_to_all(outbound, 'req', split_axis=0, concat_axis=0, tiled=True)  21.5 us
    reduce_scatter x1, waiting for transfers between devices, body(): lax.psum_scatter(jnp.einsum('kct,kcd->td', columns, weighted, precision=l...  19.1 us
    all_to_all x1, waiting for transfers between devices, body(): lax.all_to_all(jnp.einsum('scf,fd->scd', activated, outer_weights, prefer...  18.6 us
    all_gather x1, blocking collectives, body(): lax.all_gather(normed, 'exp', axis=0, tiled=True)  15.1 us
    dot_general x1, matrix products, body(): jnp.einsum('scf,fd->scd', activated, outer_weights, preferred_element_typ...  9.35 us
    all_to_all x1, starting transfers between devices, body(): lax.all_to_all(jnp.einsum('scf,fd->scd', activated, outer_weights, prefer...  3.7 us
    ppermute x1, starting transfers between devices, with_halo(): lax.ppermute(lax.slice_in_dim(block, 0, width, axis=dim), axis, backward)  2.96 us
  transfers between devices with their start and end apart: 4, of which 4 were waited for; matrix products, arithmetic and copies ran while one was open for 1% of the time, Pallas kernels for 0%

commit v1 on v0

v1 whole, which is shorter than its diff:
```python
import jax
import jax.numpy as jnp
from jax import lax
from jax.sharding import PartitionSpec as P

HEADS = 28
KV_HEADS = 4
HEAD_DIM = 128
EXP_DEV = 4
CAP = 24


neg_big = -1e30
norm_eps = 1e-06


def partner_steps(count):
    if count & (count - 1):
        raise ValueError("axis size")
    return [[i ^ k for i in range(count)] for k in range(1, count)]


def partner_of(index, steps):
    table = jnp.array([list(range(len(steps[0])))] + steps, dtype=jnp.int32)
    return table[:, index]


def ring_pages(block, axis, up):
    count = lax.axis_size(axis)
    pairs = [(i, (i + 1) % count) for i in range(count)]
    if not up:
        pairs = [(target, source) for source, target in pairs]
    return lax.ppermute(block, axis, pairs)


def swap_plane(block, step, group_size):
    pairs = [(q * group_size + g, p * group_size + g) for q, p in enumerate(step) for g in range(group_size)]
    return lax.ppermute(block, "req", pairs)


def swap_group(block, step, group_size):
    pairs = [(q * group_size + g, q * group_size + p) for q in range(EXP_DEV) for g, p in enumerate(step)]
    return lax.ppermute(block, "req", pairs)


def swap_exp(block, step):
    return lax.ppermute(block, "exp", list(enumerate(step)))


def partial_attention(query_grid, key_rows, visible):
    request_count = key_rows.shape[0]
    span = key_rows.shape[1]
    key_width = KV_HEADS * HEAD_DIM
    key_part = key_rows[:, :, :key_width].reshape(request_count, span, KV_HEADS, HEAD_DIM)
    value_part = (
        key_rows[:, :, key_width:]
        .reshape(request_count, span, KV_HEADS, HEAD_DIM)
        .astype(jnp.float32)
    )
    scores = jnp.einsum(
        "rdkgh,rpkh->rdkgp", query_grid, key_part, preferred_element_type=jnp.float32
    ) * HEAD_DIM ** (-0.5)
    live = visible[:, :, None, None, :]
    scores = jnp.where(live, scores, neg_big)
    highest = jnp.max(scores, axis=-1)
    weights = jnp.where(live, jnp.exp(scores - highest[..., None]), 0.0)
    weight_sum = jnp.sum(weights, axis=-1)
    summed = jnp.einsum("rdkgp,rpkh->rdkgh", weights, value_part, precision=lax.Precision.HIGHEST)
    return (highest, weight_sum, summed)


def body(
    resid_in,
    queries,
    fresh_kv,
    kv_pool,
    block_table,
    lengths,
    mig_source,
    mig_target,
    expert_ids,
    gate_values,
    norm_gain,
    w_in,
    w_out,
):
    request_count = block_table.shape[0]
    table_width = block_table.shape[1]
    page_tokens = kv_pool.shape[3]
    kv_width = kv_pool.shape[4]
    cache_span = table_width * page_tokens
    token_count = resid_in.shape[0]
    draft_count = token_count // request_count
    model_width = resid_in.shape[1]
    exp_count = lax.axis_size("exp")
    group_size = lax.axis_size("req") // EXP_DEV
    plane_steps = partner_steps(EXP_DEV)
    group_steps = partner_steps(group_size)
    exp_steps = partner_steps(exp_count)

    pool_pages = kv_pool[0, 0]
    sources = mig_source[0, 0]
    target_pairs = mig_target[0, 0]
    from_low = ring_pages(pool_pages[sources[0]], "req", True)
    from_high = ring_pages(pool_pages[sources[1]], "req", False)
    arrivals = jnp.concatenate([from_low, from_high], axis=0)
    targets = jnp.concatenate([target_pairs[0], target_pairs[1]], axis=0)

    query_grid = queries.reshape(request_count, draft_count, KV_HEADS, HEADS // KV_HEADS, HEAD_DIM)
    fresh_rows = fresh_kv.reshape(request_count, draft_count, kv_width)
    position = jnp.arange(cache_span)
    cache_visible = jnp.broadcast_to(
        position[None, None, :] < lengths[:, None, None], (request_count, draft_count, cache_span)
    )
    draft_index = jnp.arange(draft_count)
    draft_visible = jnp.broadcast_to(
        draft_index[None, :] <= draft_index[:, None], (request_count, draft_count, draft_count)
    )
    pool_after = pool_pages.at[targets].set(arrivals)
    cache_rows = pool_after[block_table].reshape(request_count, cache_span, kv_width)
    parts = partial_attention(
        query_grid,
        jnp.concatenate([cache_rows, fresh_rows], axis=1),
        jnp.concatenate([cache_visible, draft_visible], axis=2),
    )
    attention = (parts[2] / parts[1][..., None]).reshape(token_count, model_width)
    residual = resid_in.astype(jnp.float32) + attention
    inv_rms = lax.rsqrt(jnp.mean(residual * residual, axis=1, keepdims=True) + norm_eps)
    normed = (residual * inv_rms * norm_gain.astype(jnp.float32)).astype(jnp.bfloat16)

    exp_order = partner_of(lax.axis_index("exp"), exp_steps)
    plane_order = partner_of(lax.axis_index("req") // group_size, plane_steps)
    ids = expert_ids.reshape(exp_count, token_count, -1)[exp_order].reshape(expert_ids.shape)
    gates = gate_values.reshape(exp_count, token_count, -1)[exp_order].reshape(gate_values.shape)
    local_ids = lax.axis_index("exp") * EXP_DEV + plane_order
    matches = ids[None, :, :] == local_ids[:, None, None]
    is_named = jnp.any(matches, axis=2)
    gate_local = jnp.sum(jnp.where(matches, gates[None, :, :], 0.0), axis=2)
    slot_index = jnp.cumsum(is_named.astype(jnp.int32), axis=1) - 1
    placement = is_named[:, None, :] & (slot_index[:, None, :] == jnp.arange(CAP)[None, :, None])
    columns = placement.astype(jnp.bfloat16)
    gate_columns = jnp.where(placement, gate_local[:, None, :], 0.0)

    gathered = jnp.concatenate([normed] + [swap_exp(normed, step) for step in exp_steps], axis=0)
    packed = jnp.einsum(
        "kct,td->kcd", columns, gathered, preferred_element_type=jnp.float32
    ).astype(jnp.bfloat16)
    mine = jnp.concatenate(
        [packed[:1]] + [swap_plane(packed[k + 1 : k + 2], step, group_size) for k, step in enumerate(plane_steps)],
        axis=0,
    ).reshape(EXP_DEV * CAP, model_width)
    inbound = jnp.concatenate([mine] + [swap_group(mine, step, group_size) for step in group_steps], axis=0)

    hidden = jnp.dot(inbound, w_in[0, 0], preferred_element_type=jnp.float32)
    activated = jax.nn.silu(hidden).astype(jnp.bfloat16)
    partials = (
        jnp.dot(activated, w_out[0, 0], preferred_element_type=jnp.float32)
        .astype(jnp.bfloat16)
        .reshape(group_size, EXP_DEV, CAP, model_width)
    )

    summed = partials[0].astype(jnp.float32)
    for k, step in enumerate(group_steps):
        summed = summed + swap_group(partials[k + 1], step, group_size).astype(jnp.float32)
    summed = summed.astype(jnp.bfloat16)
    returned = jnp.concatenate(
        [summed[:1]] + [swap_plane(summed[k + 1 : k + 2], step, group_size) for k, step in enumerate(plane_steps)],
        axis=0,
    )
    mix = jnp.einsum(
        "kct,kcd->td", gate_columns, returned.astype(jnp.float32), precision=lax.Precision.HIGHEST
    )
    blocks = mix.reshape(exp_count, token_count, model_width)
    result = residual + blocks[0]
    blocks = blocks.astype(jnp.bfloat16)
    for k, step in enumerate(exp_steps):
        result = result + swap_exp(blocks[k + 1], step).astype(jnp.float32)
    return result.astype(jnp.bfloat16)


def solution(mesh):
    placed = (
        P(("req", "exp"), None),
        P(("req", "exp"), None),
        P(("req", "exp"), None),
        P("req", "exp", None, None, None),
        P(("req", "exp"), None),
        P(("req", "exp")),
        P("req", "exp", None, None),
        P("req", "exp", None, None),
        P("req", None),
        P("req", None),
        P(),
        P("exp", "req", None, None),
        P("exp", "req", None, None),
    )
    return jax.shard_map(
        body, mesh=mesh, in_specs=placed, out_specs=P(("req", "exp"), None), check_vma=False
    )
```

time: 117 us -> 68.6 us (0.59)
  blocking collectives: 36.7 us -> 0 us
  between operations: 13.6 us -> 0.32 us
  starting transfers between devices: 7.21 us -> 19.5 us
  waiting for transfers between devices: 39.4 us -> 30.3 us
  matrix products: 12.2 us -> 10.2 us
  local copies, waits for them, and re-layouts: 4.5 us -> 6 us
    ppermute x2 -> x16, waiting for transfers between devices: 1.73 us -> 30.3 us  [the longest x6 14.2 us: swap_plane(): return lax.ppermute(block, 'req', pairs)]
    all_to_all x1 -> x0, blocking collectives: 21.5 us -> none  [body(): lax.all_to_all(outbound, 'req', split_axis=0, concat_axis=0, tiled=True)]
    reduce_scatter x1 -> x0, waiting for transfers between devices: 19.1 us -> none  [body(): lax.psum_scatter(jnp.einsum('kct,kcd->td', columns, weighted, precision=l...]
    all_to_all x1 -> x0, waiting for transfers between devices: 18.6 us -> none  [body(): lax.all_to_all(jnp.einsum('scf,fd->scd', activated, outer_weights, prefer...]
    ppermute x2 -> x16, starting transfers between devices: 3.46 us -> 19.5 us  [the longest x6 8.6 us: swap_exp(): return lax.ppermute(block, 'exp', list(enumerate(step)))]
    all_gather x1 -> x0, blocking collectives: 15.1 us -> none  [body(): lax.all_gather(normed, 'exp', axis=0, tiled=True)]
    all_to_all x1 -> x0, starting transfers between devices: 3.7 us -> none  [body(): lax.all_to_all(jnp.einsum('scf,fd->scd', activated, outer_weights, prefer...]
    dot_general x3, matrix products: 11.1 us -> 9.11 us  [the longest x1 8.34 us: body(): jnp.dot(activated, w_out[0, 0], preferred_element_type=jnp.float32)]
  transfers between devices with their start and end apart: 4 -> 16, of which waited for: 4 -> 14; matrix products, arithmetic and copies ran while one was open for 1% -> 4% of each run, Pallas kernels for 0% -> 0%
where the time goes in v1:
time: 68.6 us; the launch traced here: 68.4 us
  waiting for transfers between devices  30.3 us (44%)
  starting transfers between devices  19.5 us (28%)
  matrix products  10.2 us (15%)
  local copies, waits for them, and re-layouts  6 us (9%)
  other arithmetic  2.13 us (3%)
    ppermute x6, waiting for transfers between devices, swap_plane(): return lax.ppermute(block, 'req', pairs)  14.2 us
    ppermute x6, waiting for transfers between devices, swap_exp(): return lax.ppermute(block, 'exp', list(enumerate(step)))  10.9 us
    ppermute x6, starting transfers between devices, swap_exp(): return lax.ppermute(block, 'exp', list(enumerate(step)))  8.6 us
    dot_general x1, matrix products, body(): jnp.dot(activated, w_out[0, 0], preferred_element_type=jnp.float32)  8.34 us
    ppermute x6, starting transfers between devices, swap_plane(): return lax.ppermute(block, 'req', pairs)  7.11 us
    ppermute x2, waiting for transfers between devices, swap_group(): return lax.ppermute(block, 'req', pairs)  4.12 us
    ppermute x2, starting transfers between devices, ring_pages(): return lax.ppermute(block, axis, pairs)  3.45 us
    unnamed x25, local copies, waits for them, and re-layouts  1.52 us
  transfers between devices with their start and end apart: 16, of which 14 were waited for; matrix products, arithmetic and copies ran while one was open for 4% of the time, Pallas kernels for 0%

profile of v1, /device:TPU:0, one launch (start us, length us, event | category | flops | bytes accessed | tf_op | source)
XLA Modules:
  0.0 68.4 jit_solution(9415948505585978573)
XLA Ops:
  0.1 1.3 %copy.51 = bf16[1,1,32,16,1024]{4,3,2,1,0:T(8,128)(2,1)S(1)} copy(bf16[1,1,32,16,1024]{4,3,2,1,0:T(8,128)(2,1)} %param.18) | data formatting | bytes 2097152
  1.4 0.6 gather_fusion
  2.5 0.6 gather_fusion.1
  3.0 3.0 %collective-permute-start.1 = (bf16[4,16,1024]{2,1,0:T(8,128)(2,1)S(1)}, bf16[4,16,1024]{2,1,0:T(8,128)(2,1)S(1)}, u32[]{:S(2)}, u32[]{:S(2)}) collective-permute-start(bf16[4,16,1024]{2,1,0:T(8,128)(2,1)S(1)} %gather_fusion.1), channel_id=1, source_target_pairs={{4,0},{8,4},{12,8},{16,12},{20,16},{24,20},{28,24},{0,28},{5,1},{9... | collective-permute-start | bytes 393224 | tf_op jit(solution)/shard_map/ppermute | solution.py:33
  6.3 0.5 gather_fusion.3
  8.5 0.8 %scatter_fusion = bf16[32,16,1024]{2,1,0:T(8,128)(2,1)S(1)} fusion(bf16[32,16,1024]{2,1,0:T(8,128)(2,1)S(1)} %bitcast.58, s32[8]{0:T(128)S(1)} %fusion.59, bf16[8,16,1024]{2,1,0:T(8,128)(2,1)S(1)} %pad_maximum_fusion.2), kind=kCustom, calls=%fused_computation.5 | custom fusion | bytes 786464 | tf_op jit(solution)/shard_map/scatter | solution.py:119
  9.3 0.6 gather_fusion.2
  11.1 0.6 fusion.13
  12.0 4.4 %collective-permute-start.4 = (bf16[8,3584]{1,0:T(8,128)(2,1)S(1)}, bf16[8,3584]{1,0:T(8,128)(2,1)S(1)}, u32[]{:S(2)}, u32[]{:S(2)}) collective-permute-start(bf16[8,3584]{1,0:T(8,128)(2,1)S(1)} %multiply_convert_fusion.1), channel_id=1, source_target_pairs={{0,3},{1,2},{2,1},{3,0},{4,7},{5,6},{6,5},{7,4},{8,11},{9,10},{10,... | collective-permute-start | bytes 172040 | tf_op jit(solution)/shard_map/ppermute | solution.py:47
  16.4 0.6 collective-permute-start.2
  17.1 2.1 %collective-permute-done.4 = bf16[8,3584]{1,0:T(8,128)(2,1)S(1)} collective-permute-done((bf16[8,3584]{1,0:T(8,128)(2,1)S(1)}, bf16[8,3584]{1,0:T(8,128)(2,1)S(1)}, u32[]{:S(2)}, u32[]{:S(2)}) %collective-permute-start.4) | collective-permute-done | bytes 57376 | tf_op jit(solution)/shard_map/ppermute | solution.py:47
  19.2 3.0 %collective-permute-done.3 = bf16[8,3584]{1,0:T(8,128)(2,1)S(1)} collective-permute-done((bf16[8,3584]{1,0:T(8,128)(2,1)S(1)}, bf16[8,3584]{1,0:T(8,128)(2,1)S(1)}, u32[]{:S(2)}, u32[]{:S(2)}) %collective-permute-start.3) | collective-permute-done | bytes 57376 | tf_op jit(solution)/shard_map/ppermute | solution.py:47
  22.6 1.7 %collective-permute-start.7 = (bf16[1,24,3584]{2,1,0:T(8,128)(2,1)S(1)}, bf16[1,24,3584]{2,1,0:T(8,128)(2,1)S(1)}, u32[]{:S(2)}, u32[]{:S(2)}) collective-permute-start(bf16[1,24,3584]{2,1,0:T(8,128)(2,1)S(1)} %get-tuple-element.14), channel_id=1, source_target_pairs={{0,24},{4,28},{8,16},{12,20},{16,8},{20,12},{24,0},{28,4},{1,25},{... | collective-permute-start | bytes 516104 | tf_op jit(solution)/shard_map/ppermute | solution.py:38
  24.3 0.6 collective-permute-start.6
  24.9 1.2 %collective-permute-start.5 = (bf16[1,24,3584]{2,1,0:T(8,128)(2,1)S(1)}, bf16[1,24,3584]{2,1,0:T(8,128)(2,1)S(1)}, u32[]{:S(2)}, u32[]{:S(2)}) collective-permute-start(bf16[1,24,3584]{2,1,0:T(8,128)(2,1)S(1)} %get-tuple-element.16), channel_id=1, source_target_pairs={{0,8},{4,12},{8,0},{12,4},{16,24},{20,28},{24,16},{28,20},{1,9},{5... | collective-permute-start | bytes 516104 | tf_op jit(solution)/shard_map/ppermute | solution.py:38
  26.1 4.7 %collective-permute-done.7 = bf16[1,24,3584]{2,1,0:T(8,128)(2,1)S(1)} collective-permute-done((bf16[1,24,3584]{2,1,0:T(8,128)(2,1)S(1)}, bf16[1,24,3584]{2,1,0:T(8,128)(2,1)S(1)}, u32[]{:S(2)}, u32[]{:S(2)}) %collective-permute-start.7) | collective-permute-done | bytes 172064 | tf_op jit(solution)/shard_map/ppermute | solution.py:38
  30.8 2.7 %collective-permute-done.6 = bf16[1,24,3584]{2,1,0:T(8,128)(2,1)S(1)} collective-permute-done((bf16[1,24,3584]{2,1,0:T(8,128)(2,1)S(1)}, bf16[1,24,3584]{2,1,0:T(8,128)(2,1)S(1)}, u32[]{:S(2)}, u32[]{:S(2)}) %collective-permute-start.6) | collective-permute-done | bytes 172064 | tf_op jit(solution)/shard_map/ppermute | solution.py:38
  33.7 2.1 %collective-permute-done.8 = bf16[96,3584]{1,0:T(8,128)(2,1)S(1)} collective-permute-done((bf16[96,3584]{1,0:T(8,128)(2,1)S(1)}, bf16[96,3584]{1,0:T(8,128)(2,1)S(1)}, u32[]{:S(2)}, u32[]{:S(2)}) %collective-permute-start.8) | collective-permute-done | bytes 688160 | tf_op jit(solution)/shard_map/ppermute | solution.py:43
  35.9 8.3 %fusion.4 = bf16[192,3584]{1,0:T(8,128)(2,1)S(1)} fusion(bf16[1,1,1024,3584]{3,2,1,0:T(8,128)(2,1)} %param.27, bf16[1,1,3584,1024]{3,2,1,0:T(8,128)(2,1)} %param.26, bf16[96,3584]{1,0:T(8,128)(2,1)S(1)} %collective-permute-done.8, bf16[96,3584]{1,0:T(8,128)(2,1)S(1)} %bitcast.62), kind=kOutput, calls=%fused_computation.10 | convolution fusion | flops 2822995968 | bytes 17432576 | tf_op jit(solution)/shard_map/dot_general | solution.py:157
  44.5 2.0 %collective-permute-done.9 = bf16[4,24,3584]{2,1,0:T(8,128)(2,1)S(1)} collective-permute-done((bf16[4,24,3584]{2,1,0:T(8,128)(2,1)S(1)}, bf16[4,24,3584]{2,1,0:T(8,128)(2,1)S(1)}, u32[]{:S(2)}, u32[]{:S(2)}) %collective-permute-start.9) | collective-permute-done | bytes 688160 | tf_op jit(solution)/shard_map/ppermute | solution.py:43
  46.8 1.7 %collective-permute-start.12 = (bf16[1,24,3584]{2,1,0:T(8,128)(2,1)S(1)}, bf16[1,24,3584]{2,1,0:T(8,128)(2,1)S(1)}, u32[]{:S(2)}, u32[]{:S(2)}) collective-permute-start(bf16[1,24,3584]{2,1,0:T(8,128)(2,1)S(1)} %get-tuple-element.10), channel_id=1, source_target_pairs={{0,24},{4,28},{8,16},{12,20},{16,8},{20,12},{24,0},{28,4},{1,25},{... | collective-permute-start | bytes 516104 | tf_op jit(solution)/shard_map/ppermute | solution.py:38
  48.5 1.0 %collective-permute-start.11 = (bf16[1,24,3584]{2,1,0:T(8,128)(2,1)S(1)}, bf16[1,24,3584]{2,1,0:T(8,128)(2,1)S(1)}, u32[]{:S(2)}, u32[]{:S(2)}) collective-permute-start(bf16[1,24,3584]{2,1,0:T(8,128)(2,1)S(1)} %get-tuple-element.11), channel_id=1, source_target_pairs={{0,16},{4,20},{8,24},{12,28},{16,0},{20,4},{24,8},{28,12},{1,17},{... | collective-permute-start | bytes 516104 | tf_op jit(solution)/shard_map/ppermute | solution.py:38
  49.5 0.8 %collective-permute-start.10 = (bf16[1,24,3584]{2,1,0:T(8,128)(2,1)S(1)}, bf16[1,24,3584]{2,1,0:T(8,128)(2,1)S(1)}, u32[]{:S(2)}, u32[]{:S(2)}) collective-permute-start(bf16[1,24,3584]{2,1,0:T(8,128)(2,1)S(1)} %get-tuple-element.12), channel_id=1, source_target_pairs={{0,8},{4,12},{8,0},{12,4},{16,24},{20,28},{24,16},{28,20},{1,9},{5... | collective-permute-start | bytes 516104 | tf_op jit(solution)/shard_map/ppermute | solution.py:38
  51.1 3.9 %collective-permute-done.12 = bf16[1,24,3584]{2,1,0:T(8,128)(2,1)S(1)} collective-permute-done((bf16[1,24,3584]{2,1,0:T(8,128)(2,1)S(1)}, bf16[1,24,3584]{2,1,0:T(8,128)(2,1)S(1)}, u32[]{:S(2)}, u32[]{:S(2)}) %collective-permute-start.12) | collective-permute-done | bytes 172064 | tf_op jit(solution)/shard_map/ppermute | solution.py:38
  55.0 2.9 %collective-permute-done.11 = bf16[1,24,3584]{2,1,0:T(8,128)(2,1)S(1)} collective-permute-done((bf16[1,24,3584]{2,1,0:T(8,128)(2,1)S(1)}, bf16[1,24,3584]{2,1,0:T(8,128)(2,1)S(1)}, u32[]{:S(2)}, u32[]{:S(2)}) %collective-permute-start.11) | collective-permute-done | bytes 172064 | tf_op jit(solution)/shard_map/ppermute | solution.py:38
  58.4 1.5 %collective-permute-start.13 = (bf16[8,3584]{1,0:T(8,128)(2,1)S(1)}, bf16[8,3584]{1,0:T(8,128)(2,1)S(1)}, u32[]{:S(2)}, u32[]{:S(2)}) collective-permute-start(bf16[8,3584]{1,0:T(8,128)(2,1)S(1)} %get-tuple-element.17), channel_id=1, source_target_pairs={{0,1},{1,0},{2,3},{3,2},{4,5},{5,4},{6,7},{7,6},{8,9},{9,8},{10,11... | collective-permute-start | bytes 172040 | tf_op jit(solution)/shard_map/ppermute | solution.py:47
  59.8 1.1 %collective-permute-start.15 = (bf16[8,3584]{1,0:T(8,128)(2,1)S(1)}, bf16[8,3584]{1,0:T(8,128)(2,1)S(1)}, u32[]{:S(2)}, u32[]{:S(2)}) collective-permute-start(bf16[8,3584]{1,0:T(8,128)(2,1)S(1)} %get-tuple-element.18), channel_id=1, source_target_pairs={{0,3},{1,2},{2,1},{3,0},{4,7},{5,6},{6,5},{7,4},{8,11},{9,10},{10,... | collective-permute-start | bytes 172040 | tf_op jit(solution)/shard_map/ppermute | solution.py:47
  61.0 1.0 %collective-permute-start.14 = (bf16[8,3584]{1,0:T(8,128)(2,1)S(1)}, bf16[8,3584]{1,0:T(8,128)(2,1)S(1)}, u32[]{:S(2)}, u32[]{:S(2)}) collective-permute-start(bf16[8,3584]{1,0:T(8,128)(2,1)S(1)} %get-tuple-element.19), channel_id=1, source_target_pairs={{0,2},{1,3},{2,0},{3,1},{4,6},{5,7},{6,4},{7,5},{8,10},{9,11},{10,... | collective-permute-start | bytes 172040 | tf_op jit(solution)/shard_map/ppermute | solution.py:47
  61.9 0.7 %collective-permute-done.13 = bf16[8,3584]{1,0:T(8,128)(2,1)S(1)} collective-permute-done((bf16[8,3584]{1,0:T(8,128)(2,1)S(1)}, bf16[8,3584]{1,0:T(8,128)(2,1)S(1)}, u32[]{:S(2)}, u32[]{:S(2)}) %collective-permute-start.13) | collective-permute-done | bytes 57376 | tf_op jit(solution)/shard_map/ppermute | solution.py:47
  62.6 3.3 %collective-permute-done.15 = bf16[8,3584]{1,0:T(8,128)(2,1)S(1)} collective-permute-done((bf16[8,3584]{1,0:T(8,128)(2,1)S(1)}, bf16[8,3584]{1,0:T(8,128)(2,1)S(1)}, u32[]{:S(2)}, u32[]{:S(2)}) %collective-permute-start.15) | collective-permute-done | bytes 57376 | tf_op jit(solution)/shard_map/ppermute | solution.py:47
  65.9 1.9 %collective-permute-done.14 = bf16[8,3584]{1,0:T(8,128)(2,1)S(1)} collective-permute-done((bf16[8,3584]{1,0:T(8,128)(2,1)S(1)}, bf16[8,3584]{1,0:T(8,128)(2,1)S(1)}, u32[]{:S(2)}, u32[]{:S(2)}) %collective-permute-start.14) | collective-permute-done | bytes 57376 | tf_op jit(solution)/shard_map/ppermute | solution.py:47
  67.8 0.7 fusion.46
  (77 shorter events, 6.3 us)
Async XLA Ops:
  0.0 1.4 %copy-start.9 = (s32[4,4]{0,1:T(4,128)S(1)}, s32[4,4]{0,1:T(4,128)}, u32[]{:S(2)}) copy-start(s32[4,4]{0,1:T(4,128)} %constant.59.clone) | copy-start | bytes 196
  0.0 7.3 %copy-start.1 = (bf16[8,3584]{1,0:T(8,128)(2,1)S(1)}, bf16[8,3584]{1,0:T(8,128)(2,1)}, u32[]{:S(2)}) copy-start(bf16[8,3584]{1,0:T(8,128)(2,1)} %param.16) | copy-start | bytes 172036
  0.0 7.1 %copy-start.2 = (bf16[8,1024]{1,0:T(8,128)(2,1)S(1)}, bf16[8,1024]{1,0:T(8,128)(2,1)}, u32[]{:S(2)}) copy-start(bf16[8,1024]{1,0:T(8,128)(2,1)} %param.17) | copy-start | bytes 49156
  0.0 6.1 %copy-start.6 = (s32[4,8]{1,0:T(4,128)S(1)}, s32[4,8]{1,0:T(4,128)}, u32[]{:S(2)}) copy-start(s32[4,8]{1,0:T(4,128)} %param.19) | copy-start | bytes 388
  0.0 6.0 %copy-start.10 = (s32[4]{0:T(128)S(1)}, s32[4]{0:T(128)}, u32[]{:S(2)}) copy-start(s32[4]{0:T(128)} %param.20) | copy-start | bytes 52
  0.0 1.4 %copy-start.8 = (s32[1,1,2,4]{3,2,1,0:T(2,128)S(1)}, s32[1,1,2,4]{3,2,1,0:T(2,128)}, u32[]{:S(2)}) copy-start(s32[1,1,2,4]{3,2,1,0:T(2,128)} %param.21) | copy-start | bytes 100
  0.0 6.0 %copy-start.7 = (s32[1,1,2,4]{3,2,1,0:T(2,128)S(1)}, s32[1,1,2,4]{3,2,1,0:T(2,128)}, u32[]{:S(2)}) copy-start(s32[1,1,2,4]{3,2,1,0:T(2,128)} %param.22) | copy-start | bytes 100
  0.0 6.2 %copy-start.4 = (s32[32,8]{0,1:T(8,128)S(1)}, s32[32,8]{0,1:T(8,128)}, u32[]{:S(2)}) copy-start(s32[32,8]{0,1:T(8,128)} %param.23) | copy-start | bytes 3076
  0.0 7.3 %copy-start.3 = (bf16[3584]{0:T(1024)(128)(2,1)S(1)}, bf16[3584]{0:T(1024)(128)(2,1)}, u32[]{:S(2)}) copy-start(bf16[3584]{0:T(1024)(128)(2,1)} %param.25) | copy-start | bytes 21508
  2.0 6.0 %collective-permute-start = (bf16[4,16,1024]{2,1,0:T(8,128)(2,1)S(1)}, bf16[4,16,1024]{2,1,0:T(8,128)(2,1)S(1)}, u32[]{:S(2)}, u32[]{:S(2)}) collective-permute-start(bf16[4,16,1024]{2,1,0:T(8,128)(2,1)S(1)} %gather_fusion), channel_id=1, source_target_pairs={{0,4},{4,8},{8,12},{12,16},{16,20},{20,24},{24,28},{28,0},{1,5},{5... | collective-permute-start | bytes 393224 | tf_op jit(solution)/shard_map/ppermute | solution.py:33
  3.0 5.5 %collective-permute-start.1 = (bf16[4,16,1024]{2,1,0:T(8,128)(2,1)S(1)}, bf16[4,16,1024]{2,1,0:T(8,128)(2,1)S(1)}, u32[]{:S(2)}, u32[]{:S(2)}) collective-permute-start(bf16[4,16,1024]{2,1,0:T(8,128)(2,1)S(1)} %gather_fusion.1), channel_id=1, source_target_pairs={{4,0},{8,4},{12,8},{16,12},{20,16},{24,20},{28,24},{0,28},{5,1},{9... | collective-permute-start | bytes 393224 | tf_op jit(solution)/shard_map/ppermute | solution.py:33
  10.9 0.9 %copy-start = (bf16[8,3584]{1,0:T(8,128)(2,1)S(1)}, bf16[8,3584]{1,0:T(8,128)(2,1)}, u32[]{:S(2)}) copy-start(bf16[8,3584]{1,0:T(8,128)(2,1)} %param.15) | copy-start | bytes 172036
  12.0 7.1 %collective-permute-start.4 = (bf16[8,3584]{1,0:T(8,128)(2,1)S(1)}, bf16[8,3584]{1,0:T(8,128)(2,1)S(1)}, u32[]{:S(2)}, u32[]{:S(2)}) collective-permute-start(bf16[8,3584]{1,0:T(8,128)(2,1)S(1)} %multiply_convert_fusion.1), channel_id=1, source_target_pairs={{0,3},{1,2},{2,1},{3,0},{4,7},{5,6},{6,5},{7,4},{8,11},{9,10},{10,... | collective-permute-start | bytes 172040 | tf_op jit(solution)/shard_map/ppermute | solution.py:47
  16.4 5.8 %collective-permute-start.3 = (bf16[8,3584]{1,0:T(8,128)(2,1)S(1)}, bf16[8,3584]{1,0:T(8,128)(2,1)S(1)}, u32[]{:S(2)}, u32[]{:S(2)}) collective-permute-start(bf16[8,3584]{1,0:T(8,128)(2,1)S(1)} %multiply_convert_fusion.1), channel_id=1, source_target_pairs={{0,2},{1,3},{2,0},{3,1},{4,6},{5,7},{6,4},{7,5},{8,10},{9,11},{10,... | collective-permute-start | bytes 172040 | tf_op jit(solution)/shard_map/ppermute | solution.py:47
  16.4 5.8 %collective-permute-start.2 = (bf16[8,3584]{1,0:T(8,128)(2,1)S(1)}, bf16[8,3584]{1,0:T(8,128)(2,1)S(1)}, u32[]{:S(2)}, u32[]{:S(2)}) collective-permute-start(bf16[8,3584]{1,0:T(8,128)(2,1)S(1)} %multiply_convert_fusion.1), channel_id=1, source_target_pairs={{0,1},{1,0},{2,3},{3,2},{4,5},{5,4},{6,7},{7,6},{8,9},{9,8},{10,11... | collective-permute-start | bytes 172040 | tf_op jit(solution)/shard_map/ppermute | solution.py:47
  22.6 8.2 %collective-permute-start.7 = (bf16[1,24,3584]{2,1,0:T(8,128)(2,1)S(1)}, bf16[1,24,3584]{2,1,0:T(8,128)(2,1)S(1)}, u32[]{:S(2)}, u32[]{:S(2)}) collective-permute-start(bf16[1,24,3584]{2,1,0:T(8,128)(2,1)S(1)} %get-tuple-element.14), channel_id=1, source_target_pairs={{0,24},{4,28},{8,16},{12,20},{16,8},{20,12},{24,0},{28,4},{1,25},{... | collective-permute-start | bytes 516104 | tf_op jit(solution)/shard_map/ppermute | solution.py:38
  24.3 9.2 %collective-permute-start.6 = (bf16[1,24,3584]{2,1,0:T(8,128)(2,1)S(1)}, bf16[1,24,3584]{2,1,0:T(8,128)(2,1)S(1)}, u32[]{:S(2)}, u32[]{:S(2)}) collective-permute-start(bf16[1,24,3584]{2,1,0:T(8,128)(2,1)S(1)} %get-tuple-element.15), channel_id=1, source_target_pairs={{0,16},{4,20},{8,24},{12,28},{16,0},{20,4},{24,8},{28,12},{1,17},{... | collective-permute-start | bytes 516104 | tf_op jit(solution)/shard_map/ppermute | solution.py:38
  24.9 8.6 %collective-permute-start.5 = (bf16[1,24,3584]{2,1,0:T(8,128)(2,1)S(1)}, bf16[1,24,3584]{2,1,0:T(8,128)(2,1)S(1)}, u32[]{:S(2)}, u32[]{:S(2)}) collective-permute-start(bf16[1,24,3584]{2,1,0:T(8,128)(2,1)S(1)} %get-tuple-element.16), channel_id=1, source_target_pairs={{0,8},{4,12},{8,0},{12,4},{16,24},{20,28},{24,16},{28,20},{1,9},{5... | collective-permute-start | bytes 516104 | tf_op jit(solution)/shard_map/ppermute | solution.py:38
  33.7 2.2 %collective-permute-start.8 = (bf16[96,3584]{1,0:T(8,128)(2,1)S(1)}, bf16[96,3584]{1,0:T(8,128)(2,1)S(1)}, u32[]{:S(2)}, u32[]{:S(2)}) collective-permute-start(bf16[96,3584]{1,0:T(8,128)(2,1)S(1)} %bitcast.61), channel_id=1, source_target_pairs={{0,4},{4,0},{8,12},{12,8},{16,20},{20,16},{24,28},{28,24},{1,5},{5... | collective-permute-start | bytes 2064392 | tf_op jit(solution)/shard_map/ppermute | solution.py:43
  44.3 2.2 %collective-permute-start.9 = (bf16[4,24,3584]{2,1,0:T(8,128)(2,1)S(1)}, bf16[4,24,3584]{2,1,0:T(8,128)(2,1)S(1)}, u32[]{:S(2)}, u32[]{:S(2)}) collective-permute-start(bf16[4,24,3584]{2,1,0:T(8,128)(2,1)S(1)} %bitcast.63), channel_id=1, source_target_pairs={{0,4},{4,0},{8,12},{12,8},{16,20},{20,16},{24,28},{28,24},{1,5},{5... | collective-permute-start | bytes 2064392 | tf_op jit(solution)/shard_map/ppermute | solution.py:43
  46.5 3.8 %copy-start.5 = (f32[32,8]{0,1:T(8,128)S(1)}, f32[32,8]{0,1:T(8,128)}, u32[]{:S(2)}) copy-start(f32[32,8]{0,1:T(8,128)} %param.24) | copy-start | bytes 3076
  46.8 8.2 %collective-permute-start.12 = (bf16[1,24,3584]{2,1,0:T(8,128)(2,1)S(1)}, bf16[1,24,3584]{2,1,0:T(8,128)(2,1)S(1)}, u32[]{:S(2)}, u32[]{:S(2)}) collective-permute-start(bf16[1,24,3584]{2,1,0:T(8,128)(2,1)S(1)} %get-tuple-element.10), channel_id=1, source_target_pairs={{0,24},{4,28},{8,16},{12,20},{16,8},{20,12},{24,0},{28,4},{1,25},{... | collective-permute-start | bytes 516104 | tf_op jit(solution)/shard_map/ppermute | solution.py:38
  48.5 9.4 %collective-permute-start.11 = (bf16[1,24,3584]{2,1,0:T(8,128)(2,1)S(1)}, bf16[1,24,3584]{2,1,0:T(8,128)(2,1)S(1)}, u32[]{:S(2)}, u32[]{:S(2)}) collective-permute-start(bf16[1,24,3584]{2,1,0:T(8,128)(2,1)S(1)} %get-tuple-element.11), channel_id=1, source_target_pairs={{0,16},{4,20},{8,24},{12,28},{16,0},{20,4},{24,8},{28,12},{1,17},{... | collective-permute-start | bytes 516104 | tf_op jit(solution)/shard_map/ppermute | solution.py:38
  49.5 8.3 %collective-permute-start.10 = (bf16[1,24,3584]{2,1,0:T(8,128)(2,1)S(1)}, bf16[1,24,3584]{2,1,0:T(8,128)(2,1)S(1)}, u32[]{:S(2)}, u32[]{:S(2)}) collective-permute-start(bf16[1,24,3584]{2,1,0:T(8,128)(2,1)S(1)} %get-tuple-element.12), channel_id=1, source_target_pairs={{0,8},{4,12},{8,0},{12,4},{16,24},{20,28},{24,16},{28,20},{1,9},{5... | collective-permute-start | bytes 516104 | tf_op jit(solution)/shard_map/ppermute | solution.py:38
  58.4 4.2 %collective-permute-start.13 = (bf16[8,3584]{1,0:T(8,128)(2,1)S(1)}, bf16[8,3584]{1,0:T(8,128)(2,1)S(1)}, u32[]{:S(2)}, u32[]{:S(2)}) collective-permute-start(bf16[8,3584]{1,0:T(8,128)(2,1)S(1)} %get-tuple-element.17), channel_id=1, source_target_pairs={{0,1},{1,0},{2,3},{3,2},{4,5},{5,4},{6,7},{7,6},{8,9},{9,8},{10,11... | collective-permute-start | bytes 172040 | tf_op jit(solution)/shard_map/ppermute | solution.py:47
  59.8 6.1 %collective-permute-start.15 = (bf16[8,3584]{1,0:T(8,128)(2,1)S(1)}, bf16[8,3584]{1,0:T(8,128)(2,1)S(1)}, u32[]{:S(2)}, u32[]{:S(2)}) collective-permute-start(bf16[8,3584]{1,0:T(8,128)(2,1)S(1)} %get-tuple-element.18), channel_id=1, source_target_pairs={{0,3},{1,2},{2,1},{3,0},{4,7},{5,6},{6,5},{7,4},{8,11},{9,10},{10,... | collective-permute-start | bytes 172040 | tf_op jit(solution)/shard_map/ppermute | solution.py:47
  61.0 6.8 %collective-permute-start.14 = (bf16[8,3584]{1,0:T(8,128)(2,1)S(1)}, bf16[8,3584]{1,0:T(8,128)(2,1)S(1)}, u32[]{:S(2)}, u32[]{:S(2)}) collective-permute-start(bf16[8,3584]{1,0:T(8,128)(2,1)S(1)} %get-tuple-element.19), channel_id=1, source_target_pairs={{0,2},{1,3},{2,0},{3,1},{4,6},{5,7},{6,4},{7,5},{8,10},{9,11},{10,... | collective-permute-start | bytes 172040 | tf_op jit(solution)/shard_map/ppermute | solution.py:47

commit v2 on v1

v2 whole, which is shorter than its diff:
```python
import jax
import jax.numpy as jnp
from jax import lax
from jax.experimental import pallas as pl
from jax.experimental.pallas import tpu as pltpu
from jax.sharding import PartitionSpec as P

HEADS = 28
KV_HEADS = 4
HEAD_DIM = 128
EXP_DEV = 4
CAP = 24


neg_big = -1e30
norm_eps = 1e-06


def partner_steps(count):
    if count & (count - 1):
        raise ValueError("axis size")
    return [[i ^ k for i in range(count)] for k in range(1, count)]


def partner_of(index, steps):
    return index ^ jnp.arange(len(steps) + 1, dtype=jnp.int32)


def ring_pages(block, axis, up):
    count = lax.axis_size(axis)
    pairs = [(i, (i + 1) % count) for i in range(count)]
    if not up:
        pairs = [(target, source) for source, target in pairs]
    return lax.ppermute(block, axis, pairs)


def swap_plane(block, step, group_size):
    pairs = [(q * group_size + g, p * group_size + g) for q, p in enumerate(step) for g in range(group_size)]
    return lax.ppermute(block, "req", pairs)


def swap_group(block, step, group_size):
    pairs = [(q * group_size + g, q * group_size + p) for q in range(EXP_DEV) for g, p in enumerate(step)]
    return lax.ppermute(block, "req", pairs)


def swap_exp(block, step):
    return lax.ppermute(block, "exp", list(enumerate(step)))


def send_pages_kernel(source_ref, pool_ref, up_ref, down_ref):
    for side, out_ref in enumerate((up_ref, down_ref)):
        for i in range(out_ref.shape[0]):
            out_ref[i] = pool_ref[source_ref[side, i]]


def send_pages(pool_pages, sources):
    pages = jax.ShapeDtypeStruct((sources.shape[1],) + pool_pages.shape[1:], pool_pages.dtype)
    return pl.pallas_call(
        send_pages_kernel,
        out_shape=(pages, pages),
        in_specs=[pl.BlockSpec(memory_space=pltpu.SMEM), pl.BlockSpec(memory_space=pltpu.VMEM)],
        out_specs=(pl.BlockSpec(memory_space=pltpu.VMEM),) * 2,
        compiler_params=pltpu.CompilerParams(vmem_limit_bytes=4 * 1024 * 1024),
        cost_estimate=pl.CostEstimate(
            flops=4 * 1024 * 1024 * 1024, bytes_accessed=pool_pages.size * pool_pages.dtype.itemsize, transcendentals=0
        ),
        name="send_pages",
    )(sources, pool_pages)


def weighted_values(weights, values):
    high = weights.astype(jnp.bfloat16)
    low = (weights - high.astype(jnp.float32)).astype(jnp.bfloat16)
    both = jnp.dot(
        jnp.concatenate([high, low], axis=0), values, preferred_element_type=jnp.float32
    )
    return both[: weights.shape[0]] + both[weights.shape[0] :]


def local_attention_kernel(
    table_ref, length_ref, target_ref, queries_ref, fresh_ref, pool_ref, max_ref, sum_ref, out_ref, query_ref, bias_ref
):
    request_count, table_width = table_ref.shape
    token_count, kv_width = fresh_ref.shape
    moved = target_ref.shape[1]
    page_tokens = pool_ref.shape[1]
    span = table_width * page_tokens
    draft_count = token_count // request_count
    share = HEADS // KV_HEADS
    rows_count = share * token_count
    tail = HEAD_DIM
    query = queries_ref[...].astype(jnp.float32)
    fresh = jnp.concatenate(
        [
            fresh_ref[...].astype(jnp.float32),
            jnp.zeros((tail - token_count, kv_width), jnp.float32),
        ],
        axis=0,
    ).astype(fresh_ref.dtype)
    pages = [table_ref[n, i] for n in range(request_count) for i in range(table_width)]

    def cache(first):
        rows = [pool_ref[page, :, first : first + HEAD_DIM] for page in pages]
        return jnp.concatenate(rows + [fresh[:, first : first + HEAD_DIM]], axis=0)

    token = lax.broadcasted_iota(jnp.int32, (rows_count, span), 0) % token_count
    lane = lax.broadcasted_iota(jnp.int32, (rows_count, span), 1)
    live = []
    for n in range(request_count):
        arrives = (table_ref[n, 0] == target_ref[0, 0]) | (table_ref[n, 0] == target_ref[1, 0])
        first = jnp.where(arrives, moved * page_tokens, 0)
        live.append((token // draft_count == n) & (lane >= first) & (lane < length_ref[n]))
    tail_token = lax.broadcasted_iota(jnp.int32, (rows_count, tail), 0) % token_count
    tail_lane = lax.broadcasted_iota(jnp.int32, (rows_count, tail), 1)
    live.append((tail_token // draft_count == tail_lane // draft_count) & (tail_lane <= tail_token))
    live = jnp.concatenate([jnp.where(mask, 0.0, neg_big) for mask in live], axis=1)
    key_width = KV_HEADS * HEAD_DIM
    for j in range(KV_HEADS):
        heads = range(j * share, (j + 1) * share)
        rows = jnp.concatenate([query[:, h * HEAD_DIM : (h + 1) * HEAD_DIM] for h in heads], axis=0)
        query_ref[j] = rows
        scores = lax.dot_general(
            rows.astype(jnp.bfloat16), cache(j * HEAD_DIM), (((1,), (1,)), ((), ())),
            preferred_element_type=jnp.float32,
        )
        scores = jnp.where(live < 0, neg_big, scores * HEAD_DIM ** (-0.5))
        highest = jnp.max(scores, axis=1, keepdims=True)
        weights = jnp.exp(scores - highest)
        max_ref[j] = jnp.broadcast_to(highest, max_ref.shape[1:])
        sum_ref[j] = jnp.broadcast_to(jnp.sum(weights, axis=1, keepdims=True), sum_ref.shape[1:])
        out_ref[j] = weighted_values(weights, cache(key_width + j * HEAD_DIM))

    moved_span = moved * page_tokens
    token = lax.broadcasted_iota(jnp.int32, (rows_count, 2 * moved_span), 0) % token_count
    lane = lax.broadcasted_iota(jnp.int32, (rows_count, 2 * moved_span), 1)
    seen = jnp.zeros((rows_count, 2 * moved_span), jnp.float32)
    for side in range(2):
        position = lane - side * moved_span
        for n in range(request_count):
            bound = jnp.where(table_ref[n, 0] == target_ref[side, 0], length_ref[n], 0)
            inside = (position >= 0) & (position < moved_span) & (position < bound)
            seen = seen + jnp.where((token // draft_count == n) & inside, 1.0, 0.0)
    bias_ref[...] = jnp.where(seen > 0, 0.0, neg_big)


def local_attention(table, lengths, targets, queries, fresh_kv, pool_pages):
    token_count = queries.shape[0]
    moved = targets.shape[1]
    part = jax.ShapeDtypeStruct((KV_HEADS, HEADS // KV_HEADS * token_count, HEAD_DIM), jnp.float32)
    bias = jax.ShapeDtypeStruct((part.shape[1], 2 * moved * pool_pages.shape[1]), jnp.float32)
    return pl.pallas_call(
        local_attention_kernel,
        out_shape=(part, part, part, part, bias),
        in_specs=[pl.BlockSpec(memory_space=pltpu.SMEM)] * 3 + [pl.BlockSpec(memory_space=pltpu.VMEM)] * 3,
        out_specs=(pl.BlockSpec(memory_space=pltpu.VMEM),) * 5,
        compiler_params=pltpu.CompilerParams(vmem_limit_bytes=6 * 1024 * 1024),
        cost_estimate=pl.CostEstimate(flops=40 * 1024 * 1024, bytes_accessed=2 * 1024 * 1024, transcendentals=160 * 1024),
        name="local_attention",
    )(table, lengths, targets, queries, fresh_kv, pool_pages)


def arrived_attention_kernel(
    resid_ref, gain_ref, low_ref, high_ref, max_ref, sum_ref, out_ref, query_ref, bias_ref, residual_ref, normed_ref
):
    token_count, model_width = residual_ref.shape
    share = HEADS // KV_HEADS
    key_width = KV_HEADS * HEAD_DIM
    heads = range(KV_HEADS)

    def arrived(first):
        at = pl.ds(first, HEAD_DIM)
        return jnp.concatenate([low_ref[:, at], high_ref[:, at]], axis=0)

    scores = [
        lax.dot_general(
            query_ref[j].astype(jnp.bfloat16), arrived(j * HEAD_DIM), (((1,), (1,)), ((), ())),
            preferred_element_type=jnp.float32,
        )
        for j in heads
    ]
    hidden = bias_ref[...] < 0
    scores = [jnp.where(hidden, neg_big, part * HEAD_DIM ** (-0.5)) for part in scores]
    highest = [jnp.maximum(max_ref[j], jnp.max(scores[j], axis=1, keepdims=True)) for j in heads]
    weights = [jnp.exp(scores[j] - highest[j][:, :1]) for j in heads]
    scale = [jnp.exp(max_ref[j] - highest[j]) for j in heads]
    total = [sum_ref[j] * scale[j] + jnp.sum(weights[j], axis=1, keepdims=True) for j in heads]
    summed = [
        out_ref[j] * scale[j] + weighted_values(weights[j], arrived(key_width + j * HEAD_DIM)) for j in heads
    ]
    blocks = []
    for j in heads:
        attention = summed[j] / total[j]
        for h in range(share):
            first = (j * share + h) * HEAD_DIM
            resid = resid_ref[:, first : first + HEAD_DIM].astype(jnp.float32)
            blocks.append(resid + attention[h * token_count : (h + 1) * token_count])
    squares = blocks[0] * blocks[0]
    for block in blocks[1:]:
        squares = squares + block * block
    inv_rms = lax.rsqrt(jnp.sum(squares, axis=1, keepdims=True) / model_width + norm_eps)
    residual = jnp.concatenate(blocks, axis=1)
    residual_ref[...] = residual
    normed_ref[...] = (residual * inv_rms * gain_ref[...].astype(jnp.float32)[None, :]).astype(normed_ref.dtype)


def arrived_attention(resid_in, gain, low, high, parts):
    shape = resid_in.shape
    return pl.pallas_call(
        arrived_attention_kernel,
        out_shape=(jax.ShapeDtypeStruct(shape, jnp.float32), jax.ShapeDtypeStruct(shape, jnp.bfloat16)),
        in_specs=[pl.BlockSpec(memory_space=pltpu.VMEM)] * 9,
        out_specs=(pl.BlockSpec(memory_space=pltpu.VMEM),) * 2,
        compiler_params=pltpu.CompilerParams(vmem_limit_bytes=4 * 1024 * 1024),
        cost_estimate=pl.CostEstimate(flops=8 * 1024 * 1024 * 1024, bytes_accessed=2 * 1024 * 1024, transcendentals=60 * 1024),
        name="arrived_attention",
    )(resid_in, gain, low, high, *parts)


def load_kernel(weight_ref, out_ref, sem):
    copy = pltpu.make_async_copy(weight_ref, out_ref, sem)
    copy.start()
    copy.wait()


def load(weight):
    return pl.pallas_call(
        load_kernel,
        out_shape=jax.ShapeDtypeStruct(weight.shape, weight.dtype),
        in_specs=[pl.BlockSpec(memory_space=pltpu.HBM)],
        out_specs=pl.BlockSpec(memory_space=pltpu.VMEM),
        scratch_shapes=[pltpu.SemaphoreType.DMA],
        compiler_params=pltpu.CompilerParams(vmem_limit_bytes=1024 * 1024),
        cost_estimate=pl.CostEstimate(
            flops=0, bytes_accessed=2 * weight.size * weight.dtype.itemsize, transcendentals=0
        ),
        name="load_weight",
    )(weight)


def body(
    resid_in,
    queries,
    fresh_kv,
    kv_pool,
    block_table,
    lengths,
    mig_source,
    mig_target,
    expert_ids,
    gate_values,
    norm_gain,
    w_in,
    w_out,
):
    token_count = resid_in.shape[0]
    model_width = resid_in.shape[1]
    exp_count = lax.axis_size("exp")
    group_size = lax.axis_size("req") // EXP_DEV
    plane_steps = partner_steps(EXP_DEV)
    group_steps = partner_steps(group_size)
    exp_steps = partner_steps(exp_count)

    pool_pages = kv_pool[0, 0]
    targets = mig_target[0, 0]
    up, down = send_pages(pool_pages, mig_source[0, 0])
    moved_shape = (up.shape[0] * up.shape[1], up.shape[2])
    from_low = ring_pages(up.reshape(moved_shape), "req", True)
    from_high = ring_pages(down.reshape(moved_shape), "req", False)

    parts = local_attention(block_table, lengths, targets, queries, fresh_kv, pool_pages)
    residual, normed = arrived_attention(resid_in, norm_gain, from_low, from_high, parts)
    normed, expert_ids, gate_values, inner = lax.optimization_barrier(
        (normed, expert_ids, gate_values, w_in[0, 0])
    )

    exp_order = partner_of(lax.axis_index("exp"), exp_steps)
    plane_order = partner_of(lax.axis_index("req") // group_size, plane_steps)
    ids = expert_ids.reshape(exp_count, token_count, -1)[exp_order].reshape(expert_ids.shape)
    gates = gate_values.reshape(exp_count, token_count, -1)[exp_order].reshape(gate_values.shape)
    local_ids = lax.axis_index("exp") * EXP_DEV + plane_order
    matches = ids[None, :, :] == local_ids[:, None, None]
    is_named = jnp.any(matches, axis=2)
    gate_local = jnp.sum(jnp.where(matches, gates[None, :, :], 0.0), axis=2)
    slot_index = jnp.cumsum(is_named.astype(jnp.int32), axis=1) - 1
    placement = is_named[:, None, :] & (slot_index[:, None, :] == jnp.arange(CAP)[None, :, None])
    columns = placement.astype(jnp.bfloat16)
    gate_columns = jnp.where(placement, gate_local[:, None, :], 0.0)

    gathered = jnp.concatenate([normed] + [swap_exp(normed, step) for step in exp_steps], axis=0)
    packed = jnp.einsum(
        "kct,td->kcd", columns, gathered, preferred_element_type=jnp.float32
    ).astype(jnp.bfloat16)
    packed, outer = lax.optimization_barrier((packed, w_out[0, 0]))
    inner = load(inner)
    outer = load(outer)
    pieces = [packed[0]] + [
        swap_plane(packed[k + 1], step, group_size) for k, step in enumerate(plane_steps)
    ]
    inbound = jnp.concatenate(
        pieces + [swap_group(piece, step, group_size) for step in group_steps for piece in pieces], axis=0
    )

    hidden = lax.optimization_barrier(jnp.dot(inbound, inner, preferred_element_type=jnp.float32))
    activated = lax.optimization_barrier(jax.nn.silu(hidden).astype(jnp.bfloat16))

    def outer_rows(rows):
        return jnp.dot(rows, outer, preferred_element_type=jnp.float32)

    share = EXP_DEV * CAP
    others = outer_rows(activated[share:]).astype(jnp.bfloat16)
    arrived = [
        swap_group(others[k * share : (k + 1) * share], step, group_size) for k, step in enumerate(group_steps)
    ]
    activated, others = lax.optimization_barrier((activated, others))
    summed = lax.optimization_barrier(outer_rows(activated[:share]))
    for part in arrived:
        summed = summed + part.astype(jnp.float32)
    summed = summed.astype(jnp.bfloat16).reshape(EXP_DEV, CAP, model_width)

    returned = jnp.concatenate(
        [summed[:1]] + [swap_plane(summed[k + 1 : k + 2], step, group_size) for k, step in enumerate(plane_steps)],
        axis=0,
    )
    mix = jnp.einsum(
        "kct,kcd->td", gate_columns, returned.astype(jnp.float32), precision=lax.Precision.HIGHEST
    )
    blocks = mix.reshape(exp_count, token_count, model_width)
    result = residual + blocks[0]
    blocks = blocks.astype(jnp.bfloat16)
    for k, step in enumerate(exp_steps):
        result = result + swap_exp(blocks[k + 1], step).astype(jnp.float32)
    return result.astype(jnp.bfloat16)


def solution(mesh):
    placed = (
        P(("req", "exp"), None),
        P(("req", "exp"), None),
        P(("req", "exp"), None),
        P("req", "exp", None, None, None),
        P(("req", "exp"), None),
        P(("req", "exp")),
        P("req", "exp", None, None),
        P("req", "exp", None, None),
        P("req", None),
        P("req", None),
        P(),
        P("exp", "req", None, None),
        P("exp", "req", None, None),
    )
    return jax.shard_map(
        body, mesh=mesh, in_specs=placed, out_specs=P(("req", "exp"), None), check_vma=False
    )
```

time: 68.6 us -> 60.8 us (0.89)
  waiting for transfers between devices: 30.3 us -> 18.8 us
  matrix products: 10.2 us -> 4.95 us
  Pallas kernels: 0 us -> 4.14 us
  local copies, waits for them, and re-layouts: 6 us -> 9.7 us
  starting transfers between devices: 19.5 us -> 21.3 us
  other arithmetic: 2.13 us -> 1.41 us
    unnamed x25 -> x35, local copies, waits for them, and re-layouts: 1.52 us -> 8.2 us
    dot_general x3, matrix products: 9.46 us -> 4.17 us  [the longest x2 2.59 us: outer_rows(): return jnp.dot(rows, outer, preferred_element_type=jnp.float32)]
    ppermute x6, waiting for transfers between devices: 10.9 us -> 6.55 us  [swap_exp(): return lax.ppermute(block, 'exp', list(enumerate(step)))]
    ppermute x6, waiting for transfers between devices: 14.2 us -> 9.91 us  [swap_plane(): return lax.ppermute(block, 'req', pairs)]
    pallas_call x0 -> x5, Pallas kernels: none -> 4.14 us  [the longest x1 1.92 us: local_attention(): pl.pallas_call(local_attention_kernel, out_shape=(part, part, part, part,...]
    ppermute x2 -> x5, waiting for transfers between devices: 4.12 us -> 1.46 us  [swap_group(): return lax.ppermute(block, 'req', pairs)]
    gather x3 -> x0, local copies, waits for them, and re-layouts: 1.72 us -> none  [the longest x1 0.61 us: body(): pool_after[block_table].reshape(request_count, cache_span, kv_width)]
    ppermute x2 -> x5, starting transfers between devices: 0.3 us -> 1.47 us  [swap_group(): return lax.ppermute(block, 'req', pairs)]
  transfers between devices with their start and end apart: 16 -> 19, of which waited for: 14 -> 14; matrix products, arithmetic and copies ran while one was open for 4% -> 5% of each run, Pallas kernels for 0% -> 5%
where the time goes in v2:
time: 60.8 us; the launch traced here: 60.6 us
  starting transfers between devices  21.3 us (35%)
  waiting for transfers between devices  18.8 us (31%)
  local copies, waits for them, and re-layouts  9.7 us (16%)
  matrix products  4.95 us (8%)
  Pallas kernels  4.14 us (7%)
  other arithmetic  1.41 us (2%)
    ppermute x6, waiting for transfers between devices, swap_plane(): return lax.ppermute(block, 'req', pairs)  9.91 us
    ppermute x6, starting transfers between devices, swap_exp(): return lax.ppermute(block, 'exp', list(enumerate(step)))  9.19 us
    unnamed x35, local copies, waits for them, and re-layouts  8.2 us
    ppermute x6, starting transfers between devices, swap_plane(): return lax.ppermute(block, 'req', pairs)  7.19 us
    ppermute x6, waiting for transfers between devices, swap_exp(): return lax.ppermute(block, 'exp', list(enumerate(step)))  6.55 us
    ppermute x2, starting transfers between devices, ring_pages(): return lax.ppermute(block, axis, pairs)  3.45 us
    dot_general x2, matrix products, outer_rows(): return jnp.dot(rows, outer, preferred_element_type=jnp.float32)  2.59 us
    pallas_call x1, Pallas kernels, local_attention(): pl.pallas_call(local_attention_kernel, out_shape=(part, part, part, part,...  1.92 us
  transfers between devices with their start and end apart: 19, of which 14 were waited for; matrix products, arithmetic and copies ran while one was open for 5% of the time, Pallas kernels for 5%

profile of v2, /device:TPU:0, one launch (start us, length us, event | category | flops | bytes accessed | tf_op | source)
XLA Modules:
  0.0 60.6 jit_solution(11911689173834137299)
XLA Ops:
  0.0 1.2 %copy-done.2 = bf16[1,1,32,16,1024]{4,3,2,1,0:T(8,128)(2,1)S(1)} copy-done((bf16[1,1,32,16,1024]{4,3,2,1,0:T(8,128)(2,1)S(1)}, bf16[1,1,32,16,1024]{4,3,2,1,0:T(8,128)(2,1)}, u32[]{:S(2)}) %copy-start.2) | copy-done | bytes 1048600
  1.2 0.7 %copy-done.11 = s32[1,1,2,4]{3,2,1,0:T(2,128)S(1)} copy-done((s32[1,1,2,4]{3,2,1,0:T(2,128)S(1)}, s32[1,1,2,4]{3,2,1,0:T(2,128)}, u32[]{:S(2)}) %copy-start.11) | copy-done | bytes 56
  2.0 0.6 send_pages.1
  3.0 2.9 %collective-permute-start.1 = (bf16[64,1024]{1,0:T(8,128)(2,1)S(1)}, bf16[64,1024]{1,0:T(8,128)(2,1)S(1)}, u32[]{:S(2)}, u32[]{:S(2)}) collective-permute-start(bf16[64,1024]{1,0:T(8,128)(2,1)S(1)} %bitcast.45), channel_id=1, source_target_pairs={{4,0},{8,4},{12,8},{16,12},{20,16},{24,20},{28,24},{0,28},{5,1},{9... | collective-permute-start | bytes 393224 | tf_op jit(solution)/shard_map/ppermute | solution.py:34
  6.1 1.9 %local_attention.1 = (f32[4,56,128]{2,1,0:T(8,128)S(1)}, f32[4,56,128]{2,1,0:T(8,128)S(1)}, f32[4,56,128]{2,1,0:T(8,128)S(1)}, f32[4,56,128]{2,1,0:T(8,128)S(1)}, f32[56,128]{1,0:T(8,128)S(1)}) custom-call(s32[4,8]{1,0:T(4,128)S(1)} %copy-done.6, s32[4]{0:T(128)S(1)} %copy-done.8, s32[2,4]{1,0:T(2,128)S(1)} %bitcast.44, bf16[8,3584]{1,0:T(8,128)(2,1)S(1)} %copy-done.4, ...), custom_call_target="tpu_custom_call" | custom-call | flops 41943040 | bytes 2097152 | tf_op jit(solution)/shard_map/local_attention/pallas_call | solution.py:152
  8.0 0.6 collective-permute-done.low_ref
  8.9 0.7 %arrived_attention.1 = (f32[8,3584]{1,0:T(8,128)S(1)}, bf16[8,3584]{1,0:T(8,128)(2,1)S(1)}) custom-call(bf16[8,3584]{1,0:T(8,128)(2,1)S(1)} %copy-done.9, bf16[3584]{0:T(1024)(128)(2,1)S(1)} %copy-done.10, bf16[64,1024]{1,0:T(8,128)(2,1)S(1)} %collective-permute-done.low_ref, bf16[64,1024]{1,0:T(8,128)(2,1)S(1)} %collective-permute-done.1.high_ref, ...), custom_call_target="tpu_custom_call" | custom-call | flops 8589934592 | bytes 2097152 | tf_op jit(solution)/shard_map/arrived_attention/pallas_call | solution.py:209
  9.5 2.1 %collective-permute-start.2 = (bf16[8,3584]{1,0:T(8,128)(2,1)S(1)}, bf16[8,3584]{1,0:T(8,128)(2,1)S(1)}, u32[]{:S(2)}, u32[]{:S(2)}) collective-permute-start(bf16[8,3584]{1,0:T(8,128)(2,1)S(1)} %get-tuple-element.32), channel_id=1, source_target_pairs={{0,1},{1,0},{2,3},{3,2},{4,5},{5,4},{6,7},{7,6},{8,9},{9,8},{10,11... | collective-permute-start | bytes 172040 | tf_op jit(solution)/shard_map/ppermute | solution.py:48
  11.7 2.6 %collective-permute-start.3 = (bf16[8,3584]{1,0:T(8,128)(2,1)S(1)}, bf16[8,3584]{1,0:T(8,128)(2,1)S(1)}, u32[]{:S(2)}, u32[]{:S(2)}) collective-permute-start(bf16[8,3584]{1,0:T(8,128)(2,1)S(1)} %get-tuple-element.32), channel_id=1, source_target_pairs={{0,2},{1,3},{2,0},{3,1},{4,6},{5,7},{6,4},{7,5},{8,10},{9,11},{10,... | collective-permute-start | bytes 172040 | tf_op jit(solution)/shard_map/ppermute | solution.py:48
  15.3 3.1 %copy-done = bf16[1,1,3584,1024]{3,2,1,0:T(8,128)(2,1)S(1)} copy-done((bf16[1,1,3584,1024]{3,2,1,0:T(8,128)(2,1)S(1)}, bf16[1,1,3584,1024]{3,2,1,0:T(8,128)(2,1)}, u32[]{:S(2)}) %copy-start) | copy-done | bytes 7340056
  18.9 1.8 %collective-permute-done.4 = bf16[8,3584]{1,0:T(8,128)(2,1)S(1)} collective-permute-done((bf16[8,3584]{1,0:T(8,128)(2,1)S(1)}, bf16[8,3584]{1,0:T(8,128)(2,1)S(1)}, u32[]{:S(2)}, u32[]{:S(2)}) %collective-permute-start.4) | collective-permute-done | bytes 57376 | tf_op jit(solution)/shard_map/ppermute | solution.py:48
  21.1 0.8 %collective-permute-start.5 = (bf16[24,3584]{1,0:T(8,128)(2,1)S(1)}, bf16[24,3584]{1,0:T(8,128)(2,1)S(1)}, u32[]{:S(2)}, u32[]{:S(2)}) collective-permute-start(bf16[24,3584]{1,0:T(8,128)(2,1)S(1)} %get-tuple-element.44), channel_id=1, source_target_pairs={{0,8},{4,12},{8,0},{12,4},{16,24},{20,28},{24,16},{28,20},{1,9},{5... | collective-permute-start | bytes 516104 | tf_op jit(solution)/shard_map/ppermute | solution.py:39
  21.9 1.6 %collective-permute-start.6 = (bf16[24,3584]{1,0:T(8,128)(2,1)S(1)}, bf16[24,3584]{1,0:T(8,128)(2,1)S(1)}, u32[]{:S(2)}, u32[]{:S(2)}) collective-permute-start(bf16[24,3584]{1,0:T(8,128)(2,1)S(1)} %get-tuple-element.43), channel_id=1, source_target_pairs={{0,16},{4,20},{8,24},{12,28},{16,0},{20,4},{24,8},{28,12},{1,17},{... | collective-permute-start | bytes 516104 | tf_op jit(solution)/shard_map/ppermute | solution.py:39
  23.5 1.2 %collective-permute-start.7 = (bf16[24,3584]{1,0:T(8,128)(2,1)S(1)}, bf16[24,3584]{1,0:T(8,128)(2,1)S(1)}, u32[]{:S(2)}, u32[]{:S(2)}) collective-permute-start(bf16[24,3584]{1,0:T(8,128)(2,1)S(1)} %get-tuple-element.42), channel_id=1, source_target_pairs={{0,24},{4,28},{8,16},{12,20},{16,8},{20,12},{24,0},{28,4},{1,25},{... | collective-permute-start | bytes 516104 | tf_op jit(solution)/shard_map/ppermute | solution.py:39
  24.7 3.1 %copy-done.1 = bf16[1,1,1024,3584]{3,2,1,0:T(8,128)(2,1)S(1)} copy-done((bf16[1,1,1024,3584]{3,2,1,0:T(8,128)(2,1)S(1)}, bf16[1,1,1024,3584]{3,2,1,0:T(8,128)(2,1)}, u32[]{:S(2)}) %copy-start.1) | copy-done | bytes 7340056
  28.9 3.1 %collective-permute-done.6 = bf16[24,3584]{1,0:T(8,128)(2,1)S(1)} collective-permute-done((bf16[24,3584]{1,0:T(8,128)(2,1)S(1)}, bf16[24,3584]{1,0:T(8,128)(2,1)S(1)}, u32[]{:S(2)}, u32[]{:S(2)}) %collective-permute-start.6) | collective-permute-done | bytes 172064 | tf_op jit(solution)/shard_map/ppermute | solution.py:39
  32.6 0.7 %collective-permute-done.10 = bf16[24,3584]{1,0:T(8,128)(2,1)S(1)} collective-permute-done((bf16[24,3584]{1,0:T(8,128)(2,1)S(1)}, bf16[24,3584]{1,0:T(8,128)(2,1)S(1)}, u32[]{:S(2)}, u32[]{:S(2)}) %collective-permute-start.10) | collective-permute-done | bytes 172064 | tf_op jit(solution)/shard_map/ppermute | solution.py:44
  33.6 1.6 %fusion.37 = f32[192,1024]{1,0:T(8,128)S(1)} fusion(bf16[192,3584]{1,0:T(8,128)(2,1)S(1)} %constant_dynamic-update-slice_fusion, bf16[3584,1024]{1,0:T(8,128)(2,1)S(1)} %load_weight.2), kind=kOutput, calls=%fused_computation.67 | convolution fusion | flops 1409286144 | bytes 9502720 | tf_op jit(solution)/shard_map/dot_general | solution.py:304
  35.4 1.3 %convolution_convert_fusion = bf16[96,3584]{1,0:T(8,128)(2,1)S(1)} fusion(bf16[1024,3584]{1,0:T(8,128)(2,1)S(1)} %load_weight.3, bf16[192,1024]{1,0:T(8,128)(2,1)S(1)} %multiply_convert_fusion), kind=kOutput, calls=%fused_computation.2 | convolution fusion | flops 704987136 | bytes 8224768 | tf_op jit(solution)/shard_map/dot_general | solution.py:308
  37.2 1.3 %fusion.14 = f32[96,3584]{1,0:T(8,128)S(1)} fusion(bf16[1024,3584]{1,0:T(8,128)(2,1)S(1)} %load_weight.3, bf16[192,1024]{1,0:T(8,128)(2,1)S(1)} %multiply_convert_fusion), kind=kOutput, calls=%fused_computation.22 | convolution fusion | flops 704643072 | bytes 8912896 | tf_op jit(solution)/shard_map/dot_general | solution.py:308
  39.1 0.7 %collective-permute-start.13 = (bf16[1,24,3584]{2,1,0:T(8,128)(2,1)S(1)}, bf16[1,24,3584]{2,1,0:T(8,128)(2,1)S(1)}, u32[]{:S(2)}, u32[]{:S(2)}) collective-permute-start(bf16[1,24,3584]{2,1,0:T(8,128)(2,1)S(1)} %get-tuple-element.40), channel_id=1, source_target_pairs={{0,8},{4,12},{8,0},{12,4},{16,24},{20,28},{24,16},{28,20},{1,9},{5... | collective-permute-start | bytes 516104 | tf_op jit(solution)/shard_map/ppermute | solution.py:39
  39.8 1.4 %collective-permute-start.14 = (bf16[1,24,3584]{2,1,0:T(8,128)(2,1)S(1)}, bf16[1,24,3584]{2,1,0:T(8,128)(2,1)S(1)}, u32[]{:S(2)}, u32[]{:S(2)}) collective-permute-start(bf16[1,24,3584]{2,1,0:T(8,128)(2,1)S(1)} %get-tuple-element.39), channel_id=1, source_target_pairs={{0,16},{4,20},{8,24},{12,28},{16,0},{20,4},{24,8},{28,12},{1,17},{... | collective-permute-start | bytes 516104 | tf_op jit(solution)/shard_map/ppermute | solution.py:39
  41.2 1.5 %collective-permute-start.15 = (bf16[1,24,3584]{2,1,0:T(8,128)(2,1)S(1)}, bf16[1,24,3584]{2,1,0:T(8,128)(2,1)S(1)}, u32[]{:S(2)}, u32[]{:S(2)}) collective-permute-start(bf16[1,24,3584]{2,1,0:T(8,128)(2,1)S(1)} %get-tuple-element.38), channel_id=1, source_target_pairs={{0,24},{4,28},{8,16},{12,20},{16,8},{20,12},{24,0},{28,4},{1,25},{... | collective-permute-start | bytes 516104 | tf_op jit(solution)/shard_map/ppermute | solution.py:39
  43.5 2.9 %collective-permute-done.13 = bf16[1,24,3584]{2,1,0:T(8,128)(2,1)S(1)} collective-permute-done((bf16[1,24,3584]{2,1,0:T(8,128)(2,1)S(1)}, bf16[1,24,3584]{2,1,0:T(8,128)(2,1)S(1)}, u32[]{:S(2)}, u32[]{:S(2)}) %collective-permute-start.13) | collective-permute-done | bytes 172064 | tf_op jit(solution)/shard_map/ppermute | solution.py:39
  46.4 2.4 %collective-permute-done.14 = bf16[1,24,3584]{2,1,0:T(8,128)(2,1)S(1)} collective-permute-done((bf16[1,24,3584]{2,1,0:T(8,128)(2,1)S(1)}, bf16[1,24,3584]{2,1,0:T(8,128)(2,1)S(1)}, u32[]{:S(2)}, u32[]{:S(2)}) %collective-permute-start.14) | collective-permute-done | bytes 172064 | tf_op jit(solution)/shard_map/ppermute | solution.py:39
  48.8 1.4 %collective-permute-done.15 = bf16[1,24,3584]{2,1,0:T(8,128)(2,1)S(1)} collective-permute-done((bf16[1,24,3584]{2,1,0:T(8,128)(2,1)S(1)}, bf16[1,24,3584]{2,1,0:T(8,128)(2,1)S(1)}, u32[]{:S(2)}, u32[]{:S(2)}) %collective-permute-start.15) | collective-permute-done | bytes 172064 | tf_op jit(solution)/shard_map/ppermute | solution.py:39
  50.7 1.1 %collective-permute-start.16 = (bf16[8,3584]{1,0:T(8,128)(2,1)S(1)}, bf16[8,3584]{1,0:T(8,128)(2,1)S(1)}, u32[]{:S(2)}, u32[]{:S(2)}) collective-permute-start(bf16[8,3584]{1,0:T(8,128)(2,1)S(1)} %get-tuple-element.45), channel_id=1, source_target_pairs={{0,1},{1,0},{2,3},{3,2},{4,5},{5,4},{6,7},{7,6},{8,9},{9,8},{10,11... | collective-permute-start | bytes 172040 | tf_op jit(solution)/shard_map/ppermute | solution.py:48
  51.8 2.1 %collective-permute-start.17 = (bf16[8,3584]{1,0:T(8,128)(2,1)S(1)}, bf16[8,3584]{1,0:T(8,128)(2,1)S(1)}, u32[]{:S(2)}, u32[]{:S(2)}) collective-permute-start(bf16[8,3584]{1,0:T(8,128)(2,1)S(1)} %get-tuple-element.47), channel_id=1, source_target_pairs={{0,2},{1,3},{2,0},{3,1},{4,6},{5,7},{6,4},{7,5},{8,10},{9,11},{10,... | collective-permute-start | bytes 172040 | tf_op jit(solution)/shard_map/ppermute | solution.py:48
  53.9 1.2 %collective-permute-start.18 = (bf16[8,3584]{1,0:T(8,128)(2,1)S(1)}, bf16[8,3584]{1,0:T(8,128)(2,1)S(1)}, u32[]{:S(2)}, u32[]{:S(2)}) collective-permute-start(bf16[8,3584]{1,0:T(8,128)(2,1)S(1)} %get-tuple-element.46), channel_id=1, source_target_pairs={{0,3},{1,2},{2,1},{3,0},{4,7},{5,6},{6,5},{7,4},{8,11},{9,10},{10,... | collective-permute-start | bytes 172040 | tf_op jit(solution)/shard_map/ppermute | solution.py:48
  55.3 2.8 %collective-permute-done.17 = bf16[8,3584]{1,0:T(8,128)(2,1)S(1)} collective-permute-done((bf16[8,3584]{1,0:T(8,128)(2,1)S(1)}, bf16[8,3584]{1,0:T(8,128)(2,1)S(1)}, u32[]{:S(2)}, u32[]{:S(2)}) %collective-permute-start.17) | collective-permute-done | bytes 57376 | tf_op jit(solution)/shard_map/ppermute | solution.py:48
  58.1 1.8 %collective-permute-done.18 = bf16[8,3584]{1,0:T(8,128)(2,1)S(1)} collective-permute-done((bf16[8,3584]{1,0:T(8,128)(2,1)S(1)}, bf16[8,3584]{1,0:T(8,128)(2,1)S(1)}, u32[]{:S(2)}, u32[]{:S(2)}) %collective-permute-start.18) | collective-permute-done | bytes 57376 | tf_op jit(solution)/shard_map/ppermute | solution.py:48
  59.9 0.7 %fusion.19 = bf16[8,3584]{1,0:T(8,128)(2,1)} fusion(f32[8,3584]{1,0:T(8,128)S(1)} %get-tuple-element.28, f32[32,3584]{1,0:T(8,128)S(1)} %get-tuple-element.49, bf16[8,3584]{1,0:T(8,128)(2,1)S(1)} %collective-permute-done.18, bf16[8,3584]{1,0:T(8,128)(2,1)S(1)} %collective-permute-done.17, bf16[8,3584]{1,0:T(8,128)(2,1)S(1)} %collective-permute-done.16), kind=kLoop, calls=%fused_computation.36 | loop fusion | flops 229376 | bytes 458752 | tf_op jit(solution)/shard_map/convert_element_type | solution.py:333
  (72 shorter events, 7.4 us)
Async XLA Ops:
  0.0 1.2 %copy-start.2 = (bf16[1,1,32,16,1024]{4,3,2,1,0:T(8,128)(2,1)S(1)}, bf16[1,1,32,16,1024]{4,3,2,1,0:T(8,128)(2,1)}, u32[]{:S(2)}) copy-start(bf16[1,1,32,16,1024]{4,3,2,1,0:T(8,128)(2,1)} %param.16) | copy-start | bytes 3145732
  1.9 4.1 %copy-start.3 = (bf16[1,1,32,16,1024]{4,3,2,1,0:T(8,128)(2,1)S(1)}, bf16[1,1,32,16,1024]{4,3,2,1,0:T(8,128)(2,1)}, u32[]{:S(2)}) copy-start(bf16[1,1,32,16,1024]{4,3,2,1,0:T(8,128)(2,1)} %param.16) | copy-start | bytes 3145732
  1.9 4.1 %copy-start.4 = (bf16[8,3584]{1,0:T(8,128)(2,1)S(1)}, bf16[8,3584]{1,0:T(8,128)(2,1)}, u32[]{:S(2)}) copy-start(bf16[8,3584]{1,0:T(8,128)(2,1)} %queries_ref.1) | copy-start | bytes 172036
  1.9 4.1 %copy-start.5 = (bf16[8,1024]{1,0:T(8,128)(2,1)S(1)}, bf16[8,1024]{1,0:T(8,128)(2,1)}, u32[]{:S(2)}) copy-start(bf16[8,1024]{1,0:T(8,128)(2,1)} %fresh_ref.1) | copy-start | bytes 49156
  1.9 4.1 %copy-start.6 = (s32[4,8]{1,0:T(4,128)S(1)}, s32[4,8]{1,0:T(4,128)}, u32[]{:S(2)}) copy-start(s32[4,8]{1,0:T(4,128)} %table_ref.1) | copy-start | bytes 388
  1.9 4.1 %copy-start.7 = (s32[1,1,2,4]{3,2,1,0:T(2,128)S(1)}, s32[1,1,2,4]{3,2,1,0:T(2,128)}, u32[]{:S(2)}) copy-start(s32[1,1,2,4]{3,2,1,0:T(2,128)} %param.20) | copy-start | bytes 100
  1.9 4.1 %copy-start.8 = (s32[4]{0:T(128)S(1)}, s32[4]{0:T(128)}, u32[]{:S(2)}) copy-start(s32[4]{0:T(128)} %length_ref.1) | copy-start | bytes 52
  1.9 6.9 %copy-start.9 = (bf16[8,3584]{1,0:T(8,128)(2,1)S(1)}, bf16[8,3584]{1,0:T(8,128)(2,1)}, u32[]{:S(2)}) copy-start(bf16[8,3584]{1,0:T(8,128)(2,1)} %resid_ref.1) | copy-start | bytes 172036
  1.9 6.9 %copy-start.10 = (bf16[3584]{0:T(1024)(128)(2,1)S(1)}, bf16[3584]{0:T(1024)(128)(2,1)}, u32[]{:S(2)}) copy-start(bf16[3584]{0:T(1024)(128)(2,1)} %gain_ref.1) | copy-start | bytes 21508
  2.5 6.0 %collective-permute-start = (bf16[64,1024]{1,0:T(8,128)(2,1)S(1)}, bf16[64,1024]{1,0:T(8,128)(2,1)S(1)}, u32[]{:S(2)}, u32[]{:S(2)}) collective-permute-start(bf16[64,1024]{1,0:T(8,128)(2,1)S(1)} %bitcast.46), channel_id=1, source_target_pairs={{0,4},{4,8},{8,12},{12,16},{16,20},{20,24},{24,28},{28,0},{1,5},{5... | collective-permute-start | bytes 393224 | tf_op jit(solution)/shard_map/ppermute | solution.py:34
  3.0 5.8 %collective-permute-start.1 = (bf16[64,1024]{1,0:T(8,128)(2,1)S(1)}, bf16[64,1024]{1,0:T(8,128)(2,1)S(1)}, u32[]{:S(2)}, u32[]{:S(2)}) collective-permute-start(bf16[64,1024]{1,0:T(8,128)(2,1)S(1)} %bitcast.45), channel_id=1, source_target_pairs={{4,0},{8,4},{12,8},{16,12},{20,16},{24,20},{28,24},{0,28},{5,1},{9... | collective-permute-start | bytes 393224 | tf_op jit(solution)/shard_map/ppermute | solution.py:34
  8.8 5.4 %copy-start.12 = (s32[32,8]{0,1:T(8,128)S(1)}, s32[32,8]{0,1:T(8,128)}, u32[]{:S(2)}) copy-start(s32[32,8]{0,1:T(8,128)} %param.21) | copy-start | bytes 3076
  9.5 9.4 %collective-permute-start.2 = (bf16[8,3584]{1,0:T(8,128)(2,1)S(1)}, bf16[8,3584]{1,0:T(8,128)(2,1)S(1)}, u32[]{:S(2)}, u32[]{:S(2)}) collective-permute-start(bf16[8,3584]{1,0:T(8,128)(2,1)S(1)} %get-tuple-element.32), channel_id=1, source_target_pairs={{0,1},{1,0},{2,3},{3,2},{4,5},{5,4},{6,7},{7,6},{8,9},{9,8},{10,11... | collective-permute-start | bytes 172040 | tf_op jit(solution)/shard_map/ppermute | solution.py:48
  11.7 7.2 %collective-permute-start.3 = (bf16[8,3584]{1,0:T(8,128)(2,1)S(1)}, bf16[8,3584]{1,0:T(8,128)(2,1)S(1)}, u32[]{:S(2)}, u32[]{:S(2)}) collective-permute-start(bf16[8,3584]{1,0:T(8,128)(2,1)S(1)} %get-tuple-element.32), channel_id=1, source_target_pairs={{0,2},{1,3},{2,0},{3,1},{4,6},{5,7},{6,4},{7,5},{8,10},{9,11},{10,... | collective-permute-start | bytes 172040 | tf_op jit(solution)/shard_map/ppermute | solution.py:48
  14.3 6.4 %collective-permute-start.4 = (bf16[8,3584]{1,0:T(8,128)(2,1)S(1)}, bf16[8,3584]{1,0:T(8,128)(2,1)S(1)}, u32[]{:S(2)}, u32[]{:S(2)}) collective-permute-start(bf16[8,3584]{1,0:T(8,128)(2,1)S(1)} %get-tuple-element.32), channel_id=1, source_target_pairs={{0,3},{1,2},{2,1},{3,0},{4,7},{5,6},{6,5},{7,4},{8,11},{9,10},{10,... | collective-permute-start | bytes 172040 | tf_op jit(solution)/shard_map/ppermute | solution.py:48
  15.3 3.1 %copy-start = (bf16[1,1,3584,1024]{3,2,1,0:T(8,128)(2,1)S(1)}, bf16[1,1,3584,1024]{3,2,1,0:T(8,128)(2,1)}, u32[]{:S(2)}) copy-start(bf16[1,1,3584,1024]{3,2,1,0:T(8,128)(2,1)} %param.24) | copy-start | bytes 22020100
  21.1 7.3 %collective-permute-start.5 = (bf16[24,3584]{1,0:T(8,128)(2,1)S(1)}, bf16[24,3584]{1,0:T(8,128)(2,1)S(1)}, u32[]{:S(2)}, u32[]{:S(2)}) collective-permute-start(bf16[24,3584]{1,0:T(8,128)(2,1)S(1)} %get-tuple-element.44), channel_id=1, source_target_pairs={{0,8},{4,12},{8,0},{12,4},{16,24},{20,28},{24,16},{28,20},{1,9},{5... | collective-permute-start | bytes 516104 | tf_op jit(solution)/shard_map/ppermute | solution.py:39
  21.9 10.1 %collective-permute-start.6 = (bf16[24,3584]{1,0:T(8,128)(2,1)S(1)}, bf16[24,3584]{1,0:T(8,128)(2,1)S(1)}, u32[]{:S(2)}, u32[]{:S(2)}) collective-permute-start(bf16[24,3584]{1,0:T(8,128)(2,1)S(1)} %get-tuple-element.43), channel_id=1, source_target_pairs={{0,16},{4,20},{8,24},{12,28},{16,0},{20,4},{24,8},{28,12},{1,17},{... | collective-permute-start | bytes 516104 | tf_op jit(solution)/shard_map/ppermute | solution.py:39
  23.5 8.5 %collective-permute-start.7 = (bf16[24,3584]{1,0:T(8,128)(2,1)S(1)}, bf16[24,3584]{1,0:T(8,128)(2,1)S(1)}, u32[]{:S(2)}, u32[]{:S(2)}) collective-permute-start(bf16[24,3584]{1,0:T(8,128)(2,1)S(1)} %get-tuple-element.42), channel_id=1, source_target_pairs={{0,24},{4,28},{8,16},{12,20},{16,8},{20,12},{24,0},{28,4},{1,25},{... | collective-permute-start | bytes 516104 | tf_op jit(solution)/shard_map/ppermute | solution.py:39
  24.7 7.9 %collective-permute-start.8 = (bf16[24,3584]{1,0:T(8,128)(2,1)S(1)}, bf16[24,3584]{1,0:T(8,128)(2,1)S(1)}, u32[]{:S(2)}, u32[]{:S(2)}) collective-permute-start(bf16[24,3584]{1,0:T(8,128)(2,1)S(1)} %get-tuple-element.41), channel_id=1, source_target_pairs={{0,4},{4,0},{8,12},{12,8},{16,20},{20,16},{24,28},{28,24},{1,5},{5... | collective-permute-start | bytes 516104 | tf_op jit(solution)/shard_map/ppermute | solution.py:44
  24.7 3.1 %copy-start.1 = (bf16[1,1,1024,3584]{3,2,1,0:T(8,128)(2,1)S(1)}, bf16[1,1,1024,3584]{3,2,1,0:T(8,128)(2,1)}, u32[]{:S(2)}) copy-start(bf16[1,1,1024,3584]{3,2,1,0:T(8,128)(2,1)} %param.25) | copy-start | bytes 22020100
  28.4 4.2 %collective-permute-start.9 = (bf16[24,3584]{1,0:T(8,128)(2,1)S(1)}, bf16[24,3584]{1,0:T(8,128)(2,1)S(1)}, u32[]{:S(2)}, u32[]{:S(2)}) collective-permute-start(bf16[24,3584]{1,0:T(8,128)(2,1)S(1)} %collective-permute-done.5), channel_id=1, source_target_pairs={{0,4},{4,0},{8,12},{12,8},{16,20},{20,16},{24,28},{28,24},{1,5},{5... | collective-permute-start | bytes 516104 | tf_op jit(solution)/shard_map/ppermute | solution.py:44
  32.0 1.4 %collective-permute-start.10 = (bf16[24,3584]{1,0:T(8,128)(2,1)S(1)}, bf16[24,3584]{1,0:T(8,128)(2,1)S(1)}, u32[]{:S(2)}, u32[]{:S(2)}) collective-permute-start(bf16[24,3584]{1,0:T(8,128)(2,1)S(1)} %collective-permute-done.6), channel_id=1, source_target_pairs={{0,4},{4,0},{8,12},{12,8},{16,20},{20,16},{24,28},{28,24},{1,5},{5... | collective-permute-start | bytes 516104 | tf_op jit(solution)/shard_map/ppermute | solution.py:44
  32.0 1.6 %collective-permute-start.11 = (bf16[24,3584]{1,0:T(8,128)(2,1)S(1)}, bf16[24,3584]{1,0:T(8,128)(2,1)S(1)}, u32[]{:S(2)}, u32[]{:S(2)}) collective-permute-start(bf16[24,3584]{1,0:T(8,128)(2,1)S(1)} %collective-permute-done.7), channel_id=1, source_target_pairs={{0,4},{4,0},{8,12},{12,8},{16,20},{20,16},{24,28},{28,24},{1,5},{5... | collective-permute-start | bytes 516104 | tf_op jit(solution)/shard_map/ppermute | solution.py:44
  36.7 2.2 %collective-permute-start.12 = (bf16[96,3584]{1,0:T(8,128)(2,1)S(1)}, bf16[96,3584]{1,0:T(8,128)(2,1)S(1)}, u32[]{:S(2)}, u32[]{:S(2)}) collective-permute-start(bf16[96,3584]{1,0:T(8,128)(2,1)S(1)} %convolution_convert_fusion), channel_id=1, source_target_pairs={{0,4},{4,0},{8,12},{12,8},{16,20},{20,16},{24,28},{28,24},{1,5},{5... | collective-permute-start | bytes 2064392 | tf_op jit(solution)/shard_map/ppermute | solution.py:44
  39.1 3.6 %copy-start.13 = (f32[32,8]{0,1:T(8,128)S(1)}, f32[32,8]{0,1:T(8,128)}, u32[]{:S(2)}) copy-start(f32[32,8]{0,1:T(8,128)} %param.22) | copy-start | bytes 3076
  39.1 7.3 %collective-permute-start.13 = (bf16[1,24,3584]{2,1,0:T(8,128)(2,1)S(1)}, bf16[1,24,3584]{2,1,0:T(8,128)(2,1)S(1)}, u32[]{:S(2)}, u32[]{:S(2)}) collective-permute-start(bf16[1,24,3584]{2,1,0:T(8,128)(2,1)S(1)} %get-tuple-element.40), channel_id=1, source_target_pairs={{0,8},{4,12},{8,0},{12,4},{16,24},{20,28},{24,16},{28,20},{1,9},{5... | collective-permute-start | bytes 516104 | tf_op jit(solution)/shard_map/ppermute | solution.py:39
  39.8 9.0 %collective-permute-start.14 = (bf16[1,24,3584]{2,1,0:T(8,128)(2,1)S(1)}, bf16[1,24,3584]{2,1,0:T(8,128)(2,1)S(1)}, u32[]{:S(2)}, u32[]{:S(2)}) collective-permute-start(bf16[1,24,3584]{2,1,0:T(8,128)(2,1)S(1)} %get-tuple-element.39), channel_id=1, source_target_pairs={{0,16},{4,20},{8,24},{12,28},{16,0},{20,4},{24,8},{28,12},{1,17},{... | collective-permute-start | bytes 516104 | tf_op jit(solution)/shard_map/ppermute | solution.py:39
  41.2 9.0 %collective-permute-start.15 = (bf16[1,24,3584]{2,1,0:T(8,128)(2,1)S(1)}, bf16[1,24,3584]{2,1,0:T(8,128)(2,1)S(1)}, u32[]{:S(2)}, u32[]{:S(2)}) collective-permute-start(bf16[1,24,3584]{2,1,0:T(8,128)(2,1)S(1)} %get-tuple-element.38), channel_id=1, source_target_pairs={{0,24},{4,28},{8,16},{12,20},{16,8},{20,12},{24,0},{28,4},{1,25},{... | collective-permute-start | bytes 516104 | tf_op jit(solution)/shard_map/ppermute | solution.py:39
  50.7 4.6 %collective-permute-start.16 = (bf16[8,3584]{1,0:T(8,128)(2,1)S(1)}, bf16[8,3584]{1,0:T(8,128)(2,1)S(1)}, u32[]{:S(2)}, u32[]{:S(2)}) collective-permute-start(bf16[8,3584]{1,0:T(8,128)(2,1)S(1)} %get-tuple-element.45), channel_id=1, source_target_pairs={{0,1},{1,0},{2,3},{3,2},{4,5},{5,4},{6,7},{7,6},{8,9},{9,8},{10,11... | collective-permute-start | bytes 172040 | tf_op jit(solution)/shard_map/ppermute | solution.py:48
  51.8 6.3 %collective-permute-start.17 = (bf16[8,3584]{1,0:T(8,128)(2,1)S(1)}, bf16[8,3584]{1,0:T(8,128)(2,1)S(1)}, u32[]{:S(2)}, u32[]{:S(2)}) collective-permute-start(bf16[8,3584]{1,0:T(8,128)(2,1)S(1)} %get-tuple-element.47), channel_id=1, source_target_pairs={{0,2},{1,3},{2,0},{3,1},{4,6},{5,7},{6,4},{7,5},{8,10},{9,11},{10,... | collective-permute-start | bytes 172040 | tf_op jit(solution)/shard_map/ppermute | solution.py:48
  53.9 6.0 %collective-permute-start.18 = (bf16[8,3584]{1,0:T(8,128)(2,1)S(1)}, bf16[8,3584]{1,0:T(8,128)(2,1)S(1)}, u32[]{:S(2)}, u32[]{:S(2)}) collective-permute-start(bf16[8,3584]{1,0:T(8,128)(2,1)S(1)} %get-tuple-element.46), channel_id=1, source_target_pairs={{0,3},{1,2},{2,1},{3,0},{4,7},{5,6},{6,5},{7,4},{8,11},{9,10},{10,... | collective-permute-start | bytes 172040 | tf_op jit(solution)/shard_map/ppermute | solution.py:48
  (1 other events, 0.7 us)

commit v3 on v2

--- a/solution.py
+++ b/solution.py
@@ -23,7 +23,7 @@
 
 
 def partner_of(index, steps):
-    return index ^ jnp.arange(len(steps) + 1, dtype=jnp.int32)
+    return index ^ jnp.array([0] + [step[0] for step in steps], dtype=jnp.int32)
 
 
 def ring_pages(block, axis, up):
@@ -48,25 +48,40 @@
     return lax.ppermute(block, "exp", list(enumerate(step)))
 
 
-def send_pages_kernel(source_ref, pool_ref, up_ref, down_ref):
+def opening_kernel(out_ref):
+    out_ref[...] = jnp.zeros_like(out_ref)
+
+
+def opening():
+    return pl.pallas_call(
+        opening_kernel,
+        out_shape=jax.ShapeDtypeStruct((8, HEAD_DIM), jnp.float32),
+        out_specs=pl.BlockSpec(memory_space=pltpu.VMEM),
+        compiler_params=pltpu.CompilerParams(vmem_limit_bytes=1024 * 1024),
+        cost_estimate=pl.CostEstimate(flops=4 * 1024 * 1024 * 1024, bytes_accessed=4096, transcendentals=0),
+        name="opening",
+    )()
+
+
+def send_pages_kernel(source_ref, pool_ref, after_ref, up_ref, down_ref):
     for side, out_ref in enumerate((up_ref, down_ref)):
         for i in range(out_ref.shape[0]):
             out_ref[i] = pool_ref[source_ref[side, i]]
 
 
-def send_pages(pool_pages, sources):
+def send_pages(pool_pages, sources, after):
     pages = jax.ShapeDtypeStruct((sources.shape[1],) + pool_pages.shape[1:], pool_pages.dtype)
     return pl.pallas_call(
         send_pages_kernel,
         out_shape=(pages, pages),
-        in_specs=[pl.BlockSpec(memory_space=pltpu.SMEM), pl.BlockSpec(memory_space=pltpu.VMEM)],
+        in_specs=[pl.BlockSpec(memory_space=pltpu.SMEM)] + [pl.BlockSpec(memory_space=pltpu.VMEM)] * 2,
         out_specs=(pl.BlockSpec(memory_space=pltpu.VMEM),) * 2,
         compiler_params=pltpu.CompilerParams(vmem_limit_bytes=4 * 1024 * 1024),
         cost_estimate=pl.CostEstimate(
             flops=4 * 1024 * 1024 * 1024, bytes_accessed=pool_pages.size * pool_pages.dtype.itemsize, transcendentals=0
         ),
         name="send_pages",
-    )(sources, pool_pages)
+    )(sources, pool_pages, after)
 
 
 def weighted_values(weights, values):
@@ -212,30 +227,92 @@
         in_specs=[pl.BlockSpec(memory_space=pltpu.VMEM)] * 9,
         out_specs=(pl.BlockSpec(memory_space=pltpu.VMEM),) * 2,
         compiler_params=pltpu.CompilerParams(vmem_limit_bytes=4 * 1024 * 1024),
-        cost_estimate=pl.CostEstimate(flops=8 * 1024 * 1024 * 1024, bytes_accessed=2 * 1024 * 1024, transcendentals=60 * 1024),
+        cost_estimate=pl.CostEstimate(flops=1024 * 1024 * 1024, bytes_accessed=2 * 1024 * 1024, transcendentals=60 * 1024),
         name="arrived_attention",
     )(resid_in, gain, low, high, *parts)
 
 
-def load_kernel(weight_ref, out_ref, sem):
-    copy = pltpu.make_async_copy(weight_ref, out_ref, sem)
-    copy.start()
-    copy.wait()
-
-
-def load(weight):
-    return pl.pallas_call(
-        load_kernel,
-        out_shape=jax.ShapeDtypeStruct(weight.shape, weight.dtype),
-        in_specs=[pl.BlockSpec(memory_space=pltpu.HBM)],
+def pack_kernel(columns_ref, *refs):
+    out_refs = refs[-EXP_DEV:]
+    rows = jnp.concatenate([ref[...].astype(jnp.float32) for ref in refs[:-EXP_DEV]], axis=0)
+    slots = jnp.dot(columns_ref[...], rows.astype(jnp.bfloat16), preferred_element_type=jnp.float32)
+    for k, out_ref in enumerate(out_refs):
+        out_ref[...] = slots[k * CAP : (k + 1) * CAP].astype(out_ref.dtype)
+
+
+def pack(columns, parts):
+    slots = jax.ShapeDtypeStruct((CAP, parts[0].shape[1]), parts[0].dtype)
+    return pl.pallas_call(
+        pack_kernel,
+        out_shape=(slots,) * EXP_DEV,
+        in_specs=[pl.BlockSpec(memory_space=pltpu.VMEM)] * (1 + len(parts)),
+        out_specs=(pl.BlockSpec(memory_space=pltpu.VMEM),) * EXP_DEV,
+        compiler_params=pltpu.CompilerParams(vmem_limit_bytes=8 * 1024 * 1024),
+        cost_estimate=pl.CostEstimate(
+            flops=8 * 1024 * 1024 * 1024, bytes_accessed=2 * 1024 * 1024, transcendentals=0
+        ),
+        name="pack",
+    )(columns.reshape(EXP_DEV * CAP, -1), *parts)
+
+
+def expert_kernel(rows_ref, inner_ref, outer_ref, own_ref, others_ref):
+    rows = rows_ref[...]
+    own = own_ref.shape[0]
+    tile = min(2 * HEAD_DIM, own_ref.shape[1])
+    parts = []
+    for c in range(0, own_ref.shape[1], tile):
+        hidden = jnp.dot(rows, inner_ref[:, c : c + tile], preferred_element_type=jnp.float32)
+        activated = (hidden / (1.0 + jnp.exp(-hidden))).astype(own_ref.dtype)
+        own_ref[:, c : c + tile] = activated[:own]
+        parts.append(activated[own:])
+    activated = jnp.concatenate(parts, axis=1)
+    tile = 2 * HEAD_DIM
+    for c in range(0, others_ref.shape[1], tile):
+        others_ref[:, c : c + tile] = jnp.dot(
+            activated, outer_ref[:, c : c + tile], preferred_element_type=jnp.float32
+        ).astype(others_ref.dtype)
+
+
+def expert(rows, inner, outer, own):
+    return pl.pallas_call(
+        expert_kernel,
+        out_shape=(
+            jax.ShapeDtypeStruct((own, inner.shape[1]), rows.dtype),
+            jax.ShapeDtypeStruct((rows.shape[0] - own, outer.shape[1]), rows.dtype),
+        ),
+        in_specs=[pl.BlockSpec(memory_space=pltpu.VMEM)] * 3,
+        out_specs=(pl.BlockSpec(memory_space=pltpu.VMEM),) * 2,
+        compiler_params=pltpu.CompilerParams(vmem_limit_bytes=32 * 1024 * 1024),
+        cost_estimate=pl.CostEstimate(
+            flops=2 * rows.shape[0] * (inner.size + outer.size),
+            bytes_accessed=(inner.size + outer.size) * inner.dtype.itemsize,
+            transcendentals=rows.shape[0] * inner.shape[1],
+        ),
+        name="expert",
+    )(rows, inner, outer)
+
+
+def own_rows_kernel(rows_ref, outer_ref, out_ref):
+    rows = rows_ref[...]
+    tile = 2 * HEAD_DIM
+    for c in range(0, out_ref.shape[1], tile):
+        out_ref[:, c : c + tile] = jnp.dot(rows, outer_ref[:, c : c + tile], preferred_element_type=jnp.float32)
+
+
+def own_rows(rows, outer):
+    return pl.pallas_call(
+        own_rows_kernel,
+        out_shape=jax.ShapeDtypeStruct((rows.shape[0], outer.shape[1]), jnp.float32),
+        in_specs=[pl.BlockSpec(memory_space=pltpu.VMEM)] * 2,
         out_specs=pl.BlockSpec(memory_space=pltpu.VMEM),
-        scratch_shapes=[pltpu.SemaphoreType.DMA],
-        compiler_params=pltpu.CompilerParams(vmem_limit_bytes=1024 * 1024),
+        compiler_params=pltpu.CompilerParams(vmem_limit_bytes=16 * 1024 * 1024),
         cost_estimate=pl.CostEstimate(
-            flops=0, bytes_accessed=2 * weight.size * weight.dtype.itemsize, transcendentals=0
+            flops=2 * rows.shape[0] * outer.size,
+            bytes_accessed=outer.size * outer.dtype.itemsize,
+            transcendentals=0,
         ),
-        name="load_weight",
-    )(weight)
+        name="own_rows",
+    )(rows, outer)
 
 
 def body(
@@ -257,22 +334,20 @@
     model_width = resid_in.shape[1]
     exp_count = lax.axis_size("exp")
     group_size = lax.axis_size("req") // EXP_DEV
-    plane_steps = partner_steps(EXP_DEV)
+    plane_steps = partner_steps(EXP_DEV)[::-1]
     group_steps = partner_steps(group_size)
     exp_steps = partner_steps(exp_count)
 
     pool_pages = kv_pool[0, 0]
     targets = mig_target[0, 0]
-    up, down = send_pages(pool_pages, mig_source[0, 0])
+    up, down = send_pages(pool_pages, mig_source[0, 0], opening())
     moved_shape = (up.shape[0] * up.shape[1], up.shape[2])
     from_low = ring_pages(up.reshape(moved_shape), "req", True)
     from_high = ring_pages(down.reshape(moved_shape), "req", False)
 
     parts = local_attention(block_table, lengths, targets, queries, fresh_kv, pool_pages)
     residual, normed = arrived_attention(resid_in, norm_gain, from_low, from_high, parts)
-    normed, expert_ids, gate_values, inner = lax.optimization_barrier(
-        (normed, expert_ids, gate_values, w_in[0, 0])
-    )
+    normed, expert_ids, gate_values = lax.optimization_barrier((normed, expert_ids, gate_values))
 
     exp_order = partner_of(lax.axis_index("exp"), exp_steps)
     plane_order = partner_of(lax.axis_index("req") // group_size, plane_steps)
@@ -287,13 +362,7 @@
     columns = placement.astype(jnp.bfloat16)
     gate_columns = jnp.where(placement, gate_local[:, None, :], 0.0)
 
-    gathered = jnp.concatenate([normed] + [swap_exp(normed, step) for step in exp_steps], axis=0)
-    packed = jnp.einsum(
-        "kct,td->kcd", columns, gathered, preferred_element_type=jnp.float32
-    ).astype(jnp.bfloat16)
-    packed, outer = lax.optimization_barrier((packed, w_out[0, 0]))
-    inner = load(inner)
-    outer = load(outer)
+    packed = pack(columns, [normed] + [swap_exp(normed, step) for step in exp_steps])
     pieces = [packed[0]] + [
         swap_plane(packed[k + 1], step, group_size) for k, step in enumerate(plane_steps)
     ]
@@ -301,19 +370,13 @@
         pieces + [swap_group(piece, step, group_size) for step in group_steps for piece in pieces], axis=0
     )
 
-    hidden = lax.optimization_barrier(jnp.dot(inbound, inner, preferred_element_type=jnp.float32))
-    activated = lax.optimization_barrier(jax.nn.silu(hidden).astype(jnp.bfloat16))
-
-    def outer_rows(rows):
-        return jnp.dot(rows, outer, preferred_element_type=jnp.float32)
-
     share = EXP_DEV * CAP
-    others = outer_rows(activated[share:]).astype(jnp.bfloat16)
+    activated, others = expert(inbound, w_in[0, 0], w_out[0, 0], share)
     arrived = [
         swap_group(others[k * share : (k + 1) * share], step, group_size) for k, step in enumerate(group_steps)
     ]
     activated, others = lax.optimization_barrier((activated, others))
-    summed = lax.optimization_barrier(outer_rows(activated[:share]))
+    summed = own_rows(activated, w_out[0, 0])
     for part in arrived:
         summed = summed + part.astype(jnp.float32)
     summed = summed.astype(jnp.bfloat16).reshape(EXP_DEV, CAP, model_width)

time: 60.8 us -> 58.5 us (0.962)
  local copies, waits for them, and re-layouts: 9.7 us -> 2.94 us
  waiting for transfers between devices: 18.8 us -> 24.8 us
  matrix products: 4.95 us -> 0.46 us
  Pallas kernels: 4.14 us -> 7.59 us
    unnamed x35 -> x39, local copies, waits for them, and re-layouts: 8.2 us -> 1.4 us
    dot_general x4 -> x0, matrix products: 4.49 us -> none  [the longest x2 2.59 us: outer_rows(): return jnp.dot(rows, outer, preferred_element_type=jnp.float32)]
    ppermute x6, waiting for transfers between devices: 9.91 us -> 14 us  [swap_plane(): return lax.ppermute(block, 'req', pairs)]
    pallas_call x2 -> x4, Pallas kernels: 0.99 us -> 4.44 us  [the longest x1 2.84 us: expert(): pl.pallas_call(expert_kernel, out_shape=(jax.ShapeDtypeStruct((own, inner...]
    ppermute x6, waiting for transfers between devices: 6.55 us -> 8.5 us  [swap_exp(): return lax.ppermute(block, 'exp', list(enumerate(step)))]
  transfers between devices with their start and end apart: 19 -> 19, of which waited for: 14 -> 13; matrix products, arithmetic and copies ran while one was open for 5% -> 4% of each run, Pallas kernels for 5% -> 6%
where the time goes in v3:
time: 58.5 us; the launch traced here: 58.3 us
  waiting for transfers between devices  24.8 us (42%)
  starting transfers between devices  20.9 us (36%)
  Pallas kernels  7.59 us (13%)
  local copies, waits for them, and re-layouts  2.94 us (5%)
  other arithmetic  1.33 us (2%)
    ppermute x6, waiting for transfers between devices, swap_plane(): return lax.ppermute(block, 'req', pairs)  14 us
    ppermute x6, starting transfers between devices, swap_exp(): return lax.ppermute(block, 'exp', list(enumerate(step)))  9.19 us
    ppermute x6, waiting for transfers between devices, swap_exp(): return lax.ppermute(block, 'exp', list(enumerate(step)))  8.5 us
    ppermute x6, starting transfers between devices, swap_plane(): return lax.ppermute(block, 'req', pairs)  7.19 us
    ppermute x2, starting transfers between devices, ring_pages(): return lax.ppermute(block, axis, pairs)  3.45 us
    pallas_call x1, Pallas kernels, expert(): pl.pallas_call(expert_kernel, out_shape=(jax.ShapeDtypeStruct((own, inner...  2.84 us
    pallas_call x1, Pallas kernels, local_attention(): pl.pallas_call(local_attention_kernel, out_shape=(part, part, part, part,...  1.93 us
    ppermute x5, waiting for transfers between devices, swap_group(): return lax.ppermute(block, 'req', pairs)  1.46 us
  transfers between devices with their start and end apart: 19, of which 13 were waited for; matrix products, arithmetic and copies ran while one was open for 4% of the time, Pallas kernels for 6%

profile of v3, /device:TPU:0, one launch (start us, length us, event | category | flops | bytes accessed | tf_op | source)
XLA Modules:
  0.0 58.3 jit_solution(12901201510748913543)
XLA Ops:
  0.0 0.7 %copy-done.8 = s32[1,1,2,4]{3,2,1,0:T(2,128)S(1)} copy-done((s32[1,1,2,4]{3,2,1,0:T(2,128)S(1)}, s32[1,1,2,4]{3,2,1,0:T(2,128)}, u32[]{:S(2)}) %copy-start.8) | copy-done | bytes 56
  0.7 0.6 copy-done
  1.3 0.6 send_pages.1
  2.4 2.9 %collective-permute-start.1 = (bf16[64,1024]{1,0:T(8,128)(2,1)S(1)}, bf16[64,1024]{1,0:T(8,128)(2,1)S(1)}, u32[]{:S(2)}, u32[]{:S(2)}) collective-permute-start(bf16[64,1024]{1,0:T(8,128)(2,1)S(1)} %bitcast.39), channel_id=1, source_target_pairs={{4,0},{8,4},{12,8},{16,12},{20,16},{24,20},{28,24},{0,28},{5,1},{9... | collective-permute-start | bytes 393224 | tf_op jit(solution)/shard_map/ppermute | solution.py:34
  5.5 1.9 %local_attention.1 = (f32[4,56,128]{2,1,0:T(8,128)S(1)}, f32[4,56,128]{2,1,0:T(8,128)S(1)}, f32[4,56,128]{2,1,0:T(8,128)S(1)}, f32[4,56,128]{2,1,0:T(8,128)S(1)}, f32[56,128]{1,0:T(8,128)S(1)}) custom-call(s32[4,8]{1,0:T(4,128)S(1)} %copy-done.3, s32[4]{0:T(128)S(1)} %copy-done.5, s32[2,4]{1,0:T(2,128)S(1)} %bitcast.38, bf16[8,3584]{1,0:T(8,128)(2,1)S(1)} %copy-done.1, ...), custom_call_target="tpu_custom_call" | custom-call | flops 41943040 | bytes 2097152 | tf_op jit(solution)/shard_map/local_attention/pallas_call | solution.py:167
  7.4 0.5 collective-permute-done.low_ref
  8.2 0.7 %arrived_attention.1 = (f32[8,3584]{1,0:T(8,128)S(1)}, bf16[8,3584]{1,0:T(8,128)(2,1)S(1)}) custom-call(bf16[8,3584]{1,0:T(8,128)(2,1)S(1)} %copy-done.6, bf16[3584]{0:T(1024)(128)(2,1)S(1)} %copy-done.7, bf16[64,1024]{1,0:T(8,128)(2,1)S(1)} %collective-permute-done.low_ref, bf16[64,1024]{1,0:T(8,128)(2,1)S(1)} %collective-permute-done.1.high_ref, ...), custom_call_target="tpu_custom_call" | custom-call | flops 1073741824 | bytes 2097152 | tf_op jit(solution)/shard_map/arrived_attention/pallas_call | solution.py:224
  8.9 2.1 %collective-permute-start.2 = (bf16[8,3584]{1,0:T(8,128)(2,1)S(1)}, bf16[8,3584]{1,0:T(8,128)(2,1)S(1)}, u32[]{:S(2)}, u32[]{:S(2)}) collective-permute-start(bf16[8,3584]{1,0:T(8,128)(2,1)S(1)} %get-tuple-element.35.refs_0_), channel_id=1, source_target_pairs={{0,1},{1,0},{2,3},{3,2},{4,5},{5,4},{6,7},{7,6},{8,9},{9,8},{10,11... | collective-permute-start | bytes 172040 | tf_op jit(solution)/shard_map/ppermute | solution.py:48
  11.0 2.6 %collective-permute-start.3 = (bf16[8,3584]{1,0:T(8,128)(2,1)S(1)}, bf16[8,3584]{1,0:T(8,128)(2,1)S(1)}, u32[]{:S(2)}, u32[]{:S(2)}) collective-permute-start(bf16[8,3584]{1,0:T(8,128)(2,1)S(1)} %get-tuple-element.35.refs_0_), channel_id=1, source_target_pairs={{0,2},{1,3},{2,0},{3,1},{4,6},{5,7},{6,4},{7,5},{8,10},{9,11},{10,... | collective-permute-start | bytes 172040 | tf_op jit(solution)/shard_map/ppermute | solution.py:48
  13.7 0.5 gather_fusion
  14.7 3.2 %collective-permute-done.3.refs_2_ = bf16[8,3584]{1,0:T(8,128)(2,1)S(1)} collective-permute-done((bf16[8,3584]{1,0:T(8,128)(2,1)S(1)}, bf16[8,3584]{1,0:T(8,128)(2,1)S(1)}, u32[]{:S(2)}, u32[]{:S(2)}) %collective-permute-start.3) | collective-permute-done | bytes 57376 | tf_op jit(solution)/shard_map/ppermute | solution.py:48
  17.9 2.1 %collective-permute-done.4.refs_3_ = bf16[8,3584]{1,0:T(8,128)(2,1)S(1)} collective-permute-done((bf16[8,3584]{1,0:T(8,128)(2,1)S(1)}, bf16[8,3584]{1,0:T(8,128)(2,1)S(1)}, u32[]{:S(2)}, u32[]{:S(2)}) %collective-permute-start.4) | collective-permute-done | bytes 57376 | tf_op jit(solution)/shard_map/ppermute | solution.py:48
  20.3 1.8 %collective-permute-start.5 = (bf16[24,3584]{1,0:T(8,128)(2,1)S(1)}, bf16[24,3584]{1,0:T(8,128)(2,1)S(1)}, u32[]{:S(2)}, u32[]{:S(2)}) collective-permute-start(bf16[24,3584]{1,0:T(8,128)(2,1)S(1)} %get-tuple-element.37), channel_id=1, source_target_pairs={{0,24},{4,28},{8,16},{12,20},{16,8},{20,12},{24,0},{28,4},{1,25},{... | collective-permute-start | bytes 516104 | tf_op jit(solution)/shard_map/ppermute | solution.py:39
  22.3 0.5 collective-permute-start.6
  22.8 1.3 %collective-permute-start.7 = (bf16[24,3584]{1,0:T(8,128)(2,1)S(1)}, bf16[24,3584]{1,0:T(8,128)(2,1)S(1)}, u32[]{:S(2)}, u32[]{:S(2)}) collective-permute-start(bf16[24,3584]{1,0:T(8,128)(2,1)S(1)} %get-tuple-element.39), channel_id=1, source_target_pairs={{0,8},{4,12},{8,0},{12,4},{16,24},{20,28},{24,16},{28,20},{1,9},{5... | collective-permute-start | bytes 516104 | tf_op jit(solution)/shard_map/ppermute | solution.py:39
  24.1 4.0 %collective-permute-done.5 = bf16[24,3584]{1,0:T(8,128)(2,1)S(1)} collective-permute-done((bf16[24,3584]{1,0:T(8,128)(2,1)S(1)}, bf16[24,3584]{1,0:T(8,128)(2,1)S(1)}, u32[]{:S(2)}, u32[]{:S(2)}) %collective-permute-start.5) | collective-permute-done | bytes 172064 | tf_op jit(solution)/shard_map/ppermute | solution.py:39
  28.1 3.0 %collective-permute-done.6 = bf16[24,3584]{1,0:T(8,128)(2,1)S(1)} collective-permute-done((bf16[24,3584]{1,0:T(8,128)(2,1)S(1)}, bf16[24,3584]{1,0:T(8,128)(2,1)S(1)}, u32[]{:S(2)}, u32[]{:S(2)}) %collective-permute-start.6) | collective-permute-done | bytes 172064 | tf_op jit(solution)/shard_map/ppermute | solution.py:39
  31.1 0.5 collective-permute-start.11
  31.7 0.7 %collective-permute-done.10 = bf16[24,3584]{1,0:T(8,128)(2,1)S(1)} collective-permute-done((bf16[24,3584]{1,0:T(8,128)(2,1)S(1)}, bf16[24,3584]{1,0:T(8,128)(2,1)S(1)}, u32[]{:S(2)}, u32[]{:S(2)}) %collective-permute-start.10) | collective-permute-done | bytes 172064 | tf_op jit(solution)/shard_map/ppermute | solution.py:44
  32.7 2.8 %expert.1 = (bf16[96,1024]{1,0:T(8,128)(2,1)S(1)}, bf16[96,3584]{1,0:T(8,128)(2,1)S(1)}) custom-call(bf16[192,3584]{1,0:T(8,128)(2,1)S(1)} %constant_dynamic-update-slice_fusion.rows_ref, bf16[3584,1024]{1,0:T(8,128)(2,1)S(1)} %bitcast.35, bf16[1024,3584]{1,0:T(8,128)(2,1)S(1)} %bitcast.31), custom_call_target="tpu_custom_call" | custom-call | flops 2818572288 | bytes 14680064 | tf_op jit(solution)/shard_map/expert/pallas_call | solution.py:277
  36.0 1.3 %own_rows.1 = f32[96,3584]{1,0:T(8,128)S(1)} custom-call(bf16[96,1024]{1,0:T(8,128)(2,1)S(1)} %get-tuple-element.40.rows_ref, bf16[1024,3584]{1,0:T(8,128)(2,1)S(1)} %bitcast.32), custom_call_target="tpu_custom_call" | custom-call | flops 704643072 | bytes 7340032 | tf_op jit(solution)/shard_map/own_rows/pallas_call | solution.py:303
  38.0 1.4 %collective-permute-start.15 = (bf16[1,24,3584]{2,1,0:T(8,128)(2,1)S(1)}, bf16[1,24,3584]{2,1,0:T(8,128)(2,1)S(1)}, u32[]{:S(2)}, u32[]{:S(2)}) collective-permute-start(bf16[1,24,3584]{2,1,0:T(8,128)(2,1)S(1)} %get-tuple-element.43), channel_id=1, source_target_pairs={{0,8},{4,12},{8,0},{12,4},{16,24},{20,28},{24,16},{28,20},{1,9},{5... | collective-permute-start | bytes 516104 | tf_op jit(solution)/shard_map/ppermute | solution.py:39
  39.4 1.2 %collective-permute-start.14 = (bf16[1,24,3584]{2,1,0:T(8,128)(2,1)S(1)}, bf16[1,24,3584]{2,1,0:T(8,128)(2,1)S(1)}, u32[]{:S(2)}, u32[]{:S(2)}) collective-permute-start(bf16[1,24,3584]{2,1,0:T(8,128)(2,1)S(1)} %get-tuple-element.44), channel_id=1, source_target_pairs={{0,16},{4,20},{8,24},{12,28},{16,0},{20,4},{24,8},{28,12},{1,17},{... | collective-permute-start | bytes 516104 | tf_op jit(solution)/shard_map/ppermute | solution.py:39
  40.7 0.9 %collective-permute-start.13 = (bf16[1,24,3584]{2,1,0:T(8,128)(2,1)S(1)}, bf16[1,24,3584]{2,1,0:T(8,128)(2,1)S(1)}, u32[]{:S(2)}, u32[]{:S(2)}) collective-permute-start(bf16[1,24,3584]{2,1,0:T(8,128)(2,1)S(1)} %get-tuple-element.45), channel_id=1, source_target_pairs={{0,24},{4,28},{8,16},{12,20},{16,8},{20,12},{24,0},{28,4},{1,25},{... | collective-permute-start | bytes 516104 | tf_op jit(solution)/shard_map/ppermute | solution.py:39
  41.7 0.5 gather_fusion.1
  42.4 2.9 %collective-permute-done.15 = bf16[1,24,3584]{2,1,0:T(8,128)(2,1)S(1)} collective-permute-done((bf16[1,24,3584]{2,1,0:T(8,128)(2,1)S(1)}, bf16[1,24,3584]{2,1,0:T(8,128)(2,1)S(1)}, u32[]{:S(2)}, u32[]{:S(2)}) %collective-permute-start.15) | collective-permute-done | bytes 172064 | tf_op jit(solution)/shard_map/ppermute | solution.py:39
  45.3 4.2 %collective-permute-done.14 = bf16[1,24,3584]{2,1,0:T(8,128)(2,1)S(1)} collective-permute-done((bf16[1,24,3584]{2,1,0:T(8,128)(2,1)S(1)}, bf16[1,24,3584]{2,1,0:T(8,128)(2,1)S(1)}, u32[]{:S(2)}, u32[]{:S(2)}) %collective-permute-start.14) | collective-permute-done | bytes 172064 | tf_op jit(solution)/shard_map/ppermute | solution.py:39
  50.0 1.7 %collective-permute-start.18 = (bf16[8,3584]{1,0:T(8,128)(2,1)S(1)}, bf16[8,3584]{1,0:T(8,128)(2,1)S(1)}, u32[]{:S(2)}, u32[]{:S(2)}) collective-permute-start(bf16[8,3584]{1,0:T(8,128)(2,1)S(1)} %get-tuple-element.47), channel_id=1, source_target_pairs={{0,3},{1,2},{2,1},{3,0},{4,7},{5,6},{6,5},{7,4},{8,11},{9,10},{10,... | collective-permute-start | bytes 172040 | tf_op jit(solution)/shard_map/ppermute | solution.py:48
  51.8 2.6 %collective-permute-start.16 = (bf16[8,3584]{1,0:T(8,128)(2,1)S(1)}, bf16[8,3584]{1,0:T(8,128)(2,1)S(1)}, u32[]{:S(2)}, u32[]{:S(2)}) collective-permute-start(bf16[8,3584]{1,0:T(8,128)(2,1)S(1)} %get-tuple-element.46), channel_id=1, source_target_pairs={{0,1},{1,0},{2,3},{3,2},{4,5},{5,4},{6,7},{7,6},{8,9},{9,8},{10,11... | collective-permute-start | bytes 172040 | tf_op jit(solution)/shard_map/ppermute | solution.py:48
  54.4 1.7 %collective-permute-done.18 = bf16[8,3584]{1,0:T(8,128)(2,1)S(1)} collective-permute-done((bf16[8,3584]{1,0:T(8,128)(2,1)S(1)}, bf16[8,3584]{1,0:T(8,128)(2,1)S(1)}, u32[]{:S(2)}, u32[]{:S(2)}) %collective-permute-start.18) | collective-permute-done | bytes 57376 | tf_op jit(solution)/shard_map/ppermute | solution.py:48
  56.1 1.5 %collective-permute-done.17 = bf16[8,3584]{1,0:T(8,128)(2,1)S(1)} collective-permute-done((bf16[8,3584]{1,0:T(8,128)(2,1)S(1)}, bf16[8,3584]{1,0:T(8,128)(2,1)S(1)}, u32[]{:S(2)}, u32[]{:S(2)}) %collective-permute-start.17) | collective-permute-done | bytes 57376 | tf_op jit(solution)/shard_map/ppermute | solution.py:48
  57.6 0.7 %fusion.10 = bf16[8,3584]{1,0:T(8,128)(2,1)} fusion(f32[8,3584]{1,0:T(8,128)S(1)} %get-tuple-element.31, f32[32,3584]{1,0:T(8,128)S(1)} %get-tuple-element.50, bf16[8,3584]{1,0:T(8,128)(2,1)S(1)} %collective-permute-done.18, bf16[8,3584]{1,0:T(8,128)(2,1)S(1)} %collective-permute-done.17, bf16[8,3584]{1,0:T(8,128)(2,1)S(1)} %collective-permute-done.16), kind=kLoop, calls=%fused_computation.19 | loop fusion | flops 229376 | bytes 458752 | tf_op jit(solution)/shard_map/convert_element_type | solution.py:396
  (77 shorter events, 4.3 us)
Async XLA Ops:
  1.2 4.1 %copy-start.11 = (s32[4]{0:T(128)S(1)}, s32[4]{0:T(128)}, u32[]{:S(2)}) copy-start(s32[4]{0:T(128)} %constant.40.clone) | copy-start | bytes 52
  1.2 4.2 %copy-start.1 = (bf16[8,3584]{1,0:T(8,128)(2,1)S(1)}, bf16[8,3584]{1,0:T(8,128)(2,1)}, u32[]{:S(2)}) copy-start(bf16[8,3584]{1,0:T(8,128)(2,1)} %queries_ref.1) | copy-start | bytes 172036
  1.2 4.2 %copy-start.2 = (bf16[8,1024]{1,0:T(8,128)(2,1)S(1)}, bf16[8,1024]{1,0:T(8,128)(2,1)}, u32[]{:S(2)}) copy-start(bf16[8,1024]{1,0:T(8,128)(2,1)} %fresh_ref.1) | copy-start | bytes 49156
  1.2 4.2 %copy-start.3 = (s32[4,8]{1,0:T(4,128)S(1)}, s32[4,8]{1,0:T(4,128)}, u32[]{:S(2)}) copy-start(s32[4,8]{1,0:T(4,128)} %table_ref.1) | copy-start | bytes 388
  1.3 4.2 %copy-start.4 = (s32[1,1,2,4]{3,2,1,0:T(2,128)S(1)}, s32[1,1,2,4]{3,2,1,0:T(2,128)}, u32[]{:S(2)}) copy-start(s32[1,1,2,4]{3,2,1,0:T(2,128)} %param.22) | copy-start | bytes 100
  1.3 4.2 %copy-start.5 = (s32[4]{0:T(128)S(1)}, s32[4]{0:T(128)}, u32[]{:S(2)}) copy-start(s32[4]{0:T(128)} %length_ref.1) | copy-start | bytes 52
  1.3 6.9 %copy-start.6 = (bf16[8,3584]{1,0:T(8,128)(2,1)S(1)}, bf16[8,3584]{1,0:T(8,128)(2,1)}, u32[]{:S(2)}) copy-start(bf16[8,3584]{1,0:T(8,128)(2,1)} %resid_ref.1) | copy-start | bytes 172036
  1.3 6.9 %copy-start.7 = (bf16[3584]{0:T(1024)(128)(2,1)S(1)}, bf16[3584]{0:T(1024)(128)(2,1)}, u32[]{:S(2)}) copy-start(bf16[3584]{0:T(1024)(128)(2,1)} %gain_ref.1) | copy-start | bytes 21508
  1.9 6.0 %collective-permute-start = (bf16[64,1024]{1,0:T(8,128)(2,1)S(1)}, bf16[64,1024]{1,0:T(8,128)(2,1)S(1)}, u32[]{:S(2)}, u32[]{:S(2)}) collective-permute-start(bf16[64,1024]{1,0:T(8,128)(2,1)S(1)} %bitcast.40), channel_id=1, source_target_pairs={{0,4},{4,8},{8,12},{12,16},{16,20},{20,24},{24,28},{28,0},{1,5},{5... | collective-permute-start | bytes 393224 | tf_op jit(solution)/shard_map/ppermute | solution.py:34
  2.4 5.8 %collective-permute-start.1 = (bf16[64,1024]{1,0:T(8,128)(2,1)S(1)}, bf16[64,1024]{1,0:T(8,128)(2,1)S(1)}, u32[]{:S(2)}, u32[]{:S(2)}) collective-permute-start(bf16[64,1024]{1,0:T(8,128)(2,1)S(1)} %bitcast.39), channel_id=1, source_target_pairs={{4,0},{8,4},{12,8},{16,12},{20,16},{24,20},{28,24},{0,28},{5,1},{9... | collective-permute-start | bytes 393224 | tf_op jit(solution)/shard_map/ppermute | solution.py:34
  8.2 5.4 %copy-start.9 = (s32[32,8]{0,1:T(8,128)S(1)}, s32[32,8]{0,1:T(8,128)}, u32[]{:S(2)}) copy-start(s32[32,8]{0,1:T(8,128)} %param.23) | copy-start | bytes 3076
  8.9 5.9 %collective-permute-start.2 = (bf16[8,3584]{1,0:T(8,128)(2,1)S(1)}, bf16[8,3584]{1,0:T(8,128)(2,1)S(1)}, u32[]{:S(2)}, u32[]{:S(2)}) collective-permute-start(bf16[8,3584]{1,0:T(8,128)(2,1)S(1)} %get-tuple-element.35.refs_0_), channel_id=1, source_target_pairs={{0,1},{1,0},{2,3},{3,2},{4,5},{5,4},{6,7},{7,6},{8,9},{9,8},{10,11... | collective-permute-start | bytes 172040 | tf_op jit(solution)/shard_map/ppermute | solution.py:48
  11.0 6.9 %collective-permute-start.3 = (bf16[8,3584]{1,0:T(8,128)(2,1)S(1)}, bf16[8,3584]{1,0:T(8,128)(2,1)S(1)}, u32[]{:S(2)}, u32[]{:S(2)}) collective-permute-start(bf16[8,3584]{1,0:T(8,128)(2,1)S(1)} %get-tuple-element.35.refs_0_), channel_id=1, source_target_pairs={{0,2},{1,3},{2,0},{3,1},{4,6},{5,7},{6,4},{7,5},{8,10},{9,11},{10,... | collective-permute-start | bytes 172040 | tf_op jit(solution)/shard_map/ppermute | solution.py:48
  13.6 6.4 %collective-permute-start.4 = (bf16[8,3584]{1,0:T(8,128)(2,1)S(1)}, bf16[8,3584]{1,0:T(8,128)(2,1)S(1)}, u32[]{:S(2)}, u32[]{:S(2)}) collective-permute-start(bf16[8,3584]{1,0:T(8,128)(2,1)S(1)} %get-tuple-element.35.refs_0_), channel_id=1, source_target_pairs={{0,3},{1,2},{2,1},{3,0},{4,7},{5,6},{6,5},{7,4},{8,11},{9,10},{10,... | collective-permute-start | bytes 172040 | tf_op jit(solution)/shard_map/ppermute | solution.py:48
  14.6 18.1 %slice-start = ((s8[7340032]{0:T(1024)(128)(4,1)}), s8[4194304]{0:T(1024)(128)(4,1)S(1)}, s32[]{:S(2)}) async-start(s8[7340032]{0:T(1024)(128)(4,1)} %bitcast.29), calls=%async_computation | async-start | bytes 8388608
  14.6 18.1 %slice-start.2 = ((s8[7340032]{0:T(1024)(128)(4,1)}), s8[4194304]{0:T(1024)(128)(4,1)S(1)}, s32[]{:S(2)}) async-start(s8[7340032]{0:T(1024)(128)(4,1)} %bitcast.33), calls=%async_computation.2 | async-start | bytes 8388608
  14.7 18.0 %slice-start.1 = ((s8[7340032]{0:T(1024)(128)(4,1)}), s8[3145728]{0:T(1024)(128)(4,1)S(1)}, s32[]{:S(2)}) async-start(s8[7340032]{0:T(1024)(128)(4,1)} %bitcast.29), calls=%async_computation.1 | async-start | bytes 6291456
  14.7 18.0 %slice-start.3 = ((s8[7340032]{0:T(1024)(128)(4,1)}), s8[3145728]{0:T(1024)(128)(4,1)S(1)}, s32[]{:S(2)}) async-start(s8[7340032]{0:T(1024)(128)(4,1)} %bitcast.33), calls=%async_computation.3 | async-start | bytes 6291456
  20.3 7.7 %collective-permute-start.5 = (bf16[24,3584]{1,0:T(8,128)(2,1)S(1)}, bf16[24,3584]{1,0:T(8,128)(2,1)S(1)}, u32[]{:S(2)}, u32[]{:S(2)}) collective-permute-start(bf16[24,3584]{1,0:T(8,128)(2,1)S(1)} %get-tuple-element.37), channel_id=1, source_target_pairs={{0,24},{4,28},{8,16},{12,20},{16,8},{20,12},{24,0},{28,4},{1,25},{... | collective-permute-start | bytes 516104 | tf_op jit(solution)/shard_map/ppermute | solution.py:39
  22.2 9.5 %collective-permute-start.8 = (bf16[24,3584]{1,0:T(8,128)(2,1)S(1)}, bf16[24,3584]{1,0:T(8,128)(2,1)S(1)}, u32[]{:S(2)}, u32[]{:S(2)}) collective-permute-start(bf16[24,3584]{1,0:T(8,128)(2,1)S(1)} %get-tuple-element.36), channel_id=1, source_target_pairs={{0,4},{4,0},{8,12},{12,8},{16,20},{20,16},{24,28},{28,24},{1,5},{5... | collective-permute-start | bytes 516104 | tf_op jit(solution)/shard_map/ppermute | solution.py:44
  22.3 8.8 %collective-permute-start.6 = (bf16[24,3584]{1,0:T(8,128)(2,1)S(1)}, bf16[24,3584]{1,0:T(8,128)(2,1)S(1)}, u32[]{:S(2)}, u32[]{:S(2)}) collective-permute-start(bf16[24,3584]{1,0:T(8,128)(2,1)S(1)} %get-tuple-element.38), channel_id=1, source_target_pairs={{0,16},{4,20},{8,24},{12,28},{16,0},{20,4},{24,8},{28,12},{1,17},{... | collective-permute-start | bytes 516104 | tf_op jit(solution)/shard_map/ppermute | solution.py:39
  22.8 8.3 %collective-permute-start.7 = (bf16[24,3584]{1,0:T(8,128)(2,1)S(1)}, bf16[24,3584]{1,0:T(8,128)(2,1)S(1)}, u32[]{:S(2)}, u32[]{:S(2)}) collective-permute-start(bf16[24,3584]{1,0:T(8,128)(2,1)S(1)} %get-tuple-element.39), channel_id=1, source_target_pairs={{0,8},{4,12},{8,0},{12,4},{16,24},{20,28},{24,16},{28,20},{1,9},{5... | collective-permute-start | bytes 516104 | tf_op jit(solution)/shard_map/ppermute | solution.py:39
  28.0 3.6 %collective-permute-start.9 = (bf16[24,3584]{1,0:T(8,128)(2,1)S(1)}, bf16[24,3584]{1,0:T(8,128)(2,1)S(1)}, u32[]{:S(2)}, u32[]{:S(2)}) collective-permute-start(bf16[24,3584]{1,0:T(8,128)(2,1)S(1)} %collective-permute-done.5), channel_id=1, source_target_pairs={{0,4},{4,0},{8,12},{12,8},{16,20},{20,16},{24,28},{28,24},{1,5},{5... | collective-permute-start | bytes 516104 | tf_op jit(solution)/shard_map/ppermute | solution.py:44
  31.0 1.4 %collective-permute-start.10 = (bf16[24,3584]{1,0:T(8,128)(2,1)S(1)}, bf16[24,3584]{1,0:T(8,128)(2,1)S(1)}, u32[]{:S(2)}, u32[]{:S(2)}) collective-permute-start(bf16[24,3584]{1,0:T(8,128)(2,1)S(1)} %collective-permute-done.6), channel_id=1, source_target_pairs={{0,4},{4,0},{8,12},{12,8},{16,20},{20,16},{24,28},{28,24},{1,5},{5... | collective-permute-start | bytes 516104 | tf_op jit(solution)/shard_map/ppermute | solution.py:44
  31.1 1.6 %collective-permute-start.11 = (bf16[24,3584]{1,0:T(8,128)(2,1)S(1)}, bf16[24,3584]{1,0:T(8,128)(2,1)S(1)}, u32[]{:S(2)}, u32[]{:S(2)}) collective-permute-start(bf16[24,3584]{1,0:T(8,128)(2,1)S(1)} %collective-permute-done.7), channel_id=1, source_target_pairs={{0,4},{4,0},{8,12},{12,8},{16,20},{20,16},{24,28},{28,24},{1,5},{5... | collective-permute-start | bytes 516104 | tf_op jit(solution)/shard_map/ppermute | solution.py:44
  35.6 2.2 %collective-permute-start.12 = (bf16[96,3584]{1,0:T(8,128)(2,1)S(1)}, bf16[96,3584]{1,0:T(8,128)(2,1)S(1)}, u32[]{:S(2)}, u32[]{:S(2)}) collective-permute-start(bf16[96,3584]{1,0:T(8,128)(2,1)S(1)} %get-tuple-element.41), channel_id=1, source_target_pairs={{0,4},{4,0},{8,12},{12,8},{16,20},{20,16},{24,28},{28,24},{1,5},{5... | collective-permute-start | bytes 2064392 | tf_op jit(solution)/shard_map/ppermute | solution.py:44
  38.0 7.3 %collective-permute-start.15 = (bf16[1,24,3584]{2,1,0:T(8,128)(2,1)S(1)}, bf16[1,24,3584]{2,1,0:T(8,128)(2,1)S(1)}, u32[]{:S(2)}, u32[]{:S(2)}) collective-permute-start(bf16[1,24,3584]{2,1,0:T(8,128)(2,1)S(1)} %get-tuple-element.43), channel_id=1, source_target_pairs={{0,8},{4,12},{8,0},{12,4},{16,24},{20,28},{24,16},{28,20},{1,9},{5... | collective-permute-start | bytes 516104 | tf_op jit(solution)/shard_map/ppermute | solution.py:39
  39.4 10.0 %collective-permute-start.14 = (bf16[1,24,3584]{2,1,0:T(8,128)(2,1)S(1)}, bf16[1,24,3584]{2,1,0:T(8,128)(2,1)S(1)}, u32[]{:S(2)}, u32[]{:S(2)}) collective-permute-start(bf16[1,24,3584]{2,1,0:T(8,128)(2,1)S(1)} %get-tuple-element.44), channel_id=1, source_target_pairs={{0,16},{4,20},{8,24},{12,28},{16,0},{20,4},{24,8},{28,12},{1,17},{... | collective-permute-start | bytes 516104 | tf_op jit(solution)/shard_map/ppermute | solution.py:39
  40.7 8.8 %collective-permute-start.13 = (bf16[1,24,3584]{2,1,0:T(8,128)(2,1)S(1)}, bf16[1,24,3584]{2,1,0:T(8,128)(2,1)S(1)}, u32[]{:S(2)}, u32[]{:S(2)}) collective-permute-start(bf16[1,24,3584]{2,1,0:T(8,128)(2,1)S(1)} %get-tuple-element.45), channel_id=1, source_target_pairs={{0,24},{4,28},{8,16},{12,20},{16,8},{20,12},{24,0},{28,4},{1,25},{... | collective-permute-start | bytes 516104 | tf_op jit(solution)/shard_map/ppermute | solution.py:39
  50.0 6.2 %collective-permute-start.18 = (bf16[8,3584]{1,0:T(8,128)(2,1)S(1)}, bf16[8,3584]{1,0:T(8,128)(2,1)S(1)}, u32[]{:S(2)}, u32[]{:S(2)}) collective-permute-start(bf16[8,3584]{1,0:T(8,128)(2,1)S(1)} %get-tuple-element.47), channel_id=1, source_target_pairs={{0,3},{1,2},{2,1},{3,0},{4,7},{5,6},{6,5},{7,4},{8,11},{9,10},{10,... | collective-permute-start | bytes 172040 | tf_op jit(solution)/shard_map/ppermute | solution.py:48
  51.7 6.0 %collective-permute-start.17 = (bf16[8,3584]{1,0:T(8,128)(2,1)S(1)}, bf16[8,3584]{1,0:T(8,128)(2,1)S(1)}, u32[]{:S(2)}, u32[]{:S(2)}) collective-permute-start(bf16[8,3584]{1,0:T(8,128)(2,1)S(1)} %get-tuple-element.48), channel_id=1, source_target_pairs={{0,2},{1,3},{2,0},{3,1},{4,6},{5,7},{6,4},{7,5},{8,10},{9,11},{10,... | collective-permute-start | bytes 172040 | tf_op jit(solution)/shard_map/ppermute | solution.py:48
  51.8 5.8 %collective-permute-start.16 = (bf16[8,3584]{1,0:T(8,128)(2,1)S(1)}, bf16[8,3584]{1,0:T(8,128)(2,1)S(1)}, u32[]{:S(2)}, u32[]{:S(2)}) collective-permute-start(bf16[8,3584]{1,0:T(8,128)(2,1)S(1)} %get-tuple-element.46), channel_id=1, source_target_pairs={{0,1},{1,0},{2,3},{3,2},{4,5},{5,4},{6,7},{7,6},{8,9},{9,8},{10,11... | collective-permute-start | bytes 172040 | tf_op jit(solution)/shard_map/ppermute | solution.py:48
  (3 other events, 5.6 us)

commit v4 on v3

--- a/solution.py
+++ b/solution.py
@@ -10,6 +10,7 @@
 HEAD_DIM = 128
 EXP_DEV = 4
 CAP = 24
+PLANE_ORDERS = ((2, 3, 1), (1, 3, 2))
 
 
 neg_big = -1e30
@@ -22,20 +23,26 @@
     return [[i ^ k for i in range(count)] for k in range(1, count)]
 
 
-def partner_of(index, steps):
-    return index ^ jnp.array([0] + [step[0] for step in steps], dtype=jnp.int32)
-
-
-def ring_pages(block, axis, up):
-    count = lax.axis_size(axis)
-    pairs = [(i, (i + 1) % count) for i in range(count)]
-    if not up:
-        pairs = [(target, source) for source, target in pairs]
-    return lax.ppermute(block, axis, pairs)
-
-
-def swap_plane(block, step, group_size):
-    pairs = [(q * group_size + g, p * group_size + g) for q, p in enumerate(step) for g in range(group_size)]
+def partner_of(index, orders, member):
+    return index ^ jnp.array([[0] + list(order) for order in orders], dtype=jnp.int32)[member % len(orders)]
+
+
+def swap_ring(block, offset):
+    count = lax.axis_size("req")
+    if count % 2:
+        raise ValueError("axis size")
+    pairs = []
+    for i in range(offset, count, 2):
+        pairs += [(i, (i + 1) % count), ((i + 1) % count, i)]
+    return lax.ppermute(block, "req", pairs)
+
+
+def swap_plane(block, k, orders, group_size):
+    pairs = [
+        (q * group_size + g, (q ^ orders[g % len(orders)][k]) * group_size + g)
+        for q in range(EXP_DEV)
+        for g in range(group_size)
+    ]
     return lax.ppermute(block, "req", pairs)
 
 
@@ -44,8 +51,14 @@
     return lax.ppermute(block, "req", pairs)
 
 
-def swap_exp(block, step):
-    return lax.ppermute(block, "exp", list(enumerate(step)))
+def swap_exp(block, k, orders, group_size):
+    count = lax.axis_size("exp")
+    pairs = [
+        (r * count + e, r * count + (e ^ orders[r % group_size % len(orders)][k]))
+        for r in range(lax.axis_size("req"))
+        for e in range(count)
+    ]
+    return lax.ppermute(block, ("req", "exp"), pairs)
 
 
 def opening_kernel(out_ref):
@@ -63,8 +76,9 @@
     )()
 
 
-def send_pages_kernel(source_ref, pool_ref, after_ref, up_ref, down_ref):
-    for side, out_ref in enumerate((up_ref, down_ref)):
+def send_pages_kernel(source_ref, pool_ref, after_ref, far_ref, near_ref):
+    odd = lax.rem(lax.axis_index("req"), 2)
+    for side, out_ref in ((1 - odd, far_ref), (odd, near_ref)):
         for i in range(out_ref.shape[0]):
             out_ref[i] = pool_ref[source_ref[side, i]]
 
@@ -150,8 +164,9 @@
     token = lax.broadcasted_iota(jnp.int32, (rows_count, 2 * moved_span), 0) % token_count
     lane = lax.broadcasted_iota(jnp.int32, (rows_count, 2 * moved_span), 1)
     seen = jnp.zeros((rows_count, 2 * moved_span), jnp.float32)
-    for side in range(2):
-        position = lane - side * moved_span
+    odd = lax.rem(lax.axis_index("req"), 2)
+    for block, side in enumerate((odd, 1 - odd)):
+        position = lane - block * moved_span
         for n in range(request_count):
             bound = jnp.where(table_ref[n, 0] == target_ref[side, 0], length_ref[n], 0)
             inside = (position >= 0) & (position < moved_span) & (position < bound)
@@ -176,7 +191,7 @@
 
 
 def arrived_attention_kernel(
-    resid_ref, gain_ref, low_ref, high_ref, max_ref, sum_ref, out_ref, query_ref, bias_ref, residual_ref, normed_ref
+    resid_ref, gain_ref, far_ref, near_ref, max_ref, sum_ref, out_ref, query_ref, bias_ref, residual_ref, normed_ref
 ):
     token_count, model_width = residual_ref.shape
     share = HEADS // KV_HEADS
@@ -185,7 +200,7 @@
 
     def arrived(first):
         at = pl.ds(first, HEAD_DIM)
-        return jnp.concatenate([low_ref[:, at], high_ref[:, at]], axis=0)
+        return jnp.concatenate([far_ref[:, at], near_ref[:, at]], axis=0)
 
     scores = [
         lax.dot_general(
@@ -219,7 +234,7 @@
     normed_ref[...] = (residual * inv_rms * gain_ref[...].astype(jnp.float32)[None, :]).astype(normed_ref.dtype)
 
 
-def arrived_attention(resid_in, gain, low, high, parts):
+def arrived_attention(resid_in, gain, far, near, parts):
     shape = resid_in.shape
     return pl.pallas_call(
         arrived_attention_kernel,
@@ -229,7 +244,7 @@
         compiler_params=pltpu.CompilerParams(vmem_limit_bytes=4 * 1024 * 1024),
         cost_estimate=pl.CostEstimate(flops=1024 * 1024 * 1024, bytes_accessed=2 * 1024 * 1024, transcendentals=60 * 1024),
         name="arrived_attention",
-    )(resid_in, gain, low, high, *parts)
+    )(resid_in, gain, far, near, *parts)
 
 
 def pack_kernel(columns_ref, *refs):
@@ -258,26 +273,24 @@
 def expert_kernel(rows_ref, inner_ref, outer_ref, own_ref, others_ref):
     rows = rows_ref[...]
     own = own_ref.shape[0]
-    tile = min(2 * HEAD_DIM, own_ref.shape[1])
+    tile = min(2 * HEAD_DIM, inner_ref.shape[1])
     parts = []
-    for c in range(0, own_ref.shape[1], tile):
+    for c in range(0, inner_ref.shape[1], tile):
         hidden = jnp.dot(rows, inner_ref[:, c : c + tile], preferred_element_type=jnp.float32)
-        activated = (hidden / (1.0 + jnp.exp(-hidden))).astype(own_ref.dtype)
-        own_ref[:, c : c + tile] = activated[:own]
-        parts.append(activated[own:])
+        parts.append((hidden / (1.0 + jnp.exp(-hidden))).astype(rows.dtype))
     activated = jnp.concatenate(parts, axis=1)
     tile = 2 * HEAD_DIM
-    for c in range(0, others_ref.shape[1], tile):
-        others_ref[:, c : c + tile] = jnp.dot(
-            activated, outer_ref[:, c : c + tile], preferred_element_type=jnp.float32
-        ).astype(others_ref.dtype)
+    for c in range(0, own_ref.shape[1], tile):
+        out = jnp.dot(activated, outer_ref[:, c : c + tile], preferred_element_type=jnp.float32)
+        own_ref[:, c : c + tile] = out[:own]
+        others_ref[:, c : c + tile] = out[own:].astype(others_ref.dtype)
 
 
 def expert(rows, inner, outer, own):
     return pl.pallas_call(
         expert_kernel,
         out_shape=(
-            jax.ShapeDtypeStruct((own, inner.shape[1]), rows.dtype),
+            jax.ShapeDtypeStruct((own, outer.shape[1]), jnp.float32),
             jax.ShapeDtypeStruct((rows.shape[0] - own, outer.shape[1]), rows.dtype),
         ),
         in_specs=[pl.BlockSpec(memory_space=pltpu.VMEM)] * 3,
@@ -292,27 +305,37 @@
     )(rows, inner, outer)
 
 
-def own_rows_kernel(rows_ref, outer_ref, out_ref):
-    rows = rows_ref[...]
-    tile = 2 * HEAD_DIM
-    for c in range(0, out_ref.shape[1], tile):
-        out_ref[:, c : c + tile] = jnp.dot(rows, outer_ref[:, c : c + tile], preferred_element_type=jnp.float32)
-
-
-def own_rows(rows, outer):
-    return pl.pallas_call(
-        own_rows_kernel,
-        out_shape=jax.ShapeDtypeStruct((rows.shape[0], outer.shape[1]), jnp.float32),
-        in_specs=[pl.BlockSpec(memory_space=pltpu.VMEM)] * 2,
-        out_specs=pl.BlockSpec(memory_space=pltpu.VMEM),
-        compiler_params=pltpu.CompilerParams(vmem_limit_bytes=16 * 1024 * 1024),
+def combine_kernel(gate_ref, residual_ref, *refs):
+    block_refs, out_refs = refs[:EXP_DEV], refs[EXP_DEV:]
+    rows = jnp.concatenate([ref[...].astype(jnp.float32) for ref in block_refs], axis=0).astype(jnp.bfloat16)
+    gates = jnp.concatenate([gate_ref[k] for k in range(EXP_DEV)], axis=0)
+    high = gates.astype(jnp.bfloat16)
+    low = (gates - high.astype(jnp.float32)).astype(jnp.bfloat16)
+    mix = lax.dot_general(
+        jnp.concatenate([high.astype(jnp.float32), low.astype(jnp.float32)], axis=1).astype(jnp.bfloat16), rows,
+        (((0,), (0,)), ((), ())), preferred_element_type=jnp.float32,
+    )
+    half = gates.shape[1]
+    mix = mix[:half] + mix[half:]
+    count = out_refs[0].shape[0]
+    out_refs[0][...] = residual_ref[...] + mix[:count]
+    for k, out_ref in enumerate(out_refs[1:]):
+        out_ref[...] = mix[(k + 1) * count : (k + 2) * count].astype(out_ref.dtype)
+
+
+def combine(gate_columns, residual, blocks, partners):
+    sent = jax.ShapeDtypeStruct(residual.shape, jnp.bfloat16)
+    return pl.pallas_call(
+        combine_kernel,
+        out_shape=(jax.ShapeDtypeStruct(residual.shape, jnp.float32),) + (sent,) * partners,
+        in_specs=[pl.BlockSpec(memory_space=pltpu.VMEM)] * (2 + len(blocks)),
+        out_specs=(pl.BlockSpec(memory_space=pltpu.VMEM),) * (1 + partners),
+        compiler_params=pltpu.CompilerParams(vmem_limit_bytes=12 * 1024 * 1024),
         cost_estimate=pl.CostEstimate(
-            flops=2 * rows.shape[0] * outer.size,
-            bytes_accessed=outer.size * outer.dtype.itemsize,
-            transcendentals=0,
+            flops=4 * gate_columns.size * residual.shape[1], bytes_accessed=4 * 1024 * 1024, transcendentals=0
         ),
-        name="own_rows",
-    )(rows, outer)
+        name="combine",
+    )(gate_columns, residual, *blocks)
 
 
 def body(
@@ -334,23 +357,25 @@
     model_width = resid_in.shape[1]
     exp_count = lax.axis_size("exp")
     group_size = lax.axis_size("req") // EXP_DEV
-    plane_steps = partner_steps(EXP_DEV)[::-1]
+    plane_orders = PLANE_ORDERS
+    member = lax.axis_index("req") % group_size
     group_steps = partner_steps(group_size)
-    exp_steps = partner_steps(exp_count)
+    falling = list(range(exp_count - 1, 0, -1))
+    exp_orders = (falling, falling[1::-1] + falling[2:])
 
     pool_pages = kv_pool[0, 0]
     targets = mig_target[0, 0]
-    up, down = send_pages(pool_pages, mig_source[0, 0], opening())
-    moved_shape = (up.shape[0] * up.shape[1], up.shape[2])
-    from_low = ring_pages(up.reshape(moved_shape), "req", True)
-    from_high = ring_pages(down.reshape(moved_shape), "req", False)
+    far, near = send_pages(pool_pages, mig_source[0, 0], opening())
+    moved_shape = (far.shape[0] * far.shape[1], far.shape[2])
+    far = swap_ring(far.reshape(moved_shape), 1)
+    near = swap_ring(near.reshape(moved_shape), 0)
 
     parts = local_attention(block_table, lengths, targets, queries, fresh_kv, pool_pages)
-    residual, normed = arrived_attention(resid_in, norm_gain, from_low, from_high, parts)
+    residual, normed = arrived_attention(resid_in, norm_gain, far, near, parts)
     normed, expert_ids, gate_values = lax.optimization_barrier((normed, expert_ids, gate_values))
 
-    exp_order = partner_of(lax.axis_index("exp"), exp_steps)
-    plane_order = partner_of(lax.axis_index("req") // group_size, plane_steps)
+    exp_order = partner_of(lax.axis_index("exp"), exp_orders, member)
+    plane_order = partner_of(lax.axis_index("req") // group_size, plane_orders, member)
     ids = expert_ids.reshape(exp_count, token_count, -1)[exp_order].reshape(expert_ids.shape)
     gates = gate_values.reshape(exp_count, token_count, -1)[exp_order].reshape(gate_values.shape)
     local_ids = lax.axis_index("exp") * EXP_DEV + plane_order
@@ -362,37 +387,29 @@
     columns = placement.astype(jnp.bfloat16)
     gate_columns = jnp.where(placement, gate_local[:, None, :], 0.0)
 
-    packed = pack(columns, [normed] + [swap_exp(normed, step) for step in exp_steps])
+    packed = pack(columns, [normed] + [swap_exp(normed, k, exp_orders, group_size) for k in range(exp_count - 1)])
     pieces = [packed[0]] + [
-        swap_plane(packed[k + 1], step, group_size) for k, step in enumerate(plane_steps)
+        swap_plane(packed[k + 1], k, plane_orders, group_size) for k in range(EXP_DEV - 1)
     ]
     inbound = jnp.concatenate(
         pieces + [swap_group(piece, step, group_size) for step in group_steps for piece in pieces], axis=0
     )
 
     share = EXP_DEV * CAP
-    activated, others = expert(inbound, w_in[0, 0], w_out[0, 0], share)
+    summed, others = expert(inbound, w_in[0, 0], w_out[0, 0], share)
     arrived = [
         swap_group(others[k * share : (k + 1) * share], step, group_size) for k, step in enumerate(group_steps)
     ]
-    activated, others = lax.optimization_barrier((activated, others))
-    summed = own_rows(activated, w_out[0, 0])
     for part in arrived:
         summed = summed + part.astype(jnp.float32)
-    summed = summed.astype(jnp.bfloat16).reshape(EXP_DEV, CAP, model_width)
-
-    returned = jnp.concatenate(
-        [summed[:1]] + [swap_plane(summed[k + 1 : k + 2], step, group_size) for k, step in enumerate(plane_steps)],
-        axis=0,
-    )
-    mix = jnp.einsum(
-        "kct,kcd->td", gate_columns, returned.astype(jnp.float32), precision=lax.Precision.HIGHEST
-    )
-    blocks = mix.reshape(exp_count, token_count, model_width)
-    result = residual + blocks[0]
-    blocks = blocks.astype(jnp.bfloat16)
-    for k, step in enumerate(exp_steps):
-        result = result + swap_exp(blocks[k + 1], step).astype(jnp.float32)
+    summed = summed.astype(jnp.bfloat16)
+
+    returned = [summed[:CAP]] + [
+        swap_plane(summed[(k + 1) * CAP : (k + 2) * CAP], k, plane_orders, group_size) for k in range(EXP_DEV - 1)
+    ]
+    result, *blocks = combine(gate_columns, residual, returned, exp_count - 1)
+    for k, block in enumerate(blocks):
+        result = result + swap_exp(block, k, exp_orders, group_size).astype(jnp.float32)
     return result.astype(jnp.bfloat16)
 
 

time: 58.5 us -> 57.3 us (0.979)
  starting transfers between devices: 20.9 us -> 22.4 us
  waiting for transfers between devices: 24.8 us -> 23.3 us
  Pallas kernels: 7.59 us -> 6.91 us
    ppermute x6, waiting for transfers between devices: 14 us -> 12.8 us  [swap_plane(): return lax.ppermute(block, 'req', pairs)]
    ppermute x8, starting transfers between devices: 12.6 us -> 13.6 us  [the longest x6 10.2 us: swap_exp(): return lax.ppermute(block, ('req', 'exp'), pairs)]
    ppermute x8, waiting for transfers between devices: 9.27 us -> 8.52 us  [the longest x6 7.4 us: swap_exp(): return lax.ppermute(block, ('req', 'exp'), pairs)]
    pallas_call x2, Pallas kernels: 4.12 us -> 3.44 us  [the longest x1 3.07 us: expert(): pl.pallas_call(expert_kernel, out_shape=(jax.ShapeDtypeStruct((own, outer...]
    unnamed x39 -> x41, local copies, waits for them, and re-layouts: 1.4 us -> 1.39 us
  transfers between devices with their start and end apart: 19 -> 19, of which waited for: 13 -> 13; matrix products, arithmetic and copies ran while one was open for 4% -> 4% of each run, Pallas kernels for 6% -> 3%
where the time goes in v4:
time: 57.3 us; the launch traced here: 57.2 us
  waiting for transfers between devices  23.3 us (41%)
  starting transfers between devices  22.4 us (39%)
  Pallas kernels  6.91 us (12%)
  local copies, waits for them, and re-layouts  2.92 us (5%)
  other arithmetic  1.29 us (2%)
    ppermute x6, waiting for transfers between devices, swap_plane(): return lax.ppermute(block, 'req', pairs)  12.8 us
    ppermute x6, starting transfers between devices, swap_exp(): return lax.ppermute(block, ('req', 'exp'), pairs)  10.2 us
    ppermute x6, waiting for transfers between devices, swap_exp(): return lax.ppermute(block, ('req', 'exp'), pairs)  7.4 us
    ppermute x6, starting transfers between devices, swap_plane(): return lax.ppermute(block, 'req', pairs)  7.17 us
    ppermute x2, starting transfers between devices, swap_ring(): return lax.ppermute(block, 'req', pairs)  3.4 us
    pallas_call x1, Pallas kernels, expert(): pl.pallas_call(expert_kernel, out_shape=(jax.ShapeDtypeStruct((own, outer...  3.07 us
    ppermute x5, waiting for transfers between devices, swap_group(): return lax.ppermute(block, 'req', pairs)  1.96 us
    pallas_call x1, Pallas kernels, local_attention(): pl.pallas_call(local_attention_kernel, out_shape=(part, part, part, part,...  1.92 us
  transfers between devices with their start and end apart: 19, of which 13 were waited for; matrix products, arithmetic and copies ran while one was open for 4% of the time, Pallas kernels for 3%

profile of v4, /device:TPU:0, one launch (start us, length us, event | category | flops | bytes accessed | tf_op | source)
XLA Modules:
  0.0 57.2 jit_solution(6873752501374226294)
XLA Ops:
  0.0 1.2 %copy-done = bf16[1,1,32,16,1024]{4,3,2,1,0:T(8,128)(2,1)S(1)} copy-done((bf16[1,1,32,16,1024]{4,3,2,1,0:T(8,128)(2,1)S(1)}, bf16[1,1,32,16,1024]{4,3,2,1,0:T(8,128)(2,1)}, u32[]{:S(2)}) %copy-start) | copy-done | bytes 1048600
  1.3 0.6 %send_pages.1 = (bf16[4,16,1024]{2,1,0:T(8,128)(2,1)S(1)}, bf16[4,16,1024]{2,1,0:T(8,128)(2,1)S(1)}) custom-call(s32[2,4]{1,0:T(2,128)S(1)} %bitcast.36, bf16[32,16,1024]{2,1,0:T(8,128)(2,1)S(1)} %bitcast.31, f32[8,128]{1,0:T(8,128)S(1)} %opening.1.after_ref), custom_call_target="tpu_custom_call" | custom-call | flops 4294967296 | bytes 1048576 | tf_op jit(solution)/shard_map/send_pages/pallas_call | solution.py:88
  1.9 3.4 %collective-permute-start = (bf16[64,1024]{1,0:T(8,128)(2,1)S(1)}, bf16[64,1024]{1,0:T(8,128)(2,1)S(1)}, u32[]{:S(2)}, u32[]{:S(2)}) collective-permute-start(bf16[64,1024]{1,0:T(8,128)(2,1)S(1)} %bitcast.35), channel_id=1, source_target_pairs={{4,8},{8,4},{12,16},{16,12},{20,24},{24,20},{28,0},{0,28},{5,9},{9... | collective-permute-start | bytes 393224 | tf_op jit(solution)/shard_map/ppermute | solution.py:37
  5.5 1.9 %local_attention.1 = (f32[4,56,128]{2,1,0:T(8,128)S(1)}, f32[4,56,128]{2,1,0:T(8,128)S(1)}, f32[4,56,128]{2,1,0:T(8,128)S(1)}, f32[4,56,128]{2,1,0:T(8,128)S(1)}, f32[56,128]{1,0:T(8,128)S(1)}) custom-call(s32[4,8]{1,0:T(4,128)S(1)} %copy-done.3, s32[4]{0:T(128)S(1)} %copy-done.5, s32[2,4]{1,0:T(2,128)S(1)} %bitcast.33, bf16[8,3584]{1,0:T(8,128)(2,1)S(1)} %copy-done.1, ...), custom_call_target="tpu_custom_call" | custom-call | flops 41943040 | bytes 2097152 | tf_op jit(solution)/shard_map/local_attention/pallas_call | solution.py:182
  7.4 1.1 %collective-permute-done.far_ref = bf16[64,1024]{1,0:T(8,128)(2,1)S(1)} collective-permute-done((bf16[64,1024]{1,0:T(8,128)(2,1)S(1)}, bf16[64,1024]{1,0:T(8,128)(2,1)S(1)}, u32[]{:S(2)}, u32[]{:S(2)}) %collective-permute-start) | collective-permute-done | bytes 131104 | tf_op jit(solution)/shard_map/ppermute | solution.py:37
  8.5 0.7 %arrived_attention.1 = (f32[8,3584]{1,0:T(8,128)S(1)}, bf16[8,3584]{1,0:T(8,128)(2,1)S(1)}) custom-call(bf16[8,3584]{1,0:T(8,128)(2,1)S(1)} %copy-done.6, bf16[3584]{0:T(1024)(128)(2,1)S(1)} %copy-done.7, bf16[64,1024]{1,0:T(8,128)(2,1)S(1)} %collective-permute-done.far_ref, bf16[64,1024]{1,0:T(8,128)(2,1)S(1)} %collective-permute-done.1.near_ref, ...), custom_call_target="tpu_custom_call" | custom-call | flops 1073741824 | bytes 2097152 | tf_op jit(solution)/shard_map/arrived_attention/pallas_call | solution.py:239
  9.2 5.2 %collective-permute-start.2 = (bf16[8,3584]{1,0:T(8,128)(2,1)S(1)}, bf16[8,3584]{1,0:T(8,128)(2,1)S(1)}, u32[]{:S(2)}, u32[]{:S(2)}) collective-permute-start(bf16[8,3584]{1,0:T(8,128)(2,1)S(1)} %get-tuple-element.38.refs_0_), channel_id=1, source_target_pairs={{0,3},{1,2},{2,1},{3,0},{4,6},{5,7},{6,4},{7,5},{8,11},{9,10},{10,... | collective-permute-start | bytes 172040 | tf_op jit(solution)/shard_map/ppermute | solution.py:61
  14.4 0.6 %collective-permute-start.4 = (bf16[8,3584]{1,0:T(8,128)(2,1)S(1)}, bf16[8,3584]{1,0:T(8,128)(2,1)S(1)}, u32[]{:S(2)}, u32[]{:S(2)}) collective-permute-start(bf16[8,3584]{1,0:T(8,128)(2,1)S(1)} %get-tuple-element.38.refs_0_), channel_id=1, source_target_pairs={{0,1},{1,0},{2,3},{3,2},{4,5},{5,4},{6,7},{7,6},{8,9},{9,8},{10,11... | collective-permute-start | bytes 172040 | tf_op jit(solution)/shard_map/ppermute | solution.py:61
  15.1 0.5 gather_fusion
  16.2 1.1 %collective-permute-done.2.refs_1_ = bf16[8,3584]{1,0:T(8,128)(2,1)S(1)} collective-permute-done((bf16[8,3584]{1,0:T(8,128)(2,1)S(1)}, bf16[8,3584]{1,0:T(8,128)(2,1)S(1)}, u32[]{:S(2)}, u32[]{:S(2)}) %collective-permute-start.2) | collective-permute-done | bytes 57376 | tf_op jit(solution)/shard_map/ppermute | solution.py:61
  17.2 2.2 %collective-permute-done.3.refs_2_ = bf16[8,3584]{1,0:T(8,128)(2,1)S(1)} collective-permute-done((bf16[8,3584]{1,0:T(8,128)(2,1)S(1)}, bf16[8,3584]{1,0:T(8,128)(2,1)S(1)}, u32[]{:S(2)}, u32[]{:S(2)}) %collective-permute-start.3) | collective-permute-done | bytes 57376 | tf_op jit(solution)/shard_map/ppermute | solution.py:61
  19.8 1.0 %collective-permute-start.5 = (bf16[24,3584]{1,0:T(8,128)(2,1)S(1)}, bf16[24,3584]{1,0:T(8,128)(2,1)S(1)}, u32[]{:S(2)}, u32[]{:S(2)}) collective-permute-start(bf16[24,3584]{1,0:T(8,128)(2,1)S(1)} %get-tuple-element.40), channel_id=1, source_target_pairs={{0,16},{4,12},{8,24},{12,4},{16,0},{20,28},{24,8},{28,20},{1,17},{... | collective-permute-start | bytes 516104 | tf_op jit(solution)/shard_map/ppermute | solution.py:46
  20.8 1.2 %collective-permute-start.6 = (bf16[24,3584]{1,0:T(8,128)(2,1)S(1)}, bf16[24,3584]{1,0:T(8,128)(2,1)S(1)}, u32[]{:S(2)}, u32[]{:S(2)}) collective-permute-start(bf16[24,3584]{1,0:T(8,128)(2,1)S(1)} %get-tuple-element.41), channel_id=1, source_target_pairs={{0,24},{4,28},{8,16},{12,20},{16,8},{20,12},{24,0},{28,4},{1,25},{... | collective-permute-start | bytes 516104 | tf_op jit(solution)/shard_map/ppermute | solution.py:46
  22.1 1.4 %collective-permute-start.7 = (bf16[24,3584]{1,0:T(8,128)(2,1)S(1)}, bf16[24,3584]{1,0:T(8,128)(2,1)S(1)}, u32[]{:S(2)}, u32[]{:S(2)}) collective-permute-start(bf16[24,3584]{1,0:T(8,128)(2,1)S(1)} %get-tuple-element.42), channel_id=1, source_target_pairs={{0,8},{4,20},{8,0},{12,28},{16,24},{20,4},{24,16},{28,12},{1,9},{5... | collective-permute-start | bytes 516104 | tf_op jit(solution)/shard_map/ppermute | solution.py:46
  23.5 5.8 %collective-permute-done.5 = bf16[24,3584]{1,0:T(8,128)(2,1)S(1)} collective-permute-done((bf16[24,3584]{1,0:T(8,128)(2,1)S(1)}, bf16[24,3584]{1,0:T(8,128)(2,1)S(1)}, u32[]{:S(2)}, u32[]{:S(2)}) %collective-permute-start.5) | collective-permute-done | bytes 172064 | tf_op jit(solution)/shard_map/ppermute | solution.py:46
  29.3 0.6 collective-permute-start.10
  30.1 0.5 collective-permute-start.11
  30.9 0.7 %collective-permute-done.11 = bf16[24,3584]{1,0:T(8,128)(2,1)S(1)} collective-permute-done((bf16[24,3584]{1,0:T(8,128)(2,1)S(1)}, bf16[24,3584]{1,0:T(8,128)(2,1)S(1)}, u32[]{:S(2)}, u32[]{:S(2)}) %collective-permute-start.11) | collective-permute-done | bytes 172064 | tf_op jit(solution)/shard_map/ppermute | solution.py:51
  31.7 3.1 %expert.1 = (f32[96,3584]{1,0:T(8,128)S(1)}, bf16[96,3584]{1,0:T(8,128)(2,1)S(1)}) custom-call(bf16[192,3584]{1,0:T(8,128)(2,1)S(1)} %constant_dynamic-update-slice_fusion.rows_ref, bf16[3584,1024]{1,0:T(8,128)(2,1)S(1)} %bitcast.27, bf16[1024,3584]{1,0:T(8,128)(2,1)S(1)} %bitcast.30), custom_call_target="tpu_custom_call" | custom-call | flops 2818572288 | bytes 14680064 | tf_op jit(solution)/shard_map/expert/pallas_call | solution.py:290
  34.8 0.4 collective-permute-start.12
  35.3 0.5 gather_fusion.1
  36.0 1.0 %collective-permute-done.12 = bf16[96,3584]{1,0:T(8,128)(2,1)S(1)} collective-permute-done((bf16[96,3584]{1,0:T(8,128)(2,1)S(1)}, bf16[96,3584]{1,0:T(8,128)(2,1)S(1)}, u32[]{:S(2)}, u32[]{:S(2)}) %collective-permute-start.12) | collective-permute-done | bytes 688160 | tf_op jit(solution)/shard_map/ppermute | solution.py:51
  37.2 1.0 %collective-permute-start.13 = (bf16[24,3584]{1,0:T(8,128)(2,1)S(1)}, bf16[24,3584]{1,0:T(8,128)(2,1)S(1)}, u32[]{:S(2)}, u32[]{:S(2)}) collective-permute-start(bf16[24,3584]{1,0:T(8,128)(2,1)S(1)} %get-tuple-element.51), channel_id=1, source_target_pairs={{0,16},{4,12},{8,24},{12,4},{16,0},{20,28},{24,8},{28,20},{1,17},{... | collective-permute-start | bytes 516104 | tf_op jit(solution)/shard_map/ppermute | solution.py:46
  38.1 1.5 %collective-permute-start.14 = (bf16[24,3584]{1,0:T(8,128)(2,1)S(1)}, bf16[24,3584]{1,0:T(8,128)(2,1)S(1)}, u32[]{:S(2)}, u32[]{:S(2)}) collective-permute-start(bf16[24,3584]{1,0:T(8,128)(2,1)S(1)} %get-tuple-element.50), channel_id=1, source_target_pairs={{0,24},{4,28},{8,16},{12,20},{16,8},{20,12},{24,0},{28,4},{1,25},{... | collective-permute-start | bytes 516104 | tf_op jit(solution)/shard_map/ppermute | solution.py:46
  39.6 1.1 %collective-permute-start.15 = (bf16[24,3584]{1,0:T(8,128)(2,1)S(1)}, bf16[24,3584]{1,0:T(8,128)(2,1)S(1)}, u32[]{:S(2)}, u32[]{:S(2)}) collective-permute-start(bf16[24,3584]{1,0:T(8,128)(2,1)S(1)} %get-tuple-element.49), channel_id=1, source_target_pairs={{0,8},{4,20},{8,0},{12,28},{16,24},{20,4},{24,16},{28,12},{1,9},{5... | collective-permute-start | bytes 516104 | tf_op jit(solution)/shard_map/ppermute | solution.py:46
  40.7 6.2 %collective-permute-done.13.refs_1_ = bf16[24,3584]{1,0:T(8,128)(2,1)S(1)} collective-permute-done((bf16[24,3584]{1,0:T(8,128)(2,1)S(1)}, bf16[24,3584]{1,0:T(8,128)(2,1)S(1)}, u32[]{:S(2)}, u32[]{:S(2)}) %collective-permute-start.13) | collective-permute-done | bytes 172064 | tf_op jit(solution)/shard_map/ppermute | solution.py:46
  47.0 0.7 %collective-permute-done.15.refs_3_ = bf16[24,3584]{1,0:T(8,128)(2,1)S(1)} collective-permute-done((bf16[24,3584]{1,0:T(8,128)(2,1)S(1)}, bf16[24,3584]{1,0:T(8,128)(2,1)S(1)}, u32[]{:S(2)}, u32[]{:S(2)}) %collective-permute-start.15) | collective-permute-done | bytes 172064 | tf_op jit(solution)/shard_map/ppermute | solution.py:46
  48.0 2.7 %collective-permute-start.16 = (bf16[8,3584]{1,0:T(8,128)(2,1)S(1)}, bf16[8,3584]{1,0:T(8,128)(2,1)S(1)}, u32[]{:S(2)}, u32[]{:S(2)}) collective-permute-start(bf16[8,3584]{1,0:T(8,128)(2,1)S(1)} %get-tuple-element.46), channel_id=1, source_target_pairs={{0,3},{1,2},{2,1},{3,0},{4,6},{5,7},{6,4},{7,5},{8,11},{9,10},{10,... | collective-permute-start | bytes 172040 | tf_op jit(solution)/shard_map/ppermute | solution.py:61
  50.6 1.8 %collective-permute-start.18 = (bf16[8,3584]{1,0:T(8,128)(2,1)S(1)}, bf16[8,3584]{1,0:T(8,128)(2,1)S(1)}, u32[]{:S(2)}, u32[]{:S(2)}) collective-permute-start(bf16[8,3584]{1,0:T(8,128)(2,1)S(1)} %get-tuple-element.48), channel_id=1, source_target_pairs={{0,1},{1,0},{2,3},{3,2},{4,5},{5,4},{6,7},{7,6},{8,9},{9,8},{10,11... | collective-permute-start | bytes 172040 | tf_op jit(solution)/shard_map/ppermute | solution.py:61
  52.4 1.7 %collective-permute-done.16 = bf16[8,3584]{1,0:T(8,128)(2,1)S(1)} collective-permute-done((bf16[8,3584]{1,0:T(8,128)(2,1)S(1)}, bf16[8,3584]{1,0:T(8,128)(2,1)S(1)}, u32[]{:S(2)}, u32[]{:S(2)}) %collective-permute-start.16) | collective-permute-done | bytes 57376 | tf_op jit(solution)/shard_map/ppermute | solution.py:61
  54.1 2.4 %collective-permute-done.17 = bf16[8,3584]{1,0:T(8,128)(2,1)S(1)} collective-permute-done((bf16[8,3584]{1,0:T(8,128)(2,1)S(1)}, bf16[8,3584]{1,0:T(8,128)(2,1)S(1)}, u32[]{:S(2)}, u32[]{:S(2)}) %collective-permute-start.17) | collective-permute-done | bytes 57376 | tf_op jit(solution)/shard_map/ppermute | solution.py:61
  56.5 0.7 %add_convert_fusion.1 = bf16[8,3584]{1,0:T(8,128)(2,1)} fusion(bf16[8,3584]{1,0:T(8,128)(2,1)S(1)} %collective-permute-done.18, bf16[8,3584]{1,0:T(8,128)(2,1)S(1)} %collective-permute-done.17, f32[8,3584]{1,0:T(8,128)S(1)} %get-tuple-element.45, bf16[8,3584]{1,0:T(8,128)(2,1)S(1)} %collective-permute-done.16), kind=kLoop, calls=%fused_computation.3 | loop fusion | flops 200704 | bytes 344064 | tf_op jit(solution)/shard_map/convert_element_type | solution.py:413
  (78 shorter events, 2.5 us)
Async XLA Ops:
  1.2 4.1 %copy-start.11 = (s32[2,4]{1,0:T(2,128)S(1)}, s32[2,4]{1,0:T(2,128)}, u32[]{:S(2)}) copy-start(s32[2,4]{1,0:T(2,128)} %constant.58.clone) | copy-start | bytes 100
  1.2 4.2 %copy-start.1 = (bf16[8,3584]{1,0:T(8,128)(2,1)S(1)}, bf16[8,3584]{1,0:T(8,128)(2,1)}, u32[]{:S(2)}) copy-start(bf16[8,3584]{1,0:T(8,128)(2,1)} %queries_ref.1) | copy-start | bytes 172036
  1.2 4.2 %copy-start.2 = (bf16[8,1024]{1,0:T(8,128)(2,1)S(1)}, bf16[8,1024]{1,0:T(8,128)(2,1)}, u32[]{:S(2)}) copy-start(bf16[8,1024]{1,0:T(8,128)(2,1)} %fresh_ref.1) | copy-start | bytes 49156
  1.2 4.2 %copy-start.3 = (s32[4,8]{1,0:T(4,128)S(1)}, s32[4,8]{1,0:T(4,128)}, u32[]{:S(2)}) copy-start(s32[4,8]{1,0:T(4,128)} %table_ref.1) | copy-start | bytes 388
  1.3 4.2 %copy-start.4 = (s32[1,1,2,4]{3,2,1,0:T(2,128)S(1)}, s32[1,1,2,4]{3,2,1,0:T(2,128)}, u32[]{:S(2)}) copy-start(s32[1,1,2,4]{3,2,1,0:T(2,128)} %param.22) | copy-start | bytes 100
  1.3 4.2 %copy-start.5 = (s32[4]{0:T(128)S(1)}, s32[4]{0:T(128)}, u32[]{:S(2)}) copy-start(s32[4]{0:T(128)} %length_ref.1) | copy-start | bytes 52
  1.3 7.2 %copy-start.6 = (bf16[8,3584]{1,0:T(8,128)(2,1)S(1)}, bf16[8,3584]{1,0:T(8,128)(2,1)}, u32[]{:S(2)}) copy-start(bf16[8,3584]{1,0:T(8,128)(2,1)} %resid_ref.1) | copy-start | bytes 172036
  1.3 7.2 %copy-start.7 = (bf16[3584]{0:T(1024)(128)(2,1)S(1)}, bf16[3584]{0:T(1024)(128)(2,1)}, u32[]{:S(2)}) copy-start(bf16[3584]{0:T(1024)(128)(2,1)} %gain_ref.1) | copy-start | bytes 21508
  1.9 6.6 %collective-permute-start = (bf16[64,1024]{1,0:T(8,128)(2,1)S(1)}, bf16[64,1024]{1,0:T(8,128)(2,1)S(1)}, u32[]{:S(2)}, u32[]{:S(2)}) collective-permute-start(bf16[64,1024]{1,0:T(8,128)(2,1)S(1)} %bitcast.35), channel_id=1, source_target_pairs={{4,8},{8,4},{12,16},{16,12},{20,24},{24,20},{28,0},{0,28},{5,9},{9... | collective-permute-start | bytes 393224 | tf_op jit(solution)/shard_map/ppermute | solution.py:37
  5.3 3.2 %collective-permute-start.1 = (bf16[64,1024]{1,0:T(8,128)(2,1)S(1)}, bf16[64,1024]{1,0:T(8,128)(2,1)S(1)}, u32[]{:S(2)}, u32[]{:S(2)}) collective-permute-start(bf16[64,1024]{1,0:T(8,128)(2,1)S(1)} %bitcast.34), channel_id=1, source_target_pairs={{0,4},{4,0},{8,12},{12,8},{16,20},{20,16},{24,28},{28,24},{1,5},{5... | collective-permute-start | bytes 393224 | tf_op jit(solution)/shard_map/ppermute | solution.py:37
  8.5 6.5 %copy-start.9 = (s32[32,8]{0,1:T(8,128)S(1)}, s32[32,8]{0,1:T(8,128)}, u32[]{:S(2)}) copy-start(s32[32,8]{0,1:T(8,128)} %param.23) | copy-start | bytes 3076
  9.2 8.0 %collective-permute-start.2 = (bf16[8,3584]{1,0:T(8,128)(2,1)S(1)}, bf16[8,3584]{1,0:T(8,128)(2,1)S(1)}, u32[]{:S(2)}, u32[]{:S(2)}) collective-permute-start(bf16[8,3584]{1,0:T(8,128)(2,1)S(1)} %get-tuple-element.38.refs_0_), channel_id=1, source_target_pairs={{0,3},{1,2},{2,1},{3,0},{4,6},{5,7},{6,4},{7,5},{8,11},{9,10},{10,... | collective-permute-start | bytes 172040 | tf_op jit(solution)/shard_map/ppermute | solution.py:61
  14.4 5.1 %collective-permute-start.3 = (bf16[8,3584]{1,0:T(8,128)(2,1)S(1)}, bf16[8,3584]{1,0:T(8,128)(2,1)S(1)}, u32[]{:S(2)}, u32[]{:S(2)}) collective-permute-start(bf16[8,3584]{1,0:T(8,128)(2,1)S(1)} %get-tuple-element.38.refs_0_), channel_id=1, source_target_pairs={{0,2},{1,3},{2,0},{3,1},{4,7},{5,6},{6,5},{7,4},{8,10},{9,11},{10,... | collective-permute-start | bytes 172040 | tf_op jit(solution)/shard_map/ppermute | solution.py:61
  14.4 5.1 %collective-permute-start.4 = (bf16[8,3584]{1,0:T(8,128)(2,1)S(1)}, bf16[8,3584]{1,0:T(8,128)(2,1)S(1)}, u32[]{:S(2)}, u32[]{:S(2)}) collective-permute-start(bf16[8,3584]{1,0:T(8,128)(2,1)S(1)} %get-tuple-element.38.refs_0_), channel_id=1, source_target_pairs={{0,1},{1,0},{2,3},{3,2},{4,5},{5,4},{6,7},{7,6},{8,9},{9,8},{10,11... | collective-permute-start | bytes 172040 | tf_op jit(solution)/shard_map/ppermute | solution.py:61
  16.0 15.6 %slice-start = ((s8[7340032]{0:T(1024)(128)(4,1)}), s8[4194304]{0:T(1024)(128)(4,1)S(1)}, s32[]{:S(2)}) async-start(s8[7340032]{0:T(1024)(128)(4,1)} %bitcast.25), calls=%async_computation | async-start | bytes 8388608
  16.0 15.6 %slice-start.2 = ((s8[7340032]{0:T(1024)(128)(4,1)}), s8[4194304]{0:T(1024)(128)(4,1)S(1)}, s32[]{:S(2)}) async-start(s8[7340032]{0:T(1024)(128)(4,1)} %bitcast.28), calls=%async_computation.2 | async-start | bytes 8388608
  16.1 15.5 %slice-start.1 = ((s8[7340032]{0:T(1024)(128)(4,1)}), s8[3145728]{0:T(1024)(128)(4,1)S(1)}, s32[]{:S(2)}) async-start(s8[7340032]{0:T(1024)(128)(4,1)} %bitcast.25), calls=%async_computation.1 | async-start | bytes 6291456
  16.1 15.5 %slice-start.3 = ((s8[7340032]{0:T(1024)(128)(4,1)}), s8[3145728]{0:T(1024)(128)(4,1)S(1)}, s32[]{:S(2)}) async-start(s8[7340032]{0:T(1024)(128)(4,1)} %bitcast.28), calls=%async_computation.3 | async-start | bytes 6291456
  19.8 9.5 %collective-permute-start.5 = (bf16[24,3584]{1,0:T(8,128)(2,1)S(1)}, bf16[24,3584]{1,0:T(8,128)(2,1)S(1)}, u32[]{:S(2)}, u32[]{:S(2)}) collective-permute-start(bf16[24,3584]{1,0:T(8,128)(2,1)S(1)} %get-tuple-element.40), channel_id=1, source_target_pairs={{0,16},{4,12},{8,24},{12,4},{16,0},{20,28},{24,8},{28,20},{1,17},{... | collective-permute-start | bytes 516104 | tf_op jit(solution)/shard_map/ppermute | solution.py:46
  20.8 9.8 %collective-permute-start.8 = (bf16[24,3584]{1,0:T(8,128)(2,1)S(1)}, bf16[24,3584]{1,0:T(8,128)(2,1)S(1)}, u32[]{:S(2)}, u32[]{:S(2)}) collective-permute-start(bf16[24,3584]{1,0:T(8,128)(2,1)S(1)} %get-tuple-element.39), channel_id=1, source_target_pairs={{0,4},{4,0},{8,12},{12,8},{16,20},{20,16},{24,28},{28,24},{1,5},{5... | collective-permute-start | bytes 516104 | tf_op jit(solution)/shard_map/ppermute | solution.py:51
  20.8 8.5 %collective-permute-start.6 = (bf16[24,3584]{1,0:T(8,128)(2,1)S(1)}, bf16[24,3584]{1,0:T(8,128)(2,1)S(1)}, u32[]{:S(2)}, u32[]{:S(2)}) collective-permute-start(bf16[24,3584]{1,0:T(8,128)(2,1)S(1)} %get-tuple-element.41), channel_id=1, source_target_pairs={{0,24},{4,28},{8,16},{12,20},{16,8},{20,12},{24,0},{28,4},{1,25},{... | collective-permute-start | bytes 516104 | tf_op jit(solution)/shard_map/ppermute | solution.py:46
  22.1 8.0 %collective-permute-start.7 = (bf16[24,3584]{1,0:T(8,128)(2,1)S(1)}, bf16[24,3584]{1,0:T(8,128)(2,1)S(1)}, u32[]{:S(2)}, u32[]{:S(2)}) collective-permute-start(bf16[24,3584]{1,0:T(8,128)(2,1)S(1)} %get-tuple-element.42), channel_id=1, source_target_pairs={{0,8},{4,20},{8,0},{12,28},{16,24},{20,4},{24,16},{28,12},{1,9},{5... | collective-permute-start | bytes 516104 | tf_op jit(solution)/shard_map/ppermute | solution.py:46
  29.3 1.4 %collective-permute-start.9 = (bf16[24,3584]{1,0:T(8,128)(2,1)S(1)}, bf16[24,3584]{1,0:T(8,128)(2,1)S(1)}, u32[]{:S(2)}, u32[]{:S(2)}) collective-permute-start(bf16[24,3584]{1,0:T(8,128)(2,1)S(1)} %collective-permute-done.5), channel_id=1, source_target_pairs={{0,4},{4,0},{8,12},{12,8},{16,20},{20,16},{24,28},{28,24},{1,5},{5... | collective-permute-start | bytes 516104 | tf_op jit(solution)/shard_map/ppermute | solution.py:51
  29.3 1.6 %collective-permute-start.10 = (bf16[24,3584]{1,0:T(8,128)(2,1)S(1)}, bf16[24,3584]{1,0:T(8,128)(2,1)S(1)}, u32[]{:S(2)}, u32[]{:S(2)}) collective-permute-start(bf16[24,3584]{1,0:T(8,128)(2,1)S(1)} %collective-permute-done.6), channel_id=1, source_target_pairs={{0,4},{4,0},{8,12},{12,8},{16,20},{20,16},{24,28},{28,24},{1,5},{5... | collective-permute-start | bytes 516104 | tf_op jit(solution)/shard_map/ppermute | solution.py:51
  30.1 1.6 %collective-permute-start.11 = (bf16[24,3584]{1,0:T(8,128)(2,1)S(1)}, bf16[24,3584]{1,0:T(8,128)(2,1)S(1)}, u32[]{:S(2)}, u32[]{:S(2)}) collective-permute-start(bf16[24,3584]{1,0:T(8,128)(2,1)S(1)} %collective-permute-done.7), channel_id=1, source_target_pairs={{0,4},{4,0},{8,12},{12,8},{16,20},{20,16},{24,28},{28,24},{1,5},{5... | collective-permute-start | bytes 516104 | tf_op jit(solution)/shard_map/ppermute | solution.py:51
  34.8 2.2 %collective-permute-start.12 = (bf16[96,3584]{1,0:T(8,128)(2,1)S(1)}, bf16[96,3584]{1,0:T(8,128)(2,1)S(1)}, u32[]{:S(2)}, u32[]{:S(2)}) collective-permute-start(bf16[96,3584]{1,0:T(8,128)(2,1)S(1)} %get-tuple-element.44), channel_id=1, source_target_pairs={{0,4},{4,0},{8,12},{12,8},{16,20},{20,16},{24,28},{28,24},{1,5},{5... | collective-permute-start | bytes 2064392 | tf_op jit(solution)/shard_map/ppermute | solution.py:51
  37.2 9.8 %collective-permute-start.13 = (bf16[24,3584]{1,0:T(8,128)(2,1)S(1)}, bf16[24,3584]{1,0:T(8,128)(2,1)S(1)}, u32[]{:S(2)}, u32[]{:S(2)}) collective-permute-start(bf16[24,3584]{1,0:T(8,128)(2,1)S(1)} %get-tuple-element.51), channel_id=1, source_target_pairs={{0,16},{4,12},{8,24},{12,4},{16,0},{20,28},{24,8},{28,20},{1,17},{... | collective-permute-start | bytes 516104 | tf_op jit(solution)/shard_map/ppermute | solution.py:46
  38.1 8.8 %collective-permute-start.14 = (bf16[24,3584]{1,0:T(8,128)(2,1)S(1)}, bf16[24,3584]{1,0:T(8,128)(2,1)S(1)}, u32[]{:S(2)}, u32[]{:S(2)}) collective-permute-start(bf16[24,3584]{1,0:T(8,128)(2,1)S(1)} %get-tuple-element.50), channel_id=1, source_target_pairs={{0,24},{4,28},{8,16},{12,20},{16,8},{20,12},{24,0},{28,4},{1,25},{... | collective-permute-start | bytes 516104 | tf_op jit(solution)/shard_map/ppermute | solution.py:46
  39.6 8.0 %collective-permute-start.15 = (bf16[24,3584]{1,0:T(8,128)(2,1)S(1)}, bf16[24,3584]{1,0:T(8,128)(2,1)S(1)}, u32[]{:S(2)}, u32[]{:S(2)}) collective-permute-start(bf16[24,3584]{1,0:T(8,128)(2,1)S(1)} %get-tuple-element.49), channel_id=1, source_target_pairs={{0,8},{4,20},{8,0},{12,28},{16,24},{20,4},{24,16},{28,12},{1,9},{5... | collective-permute-start | bytes 516104 | tf_op jit(solution)/shard_map/ppermute | solution.py:46
  48.0 6.2 %collective-permute-start.16 = (bf16[8,3584]{1,0:T(8,128)(2,1)S(1)}, bf16[8,3584]{1,0:T(8,128)(2,1)S(1)}, u32[]{:S(2)}, u32[]{:S(2)}) collective-permute-start(bf16[8,3584]{1,0:T(8,128)(2,1)S(1)} %get-tuple-element.46), channel_id=1, source_target_pairs={{0,3},{1,2},{2,1},{3,0},{4,6},{5,7},{6,4},{7,5},{8,11},{9,10},{10,... | collective-permute-start | bytes 172040 | tf_op jit(solution)/shard_map/ppermute | solution.py:61
  50.6 5.9 %collective-permute-start.17 = (bf16[8,3584]{1,0:T(8,128)(2,1)S(1)}, bf16[8,3584]{1,0:T(8,128)(2,1)S(1)}, u32[]{:S(2)}, u32[]{:S(2)}) collective-permute-start(bf16[8,3584]{1,0:T(8,128)(2,1)S(1)} %get-tuple-element.47), channel_id=1, source_target_pairs={{0,2},{1,3},{2,0},{3,1},{4,7},{5,6},{6,5},{7,4},{8,10},{9,11},{10,... | collective-permute-start | bytes 172040 | tf_op jit(solution)/shard_map/ppermute | solution.py:61
  50.6 5.9 %collective-permute-start.18 = (bf16[8,3584]{1,0:T(8,128)(2,1)S(1)}, bf16[8,3584]{1,0:T(8,128)(2,1)S(1)}, u32[]{:S(2)}, u32[]{:S(2)}) collective-permute-start(bf16[8,3584]{1,0:T(8,128)(2,1)S(1)} %get-tuple-element.48), channel_id=1, source_target_pairs={{0,1},{1,0},{2,3},{3,2},{4,5},{5,4},{6,7},{7,6},{8,9},{9,8},{10,11... | collective-permute-start | bytes 172040 | tf_op jit(solution)/shard_map/ppermute | solution.py:61
  (4 other events, 10.0 us)

commit v5 on v4

--- a/solution.py
+++ b/solution.py
@@ -11,6 +11,7 @@
 EXP_DEV = 4
 CAP = 24
 PLANE_ORDERS = ((2, 3, 1), (1, 3, 2))
+RETURN_ORDER = (0, 3, 2, 1)
 
 
 neg_big = -1e30
@@ -270,9 +271,8 @@
     )(columns.reshape(EXP_DEV * CAP, -1), *parts)
 
 
-def expert_kernel(rows_ref, inner_ref, outer_ref, own_ref, others_ref):
+def expert_kernel(rows_ref, inner_ref, outer_ref, *out_refs):
     rows = rows_ref[...]
-    own = own_ref.shape[0]
     tile = min(2 * HEAD_DIM, inner_ref.shape[1])
     parts = []
     for c in range(0, inner_ref.shape[1], tile):
@@ -280,21 +280,22 @@
         parts.append((hidden / (1.0 + jnp.exp(-hidden))).astype(rows.dtype))
     activated = jnp.concatenate(parts, axis=1)
     tile = 2 * HEAD_DIM
-    for c in range(0, own_ref.shape[1], tile):
+    for c in range(0, outer_ref.shape[1], tile):
         out = jnp.dot(activated, outer_ref[:, c : c + tile], preferred_element_type=jnp.float32)
-        own_ref[:, c : c + tile] = out[:own]
-        others_ref[:, c : c + tile] = out[own:].astype(others_ref.dtype)
-
-
-def expert(rows, inner, outer, own):
+        for k, out_ref in enumerate(out_refs):
+            out_ref[:, c : c + tile] = out[k * CAP : (k + 1) * CAP].astype(out_ref.dtype)
+
+
+def expert(rows, inner, outer):
+    width = outer.shape[1]
+    others = rows.shape[0] // CAP - EXP_DEV
+    out_shape = (jax.ShapeDtypeStruct((CAP, width), jnp.float32),) * EXP_DEV
+    out_shape += (jax.ShapeDtypeStruct((CAP, width), rows.dtype),) * others
     return pl.pallas_call(
         expert_kernel,
-        out_shape=(
-            jax.ShapeDtypeStruct((own, outer.shape[1]), jnp.float32),
-            jax.ShapeDtypeStruct((rows.shape[0] - own, outer.shape[1]), rows.dtype),
-        ),
+        out_shape=out_shape,
         in_specs=[pl.BlockSpec(memory_space=pltpu.VMEM)] * 3,
-        out_specs=(pl.BlockSpec(memory_space=pltpu.VMEM),) * 2,
+        out_specs=(pl.BlockSpec(memory_space=pltpu.VMEM),) * len(out_shape),
         compiler_params=pltpu.CompilerParams(vmem_limit_bytes=32 * 1024 * 1024),
         cost_estimate=pl.CostEstimate(
             flops=2 * rows.shape[0] * (inner.size + outer.size),
@@ -308,7 +309,7 @@
 def combine_kernel(gate_ref, residual_ref, *refs):
     block_refs, out_refs = refs[:EXP_DEV], refs[EXP_DEV:]
     rows = jnp.concatenate([ref[...].astype(jnp.float32) for ref in block_refs], axis=0).astype(jnp.bfloat16)
-    gates = jnp.concatenate([gate_ref[k] for k in range(EXP_DEV)], axis=0)
+    gates = jnp.concatenate([gate_ref[k] for k in RETURN_ORDER], axis=0)
     high = gates.astype(jnp.bfloat16)
     low = (gates - high.astype(jnp.float32)).astype(jnp.bfloat16)
     mix = lax.dot_general(
@@ -335,7 +336,7 @@
             flops=4 * gate_columns.size * residual.shape[1], bytes_accessed=4 * 1024 * 1024, transcendentals=0
         ),
         name="combine",
-    )(gate_columns, residual, *blocks)
+    )(gate_columns, residual, *[blocks[k] for k in RETURN_ORDER])
 
 
 def body(
@@ -395,21 +396,20 @@
         pieces + [swap_group(piece, step, group_size) for step in group_steps for piece in pieces], axis=0
     )
 
-    share = EXP_DEV * CAP
-    summed, others = expert(inbound, w_in[0, 0], w_out[0, 0], share)
-    arrived = [
-        swap_group(others[k * share : (k + 1) * share], step, group_size) for k, step in enumerate(group_steps)
-    ]
-    for part in arrived:
-        summed = summed + part.astype(jnp.float32)
-    summed = summed.astype(jnp.bfloat16)
-
-    returned = [summed[:CAP]] + [
-        swap_plane(summed[(k + 1) * CAP : (k + 2) * CAP], k, plane_orders, group_size) for k in range(EXP_DEV - 1)
+    slots = expert(inbound, w_in[0, 0], w_out[0, 0])
+    summed = []
+    for j in range(EXP_DEV):
+        total = slots[j]
+        for k, step in enumerate(group_steps):
+            total = total + swap_group(slots[(k + 1) * EXP_DEV + j], step, group_size).astype(jnp.float32)
+        summed.append(total.astype(jnp.bfloat16))
+
+    returned = [summed[0]] + [
+        swap_plane(summed[k + 1], k, plane_orders, group_size) for k in range(EXP_DEV - 1)
     ]
     result, *blocks = combine(gate_columns, residual, returned, exp_count - 1)
-    for k, block in enumerate(blocks):
-        result = result + swap_exp(block, k, exp_orders, group_size).astype(jnp.float32)
+    for k in [0] + list(range(exp_count - 2, 0, -1)):
+        result = result + swap_exp(blocks[k], k, exp_orders, group_size).astype(jnp.float32)
     return result.astype(jnp.bfloat16)
 
 

time: 57.3 us -> 55.8 us (0.974)
  waiting for transfers between devices: 23.3 us -> 20.9 us
  starting transfers between devices: 22.4 us -> 23.3 us
    ppermute x6, waiting for transfers between devices: 7.4 us -> 5.9 us  [swap_exp(): return lax.ppermute(block, ('req', 'exp'), pairs)]
    ppermute x5 -> x8, starting transfers between devices: 1.59 us -> 2.32 us  [swap_group(): return lax.ppermute(block, 'req', pairs)]
    ppermute x5 -> x8, waiting for transfers between devices: 1.96 us -> 1.27 us  [swap_group(): return lax.ppermute(block, 'req', pairs)]
  transfers between devices with their start and end apart: 19 -> 22, of which waited for: 13 -> 14; matrix products, arithmetic and copies ran while one was open for 4% -> 4% of each run, Pallas kernels for 3% -> 3%
where the time goes in v5:
time: 55.8 us; the launch traced here: 55.6 us
  starting transfers between devices  23.3 us (42%)
  waiting for transfers between devices  20.9 us (37%)
  Pallas kernels  6.9 us (12%)
  local copies, waits for them, and re-layouts  2.88 us (5%)
  other arithmetic  1.34 us (2%)
    ppermute x6, waiting for transfers between devices, swap_plane(): return lax.ppermute(block, 'req', pairs)  12.6 us
    ppermute x6, starting transfers between devices, swap_exp(): return lax.ppermute(block, ('req', 'exp'), pairs)  10.2 us
    ppermute x6, starting transfers between devices, swap_plane(): return lax.ppermute(block, 'req', pairs)  7.3 us
    ppermute x6, waiting for transfers between devices, swap_exp(): return lax.ppermute(block, ('req', 'exp'), pairs)  5.9 us
    ppermute x2, starting transfers between devices, swap_ring(): return lax.ppermute(block, 'req', pairs)  3.4 us
    pallas_call x1, Pallas kernels, expert(): pl.pallas_call(expert_kernel, out_shape=out_shape, in_specs=[pl.BlockSpec...  3.06 us
    ppermute x8, starting transfers between devices, swap_group(): return lax.ppermute(block, 'req', pairs)  2.32 us
    pallas_call x1, Pallas kernels, local_attention(): pl.pallas_call(local_attention_kernel, out_shape=(part, part, part, part,...  1.92 us
  transfers between devices with their start and end apart: 22, of which 14 were waited for; matrix products, arithmetic and copies ran while one was open for 4% of the time, Pallas kernels for 3%

profile of v5, /device:TPU:0, one launch (start us, length us, event | category | flops | bytes accessed | tf_op | source)
XLA Modules:
  0.0 55.6 jit_solution(13881694076183457496)
XLA Ops:
  0.0 1.2 %copy-done = bf16[1,1,32,16,1024]{4,3,2,1,0:T(8,128)(2,1)S(1)} copy-done((bf16[1,1,32,16,1024]{4,3,2,1,0:T(8,128)(2,1)S(1)}, bf16[1,1,32,16,1024]{4,3,2,1,0:T(8,128)(2,1)}, u32[]{:S(2)}) %copy-start) | copy-done | bytes 1048600
  1.3 0.6 %send_pages.1 = (bf16[4,16,1024]{2,1,0:T(8,128)(2,1)S(1)}, bf16[4,16,1024]{2,1,0:T(8,128)(2,1)S(1)}) custom-call(s32[2,4]{1,0:T(2,128)S(1)} %bitcast.36, bf16[32,16,1024]{2,1,0:T(8,128)(2,1)S(1)} %bitcast.31, f32[8,128]{1,0:T(8,128)S(1)} %opening.1.after_ref), custom_call_target="tpu_custom_call" | custom-call | flops 4294967296 | bytes 1048576 | tf_op jit(solution)/shard_map/send_pages/pallas_call | solution.py:89
  1.9 3.4 %collective-permute-start = (bf16[64,1024]{1,0:T(8,128)(2,1)S(1)}, bf16[64,1024]{1,0:T(8,128)(2,1)S(1)}, u32[]{:S(2)}, u32[]{:S(2)}) collective-permute-start(bf16[64,1024]{1,0:T(8,128)(2,1)S(1)} %bitcast.35), channel_id=1, source_target_pairs={{4,8},{8,4},{12,16},{16,12},{20,24},{24,20},{28,0},{0,28},{5,9},{9... | collective-permute-start | bytes 393224 | tf_op jit(solution)/shard_map/ppermute | solution.py:38
  5.5 1.9 %local_attention.1 = (f32[4,56,128]{2,1,0:T(8,128)S(1)}, f32[4,56,128]{2,1,0:T(8,128)S(1)}, f32[4,56,128]{2,1,0:T(8,128)S(1)}, f32[4,56,128]{2,1,0:T(8,128)S(1)}, f32[56,128]{1,0:T(8,128)S(1)}) custom-call(s32[4,8]{1,0:T(4,128)S(1)} %copy-done.3, s32[4]{0:T(128)S(1)} %copy-done.5, s32[2,4]{1,0:T(2,128)S(1)} %bitcast.33, bf16[8,3584]{1,0:T(8,128)(2,1)S(1)} %copy-done.1, ...), custom_call_target="tpu_custom_call" | custom-call | flops 41943040 | bytes 2097152 | tf_op jit(solution)/shard_map/local_attention/pallas_call | solution.py:183
  7.4 1.1 %collective-permute-done.far_ref = bf16[64,1024]{1,0:T(8,128)(2,1)S(1)} collective-permute-done((bf16[64,1024]{1,0:T(8,128)(2,1)S(1)}, bf16[64,1024]{1,0:T(8,128)(2,1)S(1)}, u32[]{:S(2)}, u32[]{:S(2)}) %collective-permute-start) | collective-permute-done | bytes 131104 | tf_op jit(solution)/shard_map/ppermute | solution.py:38
  8.6 0.7 %arrived_attention.1 = (f32[8,3584]{1,0:T(8,128)S(1)}, bf16[8,3584]{1,0:T(8,128)(2,1)S(1)}) custom-call(bf16[8,3584]{1,0:T(8,128)(2,1)S(1)} %copy-done.6, bf16[3584]{0:T(1024)(128)(2,1)S(1)} %copy-done.7, bf16[64,1024]{1,0:T(8,128)(2,1)S(1)} %collective-permute-done.far_ref, bf16[64,1024]{1,0:T(8,128)(2,1)S(1)} %collective-permute-done.1.near_ref, ...), custom_call_target="tpu_custom_call" | custom-call | flops 1073741824 | bytes 2097152 | tf_op jit(solution)/shard_map/arrived_attention/pallas_call | solution.py:240
  9.2 5.1 %collective-permute-start.2 = (bf16[8,3584]{1,0:T(8,128)(2,1)S(1)}, bf16[8,3584]{1,0:T(8,128)(2,1)S(1)}, u32[]{:S(2)}, u32[]{:S(2)}) collective-permute-start(bf16[8,3584]{1,0:T(8,128)(2,1)S(1)} %get-tuple-element.44.refs_0_), channel_id=1, source_target_pairs={{0,3},{1,2},{2,1},{3,0},{4,6},{5,7},{6,4},{7,5},{8,11},{9,10},{10,... | collective-permute-start | bytes 172040 | tf_op jit(solution)/shard_map/ppermute | solution.py:62
  14.4 0.6 %collective-permute-start.4 = (bf16[8,3584]{1,0:T(8,128)(2,1)S(1)}, bf16[8,3584]{1,0:T(8,128)(2,1)S(1)}, u32[]{:S(2)}, u32[]{:S(2)}) collective-permute-start(bf16[8,3584]{1,0:T(8,128)(2,1)S(1)} %get-tuple-element.44.refs_0_), channel_id=1, source_target_pairs={{0,1},{1,0},{2,3},{3,2},{4,5},{5,4},{6,7},{7,6},{8,9},{9,8},{10,11... | collective-permute-start | bytes 172040 | tf_op jit(solution)/shard_map/ppermute | solution.py:62
  15.1 0.5 gather_fusion
  16.1 0.6 gather_fusion.1
  17.2 2.2 %collective-permute-done.3.refs_2_ = bf16[8,3584]{1,0:T(8,128)(2,1)S(1)} collective-permute-done((bf16[8,3584]{1,0:T(8,128)(2,1)S(1)}, bf16[8,3584]{1,0:T(8,128)(2,1)S(1)}, u32[]{:S(2)}, u32[]{:S(2)}) %collective-permute-start.3) | collective-permute-done | bytes 57376 | tf_op jit(solution)/shard_map/ppermute | solution.py:62
  19.8 1.0 %collective-permute-start.5 = (bf16[24,3584]{1,0:T(8,128)(2,1)S(1)}, bf16[24,3584]{1,0:T(8,128)(2,1)S(1)}, u32[]{:S(2)}, u32[]{:S(2)}) collective-permute-start(bf16[24,3584]{1,0:T(8,128)(2,1)S(1)} %get-tuple-element.46), channel_id=1, source_target_pairs={{0,16},{4,12},{8,24},{12,4},{16,0},{20,28},{24,8},{28,20},{1,17},{... | collective-permute-start | bytes 516104 | tf_op jit(solution)/shard_map/ppermute | solution.py:47
  20.8 1.2 %collective-permute-start.6 = (bf16[24,3584]{1,0:T(8,128)(2,1)S(1)}, bf16[24,3584]{1,0:T(8,128)(2,1)S(1)}, u32[]{:S(2)}, u32[]{:S(2)}) collective-permute-start(bf16[24,3584]{1,0:T(8,128)(2,1)S(1)} %get-tuple-element.47), channel_id=1, source_target_pairs={{0,24},{4,28},{8,16},{12,20},{16,8},{20,12},{24,0},{28,4},{1,25},{... | collective-permute-start | bytes 516104 | tf_op jit(solution)/shard_map/ppermute | solution.py:47
  22.1 1.4 %collective-permute-start.7 = (bf16[24,3584]{1,0:T(8,128)(2,1)S(1)}, bf16[24,3584]{1,0:T(8,128)(2,1)S(1)}, u32[]{:S(2)}, u32[]{:S(2)}) collective-permute-start(bf16[24,3584]{1,0:T(8,128)(2,1)S(1)} %get-tuple-element.48), channel_id=1, source_target_pairs={{0,8},{4,20},{8,0},{12,28},{16,24},{20,4},{24,16},{28,12},{1,9},{5... | collective-permute-start | bytes 516104 | tf_op jit(solution)/shard_map/ppermute | solution.py:47
  23.5 5.8 %collective-permute-done.5 = bf16[24,3584]{1,0:T(8,128)(2,1)S(1)} collective-permute-done((bf16[24,3584]{1,0:T(8,128)(2,1)S(1)}, bf16[24,3584]{1,0:T(8,128)(2,1)S(1)}, u32[]{:S(2)}, u32[]{:S(2)}) %collective-permute-start.5) | collective-permute-done | bytes 172064 | tf_op jit(solution)/shard_map/ppermute | solution.py:47
  29.3 0.6 %collective-permute-start.10 = (bf16[24,3584]{1,0:T(8,128)(2,1)S(1)}, bf16[24,3584]{1,0:T(8,128)(2,1)S(1)}, u32[]{:S(2)}, u32[]{:S(2)}) collective-permute-start(bf16[24,3584]{1,0:T(8,128)(2,1)S(1)} %collective-permute-done.6), channel_id=1, source_target_pairs={{0,4},{4,0},{8,12},{12,8},{16,20},{20,16},{24,28},{28,24},{1,5},{5... | collective-permute-start | bytes 516104 | tf_op jit(solution)/shard_map/ppermute | solution.py:52
  30.1 0.5 collective-permute-start.11
  31.0 0.7 %collective-permute-done.11 = bf16[24,3584]{1,0:T(8,128)(2,1)S(1)} collective-permute-done((bf16[24,3584]{1,0:T(8,128)(2,1)S(1)}, bf16[24,3584]{1,0:T(8,128)(2,1)S(1)}, u32[]{:S(2)}, u32[]{:S(2)}) %collective-permute-start.11) | collective-permute-done | bytes 172064 | tf_op jit(solution)/shard_map/ppermute | solution.py:52
  31.7 3.1 %expert.1 = (f32[24,3584]{1,0:T(8,128)S(1)}, f32[24,3584]{1,0:T(8,128)S(1)}, f32[24,3584]{1,0:T(8,128)S(1)}, f32[24,3584]{1,0:T(8,128)S(1)}, bf16[24,3584]{1,0:T...) custom-call(bf16[192,3584]{1,0:T(8,128)(2,1)S(1)} %constant_dynamic-updat, ...), custom_call_target="tpu_custom_call" | custom-call | flops 2818572288 | bytes 14680064 | tf_op jit(solution)/shard_map/expert/pallas_call | solution.py:294
  34.8 0.4 collective-permute-start.17
  36.3 1.0 %collective-permute-start.18 = (bf16[24,3584]{1,0:T(8,128)(2,1)S(1)}, bf16[24,3584]{1,0:T(8,128)(2,1)S(1)}, u32[]{:S(2)}, u32[]{:S(2)}) collective-permute-start(bf16[24,3584]{1,0:T(8,128)(2,1)S(1)} %add_convert_fusion), channel_id=1, source_target_pairs={{0,16},{4,12},{8,24},{12,4},{16,0},{20,28},{24,8},{28,20},{1,17},{... | collective-permute-start | bytes 516104 | tf_op jit(solution)/shard_map/ppermute | solution.py:47
  37.3 1.6 %collective-permute-start.16 = (bf16[24,3584]{1,0:T(8,128)(2,1)S(1)}, bf16[24,3584]{1,0:T(8,128)(2,1)S(1)}, u32[]{:S(2)}, u32[]{:S(2)}) collective-permute-start(bf16[24,3584]{1,0:T(8,128)(2,1)S(1)} %add_convert_fusion.1), channel_id=1, source_target_pairs={{0,24},{4,28},{8,16},{12,20},{16,8},{20,12},{24,0},{28,4},{1,25},{... | collective-permute-start | bytes 516104 | tf_op jit(solution)/shard_map/ppermute | solution.py:47
  38.9 1.1 %collective-permute-start.14 = (bf16[24,3584]{1,0:T(8,128)(2,1)S(1)}, bf16[24,3584]{1,0:T(8,128)(2,1)S(1)}, u32[]{:S(2)}, u32[]{:S(2)}) collective-permute-start(bf16[24,3584]{1,0:T(8,128)(2,1)S(1)} %add_convert_fusion.2), channel_id=1, source_target_pairs={{0,8},{4,20},{8,0},{12,28},{16,24},{20,4},{24,16},{28,12},{1,9},{5... | collective-permute-start | bytes 516104 | tf_op jit(solution)/shard_map/ppermute | solution.py:47
  40.1 5.7 %collective-permute-done.18.refs_3_ = bf16[24,3584]{1,0:T(8,128)(2,1)S(1)} collective-permute-done((bf16[24,3584]{1,0:T(8,128)(2,1)S(1)}, bf16[24,3584]{1,0:T(8,128)(2,1)S(1)}, u32[]{:S(2)}, u32[]{:S(2)}) %collective-permute-start.18) | collective-permute-done | bytes 172064 | tf_op jit(solution)/shard_map/ppermute | solution.py:47
  45.8 0.9 %collective-permute-done.14.refs_1_ = bf16[24,3584]{1,0:T(8,128)(2,1)S(1)} collective-permute-done((bf16[24,3584]{1,0:T(8,128)(2,1)S(1)}, bf16[24,3584]{1,0:T(8,128)(2,1)S(1)}, u32[]{:S(2)}, u32[]{:S(2)}) %collective-permute-start.14) | collective-permute-done | bytes 172064 | tf_op jit(solution)/shard_map/ppermute | solution.py:47
  46.7 0.4 combine.1
  47.1 2.8 %collective-permute-start.19 = (bf16[8,3584]{1,0:T(8,128)(2,1)S(1)}, bf16[8,3584]{1,0:T(8,128)(2,1)S(1)}, u32[]{:S(2)}, u32[]{:S(2)}) collective-permute-start(bf16[8,3584]{1,0:T(8,128)(2,1)S(1)} %get-tuple-element.58), channel_id=1, source_target_pairs={{0,3},{1,2},{2,1},{3,0},{4,6},{5,7},{6,4},{7,5},{8,11},{9,10},{10,... | collective-permute-start | bytes 172040 | tf_op jit(solution)/shard_map/ppermute | solution.py:62
  49.9 1.7 %collective-permute-start.21 = (bf16[8,3584]{1,0:T(8,128)(2,1)S(1)}, bf16[8,3584]{1,0:T(8,128)(2,1)S(1)}, u32[]{:S(2)}, u32[]{:S(2)}) collective-permute-start(bf16[8,3584]{1,0:T(8,128)(2,1)S(1)} %get-tuple-element.60), channel_id=1, source_target_pairs={{0,2},{1,3},{2,0},{3,1},{4,7},{5,6},{6,5},{7,4},{8,10},{9,11},{10,... | collective-permute-start | bytes 172040 | tf_op jit(solution)/shard_map/ppermute | solution.py:62
  51.6 1.9 %collective-permute-done.19 = bf16[8,3584]{1,0:T(8,128)(2,1)S(1)} collective-permute-done((bf16[8,3584]{1,0:T(8,128)(2,1)S(1)}, bf16[8,3584]{1,0:T(8,128)(2,1)S(1)}, u32[]{:S(2)}, u32[]{:S(2)}) %collective-permute-start.19) | collective-permute-done | bytes 57376 | tf_op jit(solution)/shard_map/ppermute | solution.py:62
  53.5 0.6 %collective-permute-done.20 = bf16[8,3584]{1,0:T(8,128)(2,1)S(1)} collective-permute-done((bf16[8,3584]{1,0:T(8,128)(2,1)S(1)}, bf16[8,3584]{1,0:T(8,128)(2,1)S(1)}, u32[]{:S(2)}, u32[]{:S(2)}) %collective-permute-start.20) | collective-permute-done | bytes 57376 | tf_op jit(solution)/shard_map/ppermute | solution.py:62
  54.1 0.8 %collective-permute-done.21 = bf16[8,3584]{1,0:T(8,128)(2,1)S(1)} collective-permute-done((bf16[8,3584]{1,0:T(8,128)(2,1)S(1)}, bf16[8,3584]{1,0:T(8,128)(2,1)S(1)}, u32[]{:S(2)}, u32[]{:S(2)}) %collective-permute-start.21) | collective-permute-done | bytes 57376 | tf_op jit(solution)/shard_map/ppermute | solution.py:62
  55.0 0.7 %add_convert_fusion.4 = bf16[8,3584]{1,0:T(8,128)(2,1)} fusion(bf16[8,3584]{1,0:T(8,128)(2,1)S(1)} %collective-permute-done.21, bf16[8,3584]{1,0:T(8,128)(2,1)S(1)} %collective-permute-done.20, f32[8,3584]{1,0:T(8,128)S(1)} %get-tuple-element.57, bf16[8,3584]{1,0:T(8,128)(2,1)S(1)} %collective-permute-done.19), kind=kLoop, calls=%fused_computation.6 | loop fusion | flops 200704 | bytes 344064 | tf_op jit(solution)/shard_map/convert_element_type | solution.py:413
  (86 shorter events, 3.4 us)
Async XLA Ops:
  1.2 4.2 %copy-start.1 = (bf16[8,3584]{1,0:T(8,128)(2,1)S(1)}, bf16[8,3584]{1,0:T(8,128)(2,1)}, u32[]{:S(2)}) copy-start(bf16[8,3584]{1,0:T(8,128)(2,1)} %queries_ref.1) | copy-start | bytes 172036
  1.2 4.2 %copy-start.2 = (bf16[8,1024]{1,0:T(8,128)(2,1)S(1)}, bf16[8,1024]{1,0:T(8,128)(2,1)}, u32[]{:S(2)}) copy-start(bf16[8,1024]{1,0:T(8,128)(2,1)} %fresh_ref.1) | copy-start | bytes 49156
  1.3 7.2 %copy-start.6 = (bf16[8,3584]{1,0:T(8,128)(2,1)S(1)}, bf16[8,3584]{1,0:T(8,128)(2,1)}, u32[]{:S(2)}) copy-start(bf16[8,3584]{1,0:T(8,128)(2,1)} %resid_ref.1) | copy-start | bytes 172036
  1.3 7.2 %copy-start.7 = (bf16[3584]{0:T(1024)(128)(2,1)S(1)}, bf16[3584]{0:T(1024)(128)(2,1)}, u32[]{:S(2)}) copy-start(bf16[3584]{0:T(1024)(128)(2,1)} %gain_ref.1) | copy-start | bytes 21508
  1.9 6.6 %collective-permute-start = (bf16[64,1024]{1,0:T(8,128)(2,1)S(1)}, bf16[64,1024]{1,0:T(8,128)(2,1)S(1)}, u32[]{:S(2)}, u32[]{:S(2)}) collective-permute-start(bf16[64,1024]{1,0:T(8,128)(2,1)S(1)} %bitcast.35), channel_id=1, source_target_pairs={{4,8},{8,4},{12,16},{16,12},{20,24},{24,20},{28,0},{0,28},{5,9},{9... | collective-permute-start | bytes 393224 | tf_op jit(solution)/shard_map/ppermute | solution.py:38
  5.3 3.2 %collective-permute-start.1 = (bf16[64,1024]{1,0:T(8,128)(2,1)S(1)}, bf16[64,1024]{1,0:T(8,128)(2,1)S(1)}, u32[]{:S(2)}, u32[]{:S(2)}) collective-permute-start(bf16[64,1024]{1,0:T(8,128)(2,1)S(1)} %bitcast.34), channel_id=1, source_target_pairs={{0,4},{4,0},{8,12},{12,8},{16,20},{20,16},{24,28},{28,24},{1,5},{5... | collective-permute-start | bytes 393224 | tf_op jit(solution)/shard_map/ppermute | solution.py:38
  8.5 6.5 %copy-start.9 = (s32[32,8]{0,1:T(8,128)S(1)}, s32[32,8]{0,1:T(8,128)}, u32[]{:S(2)}) copy-start(s32[32,8]{0,1:T(8,128)} %param.23) | copy-start | bytes 3076
  8.5 7.5 %copy-start.10 = (f32[32,8]{0,1:T(8,128)S(1)}, f32[32,8]{0,1:T(8,128)}, u32[]{:S(2)}) copy-start(f32[32,8]{0,1:T(8,128)} %param.24) | copy-start | bytes 3076
  9.2 8.0 %collective-permute-start.2 = (bf16[8,3584]{1,0:T(8,128)(2,1)S(1)}, bf16[8,3584]{1,0:T(8,128)(2,1)S(1)}, u32[]{:S(2)}, u32[]{:S(2)}) collective-permute-start(bf16[8,3584]{1,0:T(8,128)(2,1)S(1)} %get-tuple-element.44.refs_0_), channel_id=1, source_target_pairs={{0,3},{1,2},{2,1},{3,0},{4,6},{5,7},{6,4},{7,5},{8,11},{9,10},{10,... | collective-permute-start | bytes 172040 | tf_op jit(solution)/shard_map/ppermute | solution.py:62
  14.4 5.1 %collective-permute-start.3 = (bf16[8,3584]{1,0:T(8,128)(2,1)S(1)}, bf16[8,3584]{1,0:T(8,128)(2,1)S(1)}, u32[]{:S(2)}, u32[]{:S(2)}) collective-permute-start(bf16[8,3584]{1,0:T(8,128)(2,1)S(1)} %get-tuple-element.44.refs_0_), channel_id=1, source_target_pairs={{0,2},{1,3},{2,0},{3,1},{4,7},{5,6},{6,5},{7,4},{8,10},{9,11},{10,... | collective-permute-start | bytes 172040 | tf_op jit(solution)/shard_map/ppermute | solution.py:62
  14.4 5.1 %collective-permute-start.4 = (bf16[8,3584]{1,0:T(8,128)(2,1)S(1)}, bf16[8,3584]{1,0:T(8,128)(2,1)S(1)}, u32[]{:S(2)}, u32[]{:S(2)}) collective-permute-start(bf16[8,3584]{1,0:T(8,128)(2,1)S(1)} %get-tuple-element.44.refs_0_), channel_id=1, source_target_pairs={{0,1},{1,0},{2,3},{3,2},{4,5},{5,4},{6,7},{7,6},{8,9},{9,8},{10,11... | collective-permute-start | bytes 172040 | tf_op jit(solution)/shard_map/ppermute | solution.py:62
  16.8 14.8 %slice-start = ((s8[7340032]{0:T(1024)(128)(4,1)}), s8[4194304]{0:T(1024)(128)(4,1)S(1)}, s32[]{:S(2)}) async-start(s8[7340032]{0:T(1024)(128)(4,1)} %bitcast.25), calls=%async_computation | async-start | bytes 8388608
  16.8 14.8 %slice-start.2 = ((s8[7340032]{0:T(1024)(128)(4,1)}), s8[4194304]{0:T(1024)(128)(4,1)S(1)}, s32[]{:S(2)}) async-start(s8[7340032]{0:T(1024)(128)(4,1)} %bitcast.28), calls=%async_computation.2 | async-start | bytes 8388608
  16.9 14.7 %slice-start.1 = ((s8[7340032]{0:T(1024)(128)(4,1)}), s8[3145728]{0:T(1024)(128)(4,1)S(1)}, s32[]{:S(2)}) async-start(s8[7340032]{0:T(1024)(128)(4,1)} %bitcast.25), calls=%async_computation.1 | async-start | bytes 6291456
  17.0 14.7 %slice-start.3 = ((s8[7340032]{0:T(1024)(128)(4,1)}), s8[3145728]{0:T(1024)(128)(4,1)S(1)}, s32[]{:S(2)}) async-start(s8[7340032]{0:T(1024)(128)(4,1)} %bitcast.28), calls=%async_computation.3 | async-start | bytes 6291456
  19.8 9.5 %collective-permute-start.5 = (bf16[24,3584]{1,0:T(8,128)(2,1)S(1)}, bf16[24,3584]{1,0:T(8,128)(2,1)S(1)}, u32[]{:S(2)}, u32[]{:S(2)}) collective-permute-start(bf16[24,3584]{1,0:T(8,128)(2,1)S(1)} %get-tuple-element.46), channel_id=1, source_target_pairs={{0,16},{4,12},{8,24},{12,4},{16,0},{20,28},{24,8},{28,20},{1,17},{... | collective-permute-start | bytes 516104 | tf_op jit(solution)/shard_map/ppermute | solution.py:47
  20.8 9.8 %collective-permute-start.8 = (bf16[24,3584]{1,0:T(8,128)(2,1)S(1)}, bf16[24,3584]{1,0:T(8,128)(2,1)S(1)}, u32[]{:S(2)}, u32[]{:S(2)}) collective-permute-start(bf16[24,3584]{1,0:T(8,128)(2,1)S(1)} %get-tuple-element.45), channel_id=1, source_target_pairs={{0,4},{4,0},{8,12},{12,8},{16,20},{20,16},{24,28},{28,24},{1,5},{5... | collective-permute-start | bytes 516104 | tf_op jit(solution)/shard_map/ppermute | solution.py:52
  20.8 8.5 %collective-permute-start.6 = (bf16[24,3584]{1,0:T(8,128)(2,1)S(1)}, bf16[24,3584]{1,0:T(8,128)(2,1)S(1)}, u32[]{:S(2)}, u32[]{:S(2)}) collective-permute-start(bf16[24,3584]{1,0:T(8,128)(2,1)S(1)} %get-tuple-element.47), channel_id=1, source_target_pairs={{0,24},{4,28},{8,16},{12,20},{16,8},{20,12},{24,0},{28,4},{1,25},{... | collective-permute-start | bytes 516104 | tf_op jit(solution)/shard_map/ppermute | solution.py:47
  22.1 8.0 %collective-permute-start.7 = (bf16[24,3584]{1,0:T(8,128)(2,1)S(1)}, bf16[24,3584]{1,0:T(8,128)(2,1)S(1)}, u32[]{:S(2)}, u32[]{:S(2)}) collective-permute-start(bf16[24,3584]{1,0:T(8,128)(2,1)S(1)} %get-tuple-element.48), channel_id=1, source_target_pairs={{0,8},{4,20},{8,0},{12,28},{16,24},{20,4},{24,16},{28,12},{1,9},{5... | collective-permute-start | bytes 516104 | tf_op jit(solution)/shard_map/ppermute | solution.py:47
  29.3 1.4 %collective-permute-start.9 = (bf16[24,3584]{1,0:T(8,128)(2,1)S(1)}, bf16[24,3584]{1,0:T(8,128)(2,1)S(1)}, u32[]{:S(2)}, u32[]{:S(2)}) collective-permute-start(bf16[24,3584]{1,0:T(8,128)(2,1)S(1)} %collective-permute-done.5), channel_id=1, source_target_pairs={{0,4},{4,0},{8,12},{12,8},{16,20},{20,16},{24,28},{28,24},{1,5},{5... | collective-permute-start | bytes 516104 | tf_op jit(solution)/shard_map/ppermute | solution.py:52
  29.3 1.6 %collective-permute-start.10 = (bf16[24,3584]{1,0:T(8,128)(2,1)S(1)}, bf16[24,3584]{1,0:T(8,128)(2,1)S(1)}, u32[]{:S(2)}, u32[]{:S(2)}) collective-permute-start(bf16[24,3584]{1,0:T(8,128)(2,1)S(1)} %collective-permute-done.6), channel_id=1, source_target_pairs={{0,4},{4,0},{8,12},{12,8},{16,20},{20,16},{24,28},{28,24},{1,5},{5... | collective-permute-start | bytes 516104 | tf_op jit(solution)/shard_map/ppermute | solution.py:52
  30.1 1.6 %collective-permute-start.11 = (bf16[24,3584]{1,0:T(8,128)(2,1)S(1)}, bf16[24,3584]{1,0:T(8,128)(2,1)S(1)}, u32[]{:S(2)}, u32[]{:S(2)}) collective-permute-start(bf16[24,3584]{1,0:T(8,128)(2,1)S(1)} %collective-permute-done.7), channel_id=1, source_target_pairs={{0,4},{4,0},{8,12},{12,8},{16,20},{20,16},{24,28},{28,24},{1,5},{5... | collective-permute-start | bytes 516104 | tf_op jit(solution)/shard_map/ppermute | solution.py:52
  34.8 1.5 %collective-permute-start.17 = (bf16[24,3584]{1,0:T(8,128)(2,1)S(1)}, bf16[24,3584]{1,0:T(8,128)(2,1)S(1)}, u32[]{:S(2)}, u32[]{:S(2)}) collective-permute-start(bf16[24,3584]{1,0:T(8,128)(2,1)S(1)} %get-tuple-element.56), channel_id=1, source_target_pairs={{0,4},{4,0},{8,12},{12,8},{16,20},{20,16},{24,28},{28,24},{1,5},{5... | collective-permute-start | bytes 516104 | tf_op jit(solution)/shard_map/ppermute | solution.py:52
  35.2 2.0 %collective-permute-start.15 = (bf16[24,3584]{1,0:T(8,128)(2,1)S(1)}, bf16[24,3584]{1,0:T(8,128)(2,1)S(1)}, u32[]{:S(2)}, u32[]{:S(2)}) collective-permute-start(bf16[24,3584]{1,0:T(8,128)(2,1)S(1)} %get-tuple-element.54), channel_id=1, source_target_pairs={{0,4},{4,0},{8,12},{12,8},{16,20},{20,16},{24,28},{28,24},{1,5},{5... | collective-permute-start | bytes 516104 | tf_op jit(solution)/shard_map/ppermute | solution.py:52
  35.4 3.5 %collective-permute-start.13 = (bf16[24,3584]{1,0:T(8,128)(2,1)S(1)}, bf16[24,3584]{1,0:T(8,128)(2,1)S(1)}, u32[]{:S(2)}, u32[]{:S(2)}) collective-permute-start(bf16[24,3584]{1,0:T(8,128)(2,1)S(1)} %get-tuple-element.52), channel_id=1, source_target_pairs={{0,4},{4,0},{8,12},{12,8},{16,20},{20,16},{24,28},{28,24},{1,5},{5... | collective-permute-start | bytes 516104 | tf_op jit(solution)/shard_map/ppermute | solution.py:52
  35.8 4.3 %collective-permute-start.12 = (bf16[24,3584]{1,0:T(8,128)(2,1)S(1)}, bf16[24,3584]{1,0:T(8,128)(2,1)S(1)}, u32[]{:S(2)}, u32[]{:S(2)}) collective-permute-start(bf16[24,3584]{1,0:T(8,128)(2,1)S(1)} %get-tuple-element.50), channel_id=1, source_target_pairs={{0,4},{4,0},{8,12},{12,8},{16,20},{20,16},{24,28},{28,24},{1,5},{5... | collective-permute-start | bytes 516104 | tf_op jit(solution)/shard_map/ppermute | solution.py:52
  36.3 9.5 %collective-permute-start.18 = (bf16[24,3584]{1,0:T(8,128)(2,1)S(1)}, bf16[24,3584]{1,0:T(8,128)(2,1)S(1)}, u32[]{:S(2)}, u32[]{:S(2)}) collective-permute-start(bf16[24,3584]{1,0:T(8,128)(2,1)S(1)} %add_convert_fusion), channel_id=1, source_target_pairs={{0,16},{4,12},{8,24},{12,4},{16,0},{20,28},{24,8},{28,20},{1,17},{... | collective-permute-start | bytes 516104 | tf_op jit(solution)/shard_map/ppermute | solution.py:47
  37.3 8.5 %collective-permute-start.16 = (bf16[24,3584]{1,0:T(8,128)(2,1)S(1)}, bf16[24,3584]{1,0:T(8,128)(2,1)S(1)}, u32[]{:S(2)}, u32[]{:S(2)}) collective-permute-start(bf16[24,3584]{1,0:T(8,128)(2,1)S(1)} %add_convert_fusion.1), channel_id=1, source_target_pairs={{0,24},{4,28},{8,16},{12,20},{16,8},{20,12},{24,0},{28,4},{1,25},{... | collective-permute-start | bytes 516104 | tf_op jit(solution)/shard_map/ppermute | solution.py:47
  38.9 7.8 %collective-permute-start.14 = (bf16[24,3584]{1,0:T(8,128)(2,1)S(1)}, bf16[24,3584]{1,0:T(8,128)(2,1)S(1)}, u32[]{:S(2)}, u32[]{:S(2)}) collective-permute-start(bf16[24,3584]{1,0:T(8,128)(2,1)S(1)} %add_convert_fusion.2), channel_id=1, source_target_pairs={{0,8},{4,20},{8,0},{12,28},{16,24},{20,4},{24,16},{28,12},{1,9},{5... | collective-permute-start | bytes 516104 | tf_op jit(solution)/shard_map/ppermute | solution.py:47
  47.1 6.4 %collective-permute-start.19 = (bf16[8,3584]{1,0:T(8,128)(2,1)S(1)}, bf16[8,3584]{1,0:T(8,128)(2,1)S(1)}, u32[]{:S(2)}, u32[]{:S(2)}) collective-permute-start(bf16[8,3584]{1,0:T(8,128)(2,1)S(1)} %get-tuple-element.58), channel_id=1, source_target_pairs={{0,3},{1,2},{2,1},{3,0},{4,6},{5,7},{6,4},{7,5},{8,11},{9,10},{10,... | collective-permute-start | bytes 172040 | tf_op jit(solution)/shard_map/ppermute | solution.py:62
  49.9 4.2 %collective-permute-start.20 = (bf16[8,3584]{1,0:T(8,128)(2,1)S(1)}, bf16[8,3584]{1,0:T(8,128)(2,1)S(1)}, u32[]{:S(2)}, u32[]{:S(2)}) collective-permute-start(bf16[8,3584]{1,0:T(8,128)(2,1)S(1)} %get-tuple-element.59), channel_id=1, source_target_pairs={{0,1},{1,0},{2,3},{3,2},{4,5},{5,4},{6,7},{7,6},{8,9},{9,8},{10,11... | collective-permute-start | bytes 172040 | tf_op jit(solution)/shard_map/ppermute | solution.py:62
  49.9 5.1 %collective-permute-start.21 = (bf16[8,3584]{1,0:T(8,128)(2,1)S(1)}, bf16[8,3584]{1,0:T(8,128)(2,1)S(1)}, u32[]{:S(2)}, u32[]{:S(2)}) collective-permute-start(bf16[8,3584]{1,0:T(8,128)(2,1)S(1)} %get-tuple-element.60), channel_id=1, source_target_pairs={{0,2},{1,3},{2,0},{3,1},{4,7},{5,6},{6,5},{7,4},{8,10},{9,11},{10,... | collective-permute-start | bytes 172040 | tf_op jit(solution)/shard_map/ppermute | solution.py:62
  (7 other events, 23.2 us)

commit v6 on v5

--- a/solution.py
+++ b/solution.py
@@ -1,3 +1,5 @@
+import functools
+
 import jax
 import jax.numpy as jnp
 from jax import lax
@@ -77,20 +79,20 @@
     )()
 
 
-def send_pages_kernel(source_ref, pool_ref, after_ref, far_ref, near_ref):
+def send_pages_kernel(source_ref, pool_ref, after_ref, out_ref, *, far):
     odd = lax.rem(lax.axis_index("req"), 2)
-    for side, out_ref in ((1 - odd, far_ref), (odd, near_ref)):
-        for i in range(out_ref.shape[0]):
-            out_ref[i] = pool_ref[source_ref[side, i]]
-
-
-def send_pages(pool_pages, sources, after):
+    side = 1 - odd if far else odd
+    for i in range(out_ref.shape[0]):
+        out_ref[i] = pool_ref[source_ref[side, i]]
+
+
+def send_pages(pool_pages, sources, after, far):
     pages = jax.ShapeDtypeStruct((sources.shape[1],) + pool_pages.shape[1:], pool_pages.dtype)
     return pl.pallas_call(
-        send_pages_kernel,
-        out_shape=(pages, pages),
+        functools.partial(send_pages_kernel, far=far),
+        out_shape=pages,
         in_specs=[pl.BlockSpec(memory_space=pltpu.SMEM)] + [pl.BlockSpec(memory_space=pltpu.VMEM)] * 2,
-        out_specs=(pl.BlockSpec(memory_space=pltpu.VMEM),) * 2,
+        out_specs=pl.BlockSpec(memory_space=pltpu.VMEM),
         compiler_params=pltpu.CompilerParams(vmem_limit_bytes=4 * 1024 * 1024),
         cost_estimate=pl.CostEstimate(
             flops=4 * 1024 * 1024 * 1024, bytes_accessed=pool_pages.size * pool_pages.dtype.itemsize, transcendentals=0
@@ -366,7 +368,8 @@
 
     pool_pages = kv_pool[0, 0]
     targets = mig_target[0, 0]
-    far, near = send_pages(pool_pages, mig_source[0, 0], opening())
+    first = opening()
+    far, near = (send_pages(pool_pages, mig_source[0, 0], first, far) for far in (True, False))
     moved_shape = (far.shape[0] * far.shape[1], far.shape[2])
     far = swap_ring(far.reshape(moved_shape), 1)
     near = swap_ring(near.reshape(moved_shape), 0)

time: 55.8 us -> 55.8 us (level)
  waiting for transfers between devices: 20.9 us -> 20.2 us
  Pallas kernels: 6.9 us -> 7.47 us
    ppermute x2, waiting for transfers between devices: 1.12 us -> 0.41 us  [swap_ring(): return lax.ppermute(block, 'req', pairs)]
    pallas_call x1 -> x2, Pallas kernels: 0.59 us -> 1.15 us  [send_pages(): pl.pallas_call(functools.partial(send_pages_kernel, far=far), out_shape=p...]
  transfers between devices with their start and end apart: 22 -> 22, of which waited for: 14 -> 14; matrix products, arithmetic and copies ran while one was open for 4% -> 4% of each run, Pallas kernels for 3% -> 4%
where the time goes in v6:
time: 55.8 us; the launch traced here: 55.6 us
  starting transfers between devices  23.3 us (42%)
  waiting for transfers between devices  20.2 us (36%)
  Pallas kernels  7.47 us (13%)
  local copies, waits for them, and re-layouts  2.89 us (5%)
  other arithmetic  1.34 us (2%)
    ppermute x6, waiting for transfers between devices, swap_plane(): return lax.ppermute(block, 'req', pairs)  12.6 us
    ppermute x6, starting transfers between devices, swap_exp(): return lax.ppermute(block, ('req', 'exp'), pairs)  10.2 us
    ppermute x6, starting transfers between devices, swap_plane(): return lax.ppermute(block, 'req', pairs)  7.3 us
    ppermute x6, waiting for transfers between devices, swap_exp(): return lax.ppermute(block, ('req', 'exp'), pairs)  5.89 us
    ppermute x2, starting transfers between devices, swap_ring(): return lax.ppermute(block, 'req', pairs)  3.47 us
    pallas_call x1, Pallas kernels, expert(): pl.pallas_call(expert_kernel, out_shape=out_shape, in_specs=[pl.BlockSpec...  3.07 us
    ppermute x8, starting transfers between devices, swap_group(): return lax.ppermute(block, 'req', pairs)  2.31 us
    pallas_call x1, Pallas kernels, local_attention(): pl.pallas_call(local_attention_kernel, out_shape=(part, part, part, part,...  1.92 us
  transfers between devices with their start and end apart: 22, of which 14 were waited for; matrix products, arithmetic and copies ran while one was open for 4% of the time, Pallas kernels for 4%

profile of v6, /device:TPU:0, one launch (start us, length us, event | category | flops | bytes accessed | tf_op | source)
XLA Modules:
  0.0 55.6 jit_solution(8307160838241364385)
XLA Ops:
  0.0 1.2 %copy-done = bf16[1,1,32,16,1024]{4,3,2,1,0:T(8,128)(2,1)S(1)} copy-done((bf16[1,1,32,16,1024]{4,3,2,1,0:T(8,128)(2,1)S(1)}, bf16[1,1,32,16,1024]{4,3,2,1,0:T(8,128)(2,1)}, u32[]{:S(2)}) %copy-start) | copy-done | bytes 1048600
  1.2 0.6 %send_pages.2 = bf16[4,16,1024]{2,1,0:T(8,128)(2,1)S(1)} custom-call(s32[2,4]{1,0:T(2,128)S(1)} %bitcast.37, bf16[32,16,1024]{2,1,0:T(8,128)(2,1)S(1)} %bitcast.31, f32[8,128]{1,0:T(8,128)S(1)} %opening.1.after_ref), custom_call_target="tpu_custom_call" | custom-call | flops 4294967296 | bytes 1048576 | tf_op jit(solution)/shard_map/send_pages/pallas_call | solution.py:91
  1.9 3.4 %collective-permute-start = (bf16[64,1024]{1,0:T(8,128)(2,1)S(1)}, bf16[64,1024]{1,0:T(8,128)(2,1)S(1)}, u32[]{:S(2)}, u32[]{:S(2)}) collective-permute-start(bf16[64,1024]{1,0:T(8,128)(2,1)S(1)} %bitcast.35), channel_id=1, source_target_pairs={{4,8},{8,4},{12,16},{16,12},{20,24},{24,20},{28,0},{0,28},{5,9},{9... | collective-permute-start | bytes 393224 | tf_op jit(solution)/shard_map/ppermute | solution.py:40
  5.3 0.6 %send_pages.3 = bf16[4,16,1024]{2,1,0:T(8,128)(2,1)S(1)} custom-call(s32[2,4]{1,0:T(2,128)S(1)} %bitcast.38, bf16[32,16,1024]{2,1,0:T(8,128)(2,1)S(1)} %bitcast.32, f32[8,128]{1,0:T(8,128)S(1)} %opening.1.after_ref), custom_call_target="tpu_custom_call" | custom-call | flops 4294967296 | bytes 1048576 | tf_op jit(solution)/shard_map/send_pages/pallas_call | solution.py:91
  6.2 1.9 %local_attention.1 = (f32[4,56,128]{2,1,0:T(8,128)S(1)}, f32[4,56,128]{2,1,0:T(8,128)S(1)}, f32[4,56,128]{2,1,0:T(8,128)S(1)}, f32[4,56,128]{2,1,0:T(8,128)S(1)}, f32[56,128]{1,0:T(8,128)S(1)}) custom-call(s32[4,8]{1,0:T(4,128)S(1)} %copy-done.3, s32[4]{0:T(128)S(1)} %copy-done.5, s32[2,4]{1,0:T(2,128)S(1)} %bitcast.34, bf16[8,3584]{1,0:T(8,128)(2,1)S(1)} %copy-done.1, ...), custom_call_target="tpu_custom_call" | custom-call | flops 41943040 | bytes 2097152 | tf_op jit(solution)/shard_map/local_attention/pallas_call | solution.py:185
  8.1 0.4 collective-permute-done.far_ref
  8.6 0.7 %arrived_attention.1 = (f32[8,3584]{1,0:T(8,128)S(1)}, bf16[8,3584]{1,0:T(8,128)(2,1)S(1)}) custom-call(bf16[8,3584]{1,0:T(8,128)(2,1)S(1)} %copy-done.6, bf16[3584]{0:T(1024)(128)(2,1)S(1)} %copy-done.7, bf16[64,1024]{1,0:T(8,128)(2,1)S(1)} %collective-permute-done.far_ref, bf16[64,1024]{1,0:T(8,128)(2,1)S(1)} %collective-permute-done.1.near_ref, ...), custom_call_target="tpu_custom_call" | custom-call | flops 1073741824 | bytes 2097152 | tf_op jit(solution)/shard_map/arrived_attention/pallas_call | solution.py:242
  9.2 5.1 %collective-permute-start.2 = (bf16[8,3584]{1,0:T(8,128)(2,1)S(1)}, bf16[8,3584]{1,0:T(8,128)(2,1)S(1)}, u32[]{:S(2)}, u32[]{:S(2)}) collective-permute-start(bf16[8,3584]{1,0:T(8,128)(2,1)S(1)} %get-tuple-element.40.refs_0_), channel_id=1, source_target_pairs={{0,3},{1,2},{2,1},{3,0},{4,6},{5,7},{6,4},{7,5},{8,11},{9,10},{10,... | collective-permute-start | bytes 172040 | tf_op jit(solution)/shard_map/ppermute | solution.py:64
  14.4 0.6 %collective-permute-start.4 = (bf16[8,3584]{1,0:T(8,128)(2,1)S(1)}, bf16[8,3584]{1,0:T(8,128)(2,1)S(1)}, u32[]{:S(2)}, u32[]{:S(2)}) collective-permute-start(bf16[8,3584]{1,0:T(8,128)(2,1)S(1)} %get-tuple-element.40.refs_0_), channel_id=1, source_target_pairs={{0,1},{1,0},{2,3},{3,2},{4,5},{5,4},{6,7},{7,6},{8,9},{9,8},{10,11... | collective-permute-start | bytes 172040 | tf_op jit(solution)/shard_map/ppermute | solution.py:64
  15.1 0.5 gather_fusion
  16.1 0.6 gather_fusion.1
  17.1 2.3 %collective-permute-done.3.refs_2_ = bf16[8,3584]{1,0:T(8,128)(2,1)S(1)} collective-permute-done((bf16[8,3584]{1,0:T(8,128)(2,1)S(1)}, bf16[8,3584]{1,0:T(8,128)(2,1)S(1)}, u32[]{:S(2)}, u32[]{:S(2)}) %collective-permute-start.3) | collective-permute-done | bytes 57376 | tf_op jit(solution)/shard_map/ppermute | solution.py:64
  19.8 1.0 %collective-permute-start.5 = (bf16[24,3584]{1,0:T(8,128)(2,1)S(1)}, bf16[24,3584]{1,0:T(8,128)(2,1)S(1)}, u32[]{:S(2)}, u32[]{:S(2)}) collective-permute-start(bf16[24,3584]{1,0:T(8,128)(2,1)S(1)} %get-tuple-element.42), channel_id=1, source_target_pairs={{0,16},{4,12},{8,24},{12,4},{16,0},{20,28},{24,8},{28,20},{1,17},{... | collective-permute-start | bytes 516104 | tf_op jit(solution)/shard_map/ppermute | solution.py:49
  20.9 1.2 %collective-permute-start.6 = (bf16[24,3584]{1,0:T(8,128)(2,1)S(1)}, bf16[24,3584]{1,0:T(8,128)(2,1)S(1)}, u32[]{:S(2)}, u32[]{:S(2)}) collective-permute-start(bf16[24,3584]{1,0:T(8,128)(2,1)S(1)} %get-tuple-element.43), channel_id=1, source_target_pairs={{0,24},{4,28},{8,16},{12,20},{16,8},{20,12},{24,0},{28,4},{1,25},{... | collective-permute-start | bytes 516104 | tf_op jit(solution)/shard_map/ppermute | solution.py:49
  22.1 1.4 %collective-permute-start.7 = (bf16[24,3584]{1,0:T(8,128)(2,1)S(1)}, bf16[24,3584]{1,0:T(8,128)(2,1)S(1)}, u32[]{:S(2)}, u32[]{:S(2)}) collective-permute-start(bf16[24,3584]{1,0:T(8,128)(2,1)S(1)} %get-tuple-element.44), channel_id=1, source_target_pairs={{0,8},{4,20},{8,0},{12,28},{16,24},{20,4},{24,16},{28,12},{1,9},{5... | collective-permute-start | bytes 516104 | tf_op jit(solution)/shard_map/ppermute | solution.py:49
  23.5 5.8 %collective-permute-done.5 = bf16[24,3584]{1,0:T(8,128)(2,1)S(1)} collective-permute-done((bf16[24,3584]{1,0:T(8,128)(2,1)S(1)}, bf16[24,3584]{1,0:T(8,128)(2,1)S(1)}, u32[]{:S(2)}, u32[]{:S(2)}) %collective-permute-start.5) | collective-permute-done | bytes 172064 | tf_op jit(solution)/shard_map/ppermute | solution.py:49
  29.3 0.6 %collective-permute-start.10 = (bf16[24,3584]{1,0:T(8,128)(2,1)S(1)}, bf16[24,3584]{1,0:T(8,128)(2,1)S(1)}, u32[]{:S(2)}, u32[]{:S(2)}) collective-permute-start(bf16[24,3584]{1,0:T(8,128)(2,1)S(1)} %collective-permute-done.6), channel_id=1, source_target_pairs={{0,4},{4,0},{8,12},{12,8},{16,20},{20,16},{24,28},{28,24},{1,5},{5... | collective-permute-start | bytes 516104 | tf_op jit(solution)/shard_map/ppermute | solution.py:54
  30.1 0.5 collective-permute-start.11
  31.0 0.7 %collective-permute-done.11 = bf16[24,3584]{1,0:T(8,128)(2,1)S(1)} collective-permute-done((bf16[24,3584]{1,0:T(8,128)(2,1)S(1)}, bf16[24,3584]{1,0:T(8,128)(2,1)S(1)}, u32[]{:S(2)}, u32[]{:S(2)}) %collective-permute-start.11) | collective-permute-done | bytes 172064 | tf_op jit(solution)/shard_map/ppermute | solution.py:54
  31.7 3.1 %expert.1 = (f32[24,3584]{1,0:T(8,128)S(1)}, f32[24,3584]{1,0:T(8,128)S(1)}, f32[24,3584]{1,0:T(8,128)S(1)}, f32[24,3584]{1,0:T(8,128)S(1)}, bf16[24,3584]{1,0:T...) custom-call(bf16[192,3584]{1,0:T(8,128)(2,1)S(1)} %constant_dynamic-updat, ...), custom_call_target="tpu_custom_call" | custom-call | flops 2818572288 | bytes 14680064 | tf_op jit(solution)/shard_map/expert/pallas_call | solution.py:296
  34.8 0.4 collective-permute-start.17
  36.3 1.0 %collective-permute-start.18 = (bf16[24,3584]{1,0:T(8,128)(2,1)S(1)}, bf16[24,3584]{1,0:T(8,128)(2,1)S(1)}, u32[]{:S(2)}, u32[]{:S(2)}) collective-permute-start(bf16[24,3584]{1,0:T(8,128)(2,1)S(1)} %add_convert_fusion), channel_id=1, source_target_pairs={{0,16},{4,12},{8,24},{12,4},{16,0},{20,28},{24,8},{28,20},{1,17},{... | collective-permute-start | bytes 516104 | tf_op jit(solution)/shard_map/ppermute | solution.py:49
  37.3 1.6 %collective-permute-start.16 = (bf16[24,3584]{1,0:T(8,128)(2,1)S(1)}, bf16[24,3584]{1,0:T(8,128)(2,1)S(1)}, u32[]{:S(2)}, u32[]{:S(2)}) collective-permute-start(bf16[24,3584]{1,0:T(8,128)(2,1)S(1)} %add_convert_fusion.1), channel_id=1, source_target_pairs={{0,24},{4,28},{8,16},{12,20},{16,8},{20,12},{24,0},{28,4},{1,25},{... | collective-permute-start | bytes 516104 | tf_op jit(solution)/shard_map/ppermute | solution.py:49
  38.9 1.2 %collective-permute-start.14 = (bf16[24,3584]{1,0:T(8,128)(2,1)S(1)}, bf16[24,3584]{1,0:T(8,128)(2,1)S(1)}, u32[]{:S(2)}, u32[]{:S(2)}) collective-permute-start(bf16[24,3584]{1,0:T(8,128)(2,1)S(1)} %add_convert_fusion.2), channel_id=1, source_target_pairs={{0,8},{4,20},{8,0},{12,28},{16,24},{20,4},{24,16},{28,12},{1,9},{5... | collective-permute-start | bytes 516104 | tf_op jit(solution)/shard_map/ppermute | solution.py:49
  40.1 5.7 %collective-permute-done.18.refs_3_ = bf16[24,3584]{1,0:T(8,128)(2,1)S(1)} collective-permute-done((bf16[24,3584]{1,0:T(8,128)(2,1)S(1)}, bf16[24,3584]{1,0:T(8,128)(2,1)S(1)}, u32[]{:S(2)}, u32[]{:S(2)}) %collective-permute-start.18) | collective-permute-done | bytes 172064 | tf_op jit(solution)/shard_map/ppermute | solution.py:49
  45.9 0.9 %collective-permute-done.14.refs_1_ = bf16[24,3584]{1,0:T(8,128)(2,1)S(1)} collective-permute-done((bf16[24,3584]{1,0:T(8,128)(2,1)S(1)}, bf16[24,3584]{1,0:T(8,128)(2,1)S(1)}, u32[]{:S(2)}, u32[]{:S(2)}) %collective-permute-start.14) | collective-permute-done | bytes 172064 | tf_op jit(solution)/shard_map/ppermute | solution.py:49
  47.1 2.8 %collective-permute-start.19 = (bf16[8,3584]{1,0:T(8,128)(2,1)S(1)}, bf16[8,3584]{1,0:T(8,128)(2,1)S(1)}, u32[]{:S(2)}, u32[]{:S(2)}) collective-permute-start(bf16[8,3584]{1,0:T(8,128)(2,1)S(1)} %get-tuple-element.54), channel_id=1, source_target_pairs={{0,3},{1,2},{2,1},{3,0},{4,6},{5,7},{6,4},{7,5},{8,11},{9,10},{10,... | collective-permute-start | bytes 172040 | tf_op jit(solution)/shard_map/ppermute | solution.py:64
  49.9 1.7 %collective-permute-start.21 = (bf16[8,3584]{1,0:T(8,128)(2,1)S(1)}, bf16[8,3584]{1,0:T(8,128)(2,1)S(1)}, u32[]{:S(2)}, u32[]{:S(2)}) collective-permute-start(bf16[8,3584]{1,0:T(8,128)(2,1)S(1)} %get-tuple-element.56), channel_id=1, source_target_pairs={{0,2},{1,3},{2,0},{3,1},{4,7},{5,6},{6,5},{7,4},{8,10},{9,11},{10,... | collective-permute-start | bytes 172040 | tf_op jit(solution)/shard_map/ppermute | solution.py:64
  51.6 1.9 %collective-permute-done.19 = bf16[8,3584]{1,0:T(8,128)(2,1)S(1)} collective-permute-done((bf16[8,3584]{1,0:T(8,128)(2,1)S(1)}, bf16[8,3584]{1,0:T(8,128)(2,1)S(1)}, u32[]{:S(2)}, u32[]{:S(2)}) %collective-permute-start.19) | collective-permute-done | bytes 57376 | tf_op jit(solution)/shard_map/ppermute | solution.py:64
  53.5 0.6 %collective-permute-done.20 = bf16[8,3584]{1,0:T(8,128)(2,1)S(1)} collective-permute-done((bf16[8,3584]{1,0:T(8,128)(2,1)S(1)}, bf16[8,3584]{1,0:T(8,128)(2,1)S(1)}, u32[]{:S(2)}, u32[]{:S(2)}) %collective-permute-start.20) | collective-permute-done | bytes 57376 | tf_op jit(solution)/shard_map/ppermute | solution.py:64
  54.1 0.8 %collective-permute-done.21 = bf16[8,3584]{1,0:T(8,128)(2,1)S(1)} collective-permute-done((bf16[8,3584]{1,0:T(8,128)(2,1)S(1)}, bf16[8,3584]{1,0:T(8,128)(2,1)S(1)}, u32[]{:S(2)}, u32[]{:S(2)}) %collective-permute-start.21) | collective-permute-done | bytes 57376 | tf_op jit(solution)/shard_map/ppermute | solution.py:64
  55.0 0.7 %add_convert_fusion.4 = bf16[8,3584]{1,0:T(8,128)(2,1)} fusion(bf16[8,3584]{1,0:T(8,128)(2,1)S(1)} %collective-permute-done.21, bf16[8,3584]{1,0:T(8,128)(2,1)S(1)} %collective-permute-done.20, f32[8,3584]{1,0:T(8,128)S(1)} %get-tuple-element.53, bf16[8,3584]{1,0:T(8,128)(2,1)S(1)} %collective-permute-done.19), kind=kLoop, calls=%fused_computation.6 | loop fusion | flops 200704 | bytes 344064 | tf_op jit(solution)/shard_map/convert_element_type | solution.py:416
  (87 shorter events, 3.7 us)
Async XLA Ops:
  1.8 4.3 %copy-start.1 = (bf16[8,3584]{1,0:T(8,128)(2,1)S(1)}, bf16[8,3584]{1,0:T(8,128)(2,1)}, u32[]{:S(2)}) copy-start(bf16[8,3584]{1,0:T(8,128)(2,1)} %queries_ref.1) | copy-start | bytes 172036
  1.8 4.3 %copy-start.2 = (bf16[8,1024]{1,0:T(8,128)(2,1)S(1)}, bf16[8,1024]{1,0:T(8,128)(2,1)}, u32[]{:S(2)}) copy-start(bf16[8,1024]{1,0:T(8,128)(2,1)} %fresh_ref.1) | copy-start | bytes 49156
  1.9 6.7 %copy-start.6 = (bf16[8,3584]{1,0:T(8,128)(2,1)S(1)}, bf16[8,3584]{1,0:T(8,128)(2,1)}, u32[]{:S(2)}) copy-start(bf16[8,3584]{1,0:T(8,128)(2,1)} %resid_ref.1) | copy-start | bytes 172036
  1.9 6.6 %copy-start.7 = (bf16[3584]{0:T(1024)(128)(2,1)S(1)}, bf16[3584]{0:T(1024)(128)(2,1)}, u32[]{:S(2)}) copy-start(bf16[3584]{0:T(1024)(128)(2,1)} %gain_ref.1) | copy-start | bytes 21508
  1.9 6.6 %collective-permute-start = (bf16[64,1024]{1,0:T(8,128)(2,1)S(1)}, bf16[64,1024]{1,0:T(8,128)(2,1)S(1)}, u32[]{:S(2)}, u32[]{:S(2)}) collective-permute-start(bf16[64,1024]{1,0:T(8,128)(2,1)S(1)} %bitcast.35), channel_id=1, source_target_pairs={{4,8},{8,4},{12,16},{16,12},{20,24},{24,20},{28,0},{0,28},{5,9},{9... | collective-permute-start | bytes 393224 | tf_op jit(solution)/shard_map/ppermute | solution.py:40
  5.9 2.6 %collective-permute-start.1 = (bf16[64,1024]{1,0:T(8,128)(2,1)S(1)}, bf16[64,1024]{1,0:T(8,128)(2,1)S(1)}, u32[]{:S(2)}, u32[]{:S(2)}) collective-permute-start(bf16[64,1024]{1,0:T(8,128)(2,1)S(1)} %bitcast.36), channel_id=1, source_target_pairs={{0,4},{4,0},{8,12},{12,8},{16,20},{20,16},{24,28},{28,24},{1,5},{5... | collective-permute-start | bytes 393224 | tf_op jit(solution)/shard_map/ppermute | solution.py:40
  8.6 6.5 %copy-start.9 = (s32[32,8]{0,1:T(8,128)S(1)}, s32[32,8]{0,1:T(8,128)}, u32[]{:S(2)}) copy-start(s32[32,8]{0,1:T(8,128)} %param.23) | copy-start | bytes 3076
  8.6 7.5 %copy-start.10 = (f32[32,8]{0,1:T(8,128)S(1)}, f32[32,8]{0,1:T(8,128)}, u32[]{:S(2)}) copy-start(f32[32,8]{0,1:T(8,128)} %param.24) | copy-start | bytes 3076
  9.2 7.9 %collective-permute-start.2 = (bf16[8,3584]{1,0:T(8,128)(2,1)S(1)}, bf16[8,3584]{1,0:T(8,128)(2,1)S(1)}, u32[]{:S(2)}, u32[]{:S(2)}) collective-permute-start(bf16[8,3584]{1,0:T(8,128)(2,1)S(1)} %get-tuple-element.40.refs_0_), channel_id=1, source_target_pairs={{0,3},{1,2},{2,1},{3,0},{4,6},{5,7},{6,4},{7,5},{8,11},{9,10},{10,... | collective-permute-start | bytes 172040 | tf_op jit(solution)/shard_map/ppermute | solution.py:64
  14.4 5.1 %collective-permute-start.3 = (bf16[8,3584]{1,0:T(8,128)(2,1)S(1)}, bf16[8,3584]{1,0:T(8,128)(2,1)S(1)}, u32[]{:S(2)}, u32[]{:S(2)}) collective-permute-start(bf16[8,3584]{1,0:T(8,128)(2,1)S(1)} %get-tuple-element.40.refs_0_), channel_id=1, source_target_pairs={{0,2},{1,3},{2,0},{3,1},{4,7},{5,6},{6,5},{7,4},{8,10},{9,11},{10,... | collective-permute-start | bytes 172040 | tf_op jit(solution)/shard_map/ppermute | solution.py:64
  14.4 5.1 %collective-permute-start.4 = (bf16[8,3584]{1,0:T(8,128)(2,1)S(1)}, bf16[8,3584]{1,0:T(8,128)(2,1)S(1)}, u32[]{:S(2)}, u32[]{:S(2)}) collective-permute-start(bf16[8,3584]{1,0:T(8,128)(2,1)S(1)} %get-tuple-element.40.refs_0_), channel_id=1, source_target_pairs={{0,1},{1,0},{2,3},{3,2},{4,5},{5,4},{6,7},{7,6},{8,9},{9,8},{10,11... | collective-permute-start | bytes 172040 | tf_op jit(solution)/shard_map/ppermute | solution.py:64
  16.9 14.8 %slice-start = ((s8[7340032]{0:T(1024)(128)(4,1)}), s8[4194304]{0:T(1024)(128)(4,1)S(1)}, s32[]{:S(2)}) async-start(s8[7340032]{0:T(1024)(128)(4,1)} %bitcast.25), calls=%async_computation | async-start | bytes 8388608
  16.9 14.8 %slice-start.2 = ((s8[7340032]{0:T(1024)(128)(4,1)}), s8[4194304]{0:T(1024)(128)(4,1)S(1)}, s32[]{:S(2)}) async-start(s8[7340032]{0:T(1024)(128)(4,1)} %bitcast.28), calls=%async_computation.2 | async-start | bytes 8388608
  17.0 14.7 %slice-start.1 = ((s8[7340032]{0:T(1024)(128)(4,1)}), s8[3145728]{0:T(1024)(128)(4,1)S(1)}, s32[]{:S(2)}) async-start(s8[7340032]{0:T(1024)(128)(4,1)} %bitcast.25), calls=%async_computation.1 | async-start | bytes 6291456
  17.0 14.7 %slice-start.3 = ((s8[7340032]{0:T(1024)(128)(4,1)}), s8[3145728]{0:T(1024)(128)(4,1)S(1)}, s32[]{:S(2)}) async-start(s8[7340032]{0:T(1024)(128)(4,1)} %bitcast.28), calls=%async_computation.3 | async-start | bytes 6291456
  19.8 9.5 %collective-permute-start.5 = (bf16[24,3584]{1,0:T(8,128)(2,1)S(1)}, bf16[24,3584]{1,0:T(8,128)(2,1)S(1)}, u32[]{:S(2)}, u32[]{:S(2)}) collective-permute-start(bf16[24,3584]{1,0:T(8,128)(2,1)S(1)} %get-tuple-element.42), channel_id=1, source_target_pairs={{0,16},{4,12},{8,24},{12,4},{16,0},{20,28},{24,8},{28,20},{1,17},{... | collective-permute-start | bytes 516104 | tf_op jit(solution)/shard_map/ppermute | solution.py:49
  20.8 9.9 %collective-permute-start.8 = (bf16[24,3584]{1,0:T(8,128)(2,1)S(1)}, bf16[24,3584]{1,0:T(8,128)(2,1)S(1)}, u32[]{:S(2)}, u32[]{:S(2)}) collective-permute-start(bf16[24,3584]{1,0:T(8,128)(2,1)S(1)} %get-tuple-element.41), channel_id=1, source_target_pairs={{0,4},{4,0},{8,12},{12,8},{16,20},{20,16},{24,28},{28,24},{1,5},{5... | collective-permute-start | bytes 516104 | tf_op jit(solution)/shard_map/ppermute | solution.py:54
  20.9 8.5 %collective-permute-start.6 = (bf16[24,3584]{1,0:T(8,128)(2,1)S(1)}, bf16[24,3584]{1,0:T(8,128)(2,1)S(1)}, u32[]{:S(2)}, u32[]{:S(2)}) collective-permute-start(bf16[24,3584]{1,0:T(8,128)(2,1)S(1)} %get-tuple-element.43), channel_id=1, source_target_pairs={{0,24},{4,28},{8,16},{12,20},{16,8},{20,12},{24,0},{28,4},{1,25},{... | collective-permute-start | bytes 516104 | tf_op jit(solution)/shard_map/ppermute | solution.py:49
  22.1 8.0 %collective-permute-start.7 = (bf16[24,3584]{1,0:T(8,128)(2,1)S(1)}, bf16[24,3584]{1,0:T(8,128)(2,1)S(1)}, u32[]{:S(2)}, u32[]{:S(2)}) collective-permute-start(bf16[24,3584]{1,0:T(8,128)(2,1)S(1)} %get-tuple-element.44), channel_id=1, source_target_pairs={{0,8},{4,20},{8,0},{12,28},{16,24},{20,4},{24,16},{28,12},{1,9},{5... | collective-permute-start | bytes 516104 | tf_op jit(solution)/shard_map/ppermute | solution.py:49
  29.3 1.4 %collective-permute-start.9 = (bf16[24,3584]{1,0:T(8,128)(2,1)S(1)}, bf16[24,3584]{1,0:T(8,128)(2,1)S(1)}, u32[]{:S(2)}, u32[]{:S(2)}) collective-permute-start(bf16[24,3584]{1,0:T(8,128)(2,1)S(1)} %collective-permute-done.5), channel_id=1, source_target_pairs={{0,4},{4,0},{8,12},{12,8},{16,20},{20,16},{24,28},{28,24},{1,5},{5... | collective-permute-start | bytes 516104 | tf_op jit(solution)/shard_map/ppermute | solution.py:54
  29.3 1.6 %collective-permute-start.10 = (bf16[24,3584]{1,0:T(8,128)(2,1)S(1)}, bf16[24,3584]{1,0:T(8,128)(2,1)S(1)}, u32[]{:S(2)}, u32[]{:S(2)}) collective-permute-start(bf16[24,3584]{1,0:T(8,128)(2,1)S(1)} %collective-permute-done.6), channel_id=1, source_target_pairs={{0,4},{4,0},{8,12},{12,8},{16,20},{20,16},{24,28},{28,24},{1,5},{5... | collective-permute-start | bytes 516104 | tf_op jit(solution)/shard_map/ppermute | solution.py:54
  30.1 1.6 %collective-permute-start.11 = (bf16[24,3584]{1,0:T(8,128)(2,1)S(1)}, bf16[24,3584]{1,0:T(8,128)(2,1)S(1)}, u32[]{:S(2)}, u32[]{:S(2)}) collective-permute-start(bf16[24,3584]{1,0:T(8,128)(2,1)S(1)} %collective-permute-done.7), channel_id=1, source_target_pairs={{0,4},{4,0},{8,12},{12,8},{16,20},{20,16},{24,28},{28,24},{1,5},{5... | collective-permute-start | bytes 516104 | tf_op jit(solution)/shard_map/ppermute | solution.py:54
  34.8 1.5 %collective-permute-start.17 = (bf16[24,3584]{1,0:T(8,128)(2,1)S(1)}, bf16[24,3584]{1,0:T(8,128)(2,1)S(1)}, u32[]{:S(2)}, u32[]{:S(2)}) collective-permute-start(bf16[24,3584]{1,0:T(8,128)(2,1)S(1)} %get-tuple-element.52), channel_id=1, source_target_pairs={{0,4},{4,0},{8,12},{12,8},{16,20},{20,16},{24,28},{28,24},{1,5},{5... | collective-permute-start | bytes 516104 | tf_op jit(solution)/shard_map/ppermute | solution.py:54
  35.2 2.0 %collective-permute-start.15 = (bf16[24,3584]{1,0:T(8,128)(2,1)S(1)}, bf16[24,3584]{1,0:T(8,128)(2,1)S(1)}, u32[]{:S(2)}, u32[]{:S(2)}) collective-permute-start(bf16[24,3584]{1,0:T(8,128)(2,1)S(1)} %get-tuple-element.50), channel_id=1, source_target_pairs={{0,4},{4,0},{8,12},{12,8},{16,20},{20,16},{24,28},{28,24},{1,5},{5... | collective-permute-start | bytes 516104 | tf_op jit(solution)/shard_map/ppermute | solution.py:54
  35.5 3.4 %collective-permute-start.13 = (bf16[24,3584]{1,0:T(8,128)(2,1)S(1)}, bf16[24,3584]{1,0:T(8,128)(2,1)S(1)}, u32[]{:S(2)}, u32[]{:S(2)}) collective-permute-start(bf16[24,3584]{1,0:T(8,128)(2,1)S(1)} %get-tuple-element.48), channel_id=1, source_target_pairs={{0,4},{4,0},{8,12},{12,8},{16,20},{20,16},{24,28},{28,24},{1,5},{5... | collective-permute-start | bytes 516104 | tf_op jit(solution)/shard_map/ppermute | solution.py:54
  35.8 4.3 %collective-permute-start.12 = (bf16[24,3584]{1,0:T(8,128)(2,1)S(1)}, bf16[24,3584]{1,0:T(8,128)(2,1)S(1)}, u32[]{:S(2)}, u32[]{:S(2)}) collective-permute-start(bf16[24,3584]{1,0:T(8,128)(2,1)S(1)} %get-tuple-element.46), channel_id=1, source_target_pairs={{0,4},{4,0},{8,12},{12,8},{16,20},{20,16},{24,28},{28,24},{1,5},{5... | collective-permute-start | bytes 516104 | tf_op jit(solution)/shard_map/ppermute | solution.py:54
  36.3 9.5 %collective-permute-start.18 = (bf16[24,3584]{1,0:T(8,128)(2,1)S(1)}, bf16[24,3584]{1,0:T(8,128)(2,1)S(1)}, u32[]{:S(2)}, u32[]{:S(2)}) collective-permute-start(bf16[24,3584]{1,0:T(8,128)(2,1)S(1)} %add_convert_fusion), channel_id=1, source_target_pairs={{0,16},{4,12},{8,24},{12,4},{16,0},{20,28},{24,8},{28,20},{1,17},{... | collective-permute-start | bytes 516104 | tf_op jit(solution)/shard_map/ppermute | solution.py:49
  37.3 8.5 %collective-permute-start.16 = (bf16[24,3584]{1,0:T(8,128)(2,1)S(1)}, bf16[24,3584]{1,0:T(8,128)(2,1)S(1)}, u32[]{:S(2)}, u32[]{:S(2)}) collective-permute-start(bf16[24,3584]{1,0:T(8,128)(2,1)S(1)} %add_convert_fusion.1), channel_id=1, source_target_pairs={{0,24},{4,28},{8,16},{12,20},{16,8},{20,12},{24,0},{28,4},{1,25},{... | collective-permute-start | bytes 516104 | tf_op jit(solution)/shard_map/ppermute | solution.py:49
  38.9 7.8 %collective-permute-start.14 = (bf16[24,3584]{1,0:T(8,128)(2,1)S(1)}, bf16[24,3584]{1,0:T(8,128)(2,1)S(1)}, u32[]{:S(2)}, u32[]{:S(2)}) collective-permute-start(bf16[24,3584]{1,0:T(8,128)(2,1)S(1)} %add_convert_fusion.2), channel_id=1, source_target_pairs={{0,8},{4,20},{8,0},{12,28},{16,24},{20,4},{24,16},{28,12},{1,9},{5... | collective-permute-start | bytes 516104 | tf_op jit(solution)/shard_map/ppermute | solution.py:49
  47.1 6.4 %collective-permute-start.19 = (bf16[8,3584]{1,0:T(8,128)(2,1)S(1)}, bf16[8,3584]{1,0:T(8,128)(2,1)S(1)}, u32[]{:S(2)}, u32[]{:S(2)}) collective-permute-start(bf16[8,3584]{1,0:T(8,128)(2,1)S(1)} %get-tuple-element.54), channel_id=1, source_target_pairs={{0,3},{1,2},{2,1},{3,0},{4,6},{5,7},{6,4},{7,5},{8,11},{9,10},{10,... | collective-permute-start | bytes 172040 | tf_op jit(solution)/shard_map/ppermute | solution.py:64
  49.9 4.3 %collective-permute-start.20 = (bf16[8,3584]{1,0:T(8,128)(2,1)S(1)}, bf16[8,3584]{1,0:T(8,128)(2,1)S(1)}, u32[]{:S(2)}, u32[]{:S(2)}) collective-permute-start(bf16[8,3584]{1,0:T(8,128)(2,1)S(1)} %get-tuple-element.55), channel_id=1, source_target_pairs={{0,1},{1,0},{2,3},{3,2},{4,5},{5,4},{6,7},{7,6},{8,9},{9,8},{10,11... | collective-permute-start | bytes 172040 | tf_op jit(solution)/shard_map/ppermute | solution.py:64
  49.9 5.1 %collective-permute-start.21 = (bf16[8,3584]{1,0:T(8,128)(2,1)S(1)}, bf16[8,3584]{1,0:T(8,128)(2,1)S(1)}, u32[]{:S(2)}, u32[]{:S(2)}) collective-permute-start(bf16[8,3584]{1,0:T(8,128)(2,1)S(1)} %get-tuple-element.56), channel_id=1, source_target_pairs={{0,2},{1,3},{2,0},{3,1},{4,7},{5,6},{6,5},{7,4},{8,10},{9,11},{10,... | collective-permute-start | bytes 172040 | tf_op jit(solution)/shard_map/ppermute | solution.py:64
  (7 other events, 23.8 us)

commit v7 on v5

--- a/solution.py
+++ b/solution.py
@@ -273,7 +273,7 @@
 
 def expert_kernel(rows_ref, inner_ref, outer_ref, *out_refs):
     rows = rows_ref[...]
-    tile = min(2 * HEAD_DIM, inner_ref.shape[1])
+    tile = min(4 * HEAD_DIM, inner_ref.shape[1])
     parts = []
     for c in range(0, inner_ref.shape[1], tile):
         hidden = jnp.dot(rows, inner_ref[:, c : c + tile], preferred_element_type=jnp.float32)

time: 55.8 us -> 55.8 us (level)
  no operation moved by 1% of the time
where the time goes in v7:
time: 55.8 us; the launch traced here: 55.6 us
  starting transfers between devices  23.3 us (42%)
  waiting for transfers between devices  20.9 us (37%)
  Pallas kernels  6.9 us (12%)
  local copies, waits for them, and re-layouts  2.88 us (5%)
  other arithmetic  1.34 us (2%)
    ppermute x6, waiting for transfers between devices, swap_plane(): return lax.ppermute(block, 'req', pairs)  12.6 us
    ppermute x6, starting transfers between devices, swap_exp(): return lax.ppermute(block, ('req', 'exp'), pairs)  10.2 us
    ppermute x6, starting transfers between devices, swap_plane(): return lax.ppermute(block, 'req', pairs)  7.3 us
    ppermute x6, waiting for transfers between devices, swap_exp(): return lax.ppermute(block, ('req', 'exp'), pairs)  5.9 us
    ppermute x2, starting transfers between devices, swap_ring(): return lax.ppermute(block, 'req', pairs)  3.4 us
    pallas_call x1, Pallas kernels, expert(): pl.pallas_call(expert_kernel, out_shape=out_shape, in_specs=[pl.BlockSpec...  3.06 us
    ppermute x8, starting transfers between devices, swap_group(): return lax.ppermute(block, 'req', pairs)  2.32 us
    pallas_call x1, Pallas kernels, local_attention(): pl.pallas_call(local_attention_kernel, out_shape=(part, part, part, part,...  1.92 us
  transfers between devices with their start and end apart: 22, of which 14 were waited for; matrix products, arithmetic and copies ran while one was open for 4% of the time, Pallas kernels for 3%

profile of v7, /device:TPU:0, one launch (start us, length us, event | category | flops | bytes accessed | tf_op | source)
XLA Modules:
  0.0 55.6 jit_solution(13881694076183457496)
XLA Ops:
  0.0 1.2 %copy-done = bf16[1,1,32,16,1024]{4,3,2,1,0:T(8,128)(2,1)S(1)} copy-done((bf16[1,1,32,16,1024]{4,3,2,1,0:T(8,128)(2,1)S(1)}, bf16[1,1,32,16,1024]{4,3,2,1,0:T(8,128)(2,1)}, u32[]{:S(2)}) %copy-start) | copy-done | bytes 1048600
  1.3 0.6 %send_pages.1 = (bf16[4,16,1024]{2,1,0:T(8,128)(2,1)S(1)}, bf16[4,16,1024]{2,1,0:T(8,128)(2,1)S(1)}) custom-call(s32[2,4]{1,0:T(2,128)S(1)} %bitcast.36, bf16[32,16,1024]{2,1,0:T(8,128)(2,1)S(1)} %bitcast.31, f32[8,128]{1,0:T(8,128)S(1)} %opening.1.after_ref), custom_call_target="tpu_custom_call" | custom-call | flops 4294967296 | bytes 1048576 | tf_op jit(solution)/shard_map/send_pages/pallas_call | solution.py:89
  1.9 3.4 %collective-permute-start = (bf16[64,1024]{1,0:T(8,128)(2,1)S(1)}, bf16[64,1024]{1,0:T(8,128)(2,1)S(1)}, u32[]{:S(2)}, u32[]{:S(2)}) collective-permute-start(bf16[64,1024]{1,0:T(8,128)(2,1)S(1)} %bitcast.35), channel_id=1, source_target_pairs={{4,8},{8,4},{12,16},{16,12},{20,24},{24,20},{28,0},{0,28},{5,9},{9... | collective-permute-start | bytes 393224 | tf_op jit(solution)/shard_map/ppermute | solution.py:38
  5.5 1.9 %local_attention.1 = (f32[4,56,128]{2,1,0:T(8,128)S(1)}, f32[4,56,128]{2,1,0:T(8,128)S(1)}, f32[4,56,128]{2,1,0:T(8,128)S(1)}, f32[4,56,128]{2,1,0:T(8,128)S(1)}, f32[56,128]{1,0:T(8,128)S(1)}) custom-call(s32[4,8]{1,0:T(4,128)S(1)} %copy-done.3, s32[4]{0:T(128)S(1)} %copy-done.5, s32[2,4]{1,0:T(2,128)S(1)} %bitcast.33, bf16[8,3584]{1,0:T(8,128)(2,1)S(1)} %copy-done.1, ...), custom_call_target="tpu_custom_call" | custom-call | flops 41943040 | bytes 2097152 | tf_op jit(solution)/shard_map/local_attention/pallas_call | solution.py:183
  7.4 1.1 %collective-permute-done.far_ref = bf16[64,1024]{1,0:T(8,128)(2,1)S(1)} collective-permute-done((bf16[64,1024]{1,0:T(8,128)(2,1)S(1)}, bf16[64,1024]{1,0:T(8,128)(2,1)S(1)}, u32[]{:S(2)}, u32[]{:S(2)}) %collective-permute-start) | collective-permute-done | bytes 131104 | tf_op jit(solution)/shard_map/ppermute | solution.py:38
  8.6 0.7 %arrived_attention.1 = (f32[8,3584]{1,0:T(8,128)S(1)}, bf16[8,3584]{1,0:T(8,128)(2,1)S(1)}) custom-call(bf16[8,3584]{1,0:T(8,128)(2,1)S(1)} %copy-done.6, bf16[3584]{0:T(1024)(128)(2,1)S(1)} %copy-done.7, bf16[64,1024]{1,0:T(8,128)(2,1)S(1)} %collective-permute-done.far_ref, bf16[64,1024]{1,0:T(8,128)(2,1)S(1)} %collective-permute-done.1.near_ref, ...), custom_call_target="tpu_custom_call" | custom-call | flops 1073741824 | bytes 2097152 | tf_op jit(solution)/shard_map/arrived_attention/pallas_call | solution.py:240
  9.2 5.1 %collective-permute-start.2 = (bf16[8,3584]{1,0:T(8,128)(2,1)S(1)}, bf16[8,3584]{1,0:T(8,128)(2,1)S(1)}, u32[]{:S(2)}, u32[]{:S(2)}) collective-permute-start(bf16[8,3584]{1,0:T(8,128)(2,1)S(1)} %get-tuple-element.44.refs_0_), channel_id=1, source_target_pairs={{0,3},{1,2},{2,1},{3,0},{4,6},{5,7},{6,4},{7,5},{8,11},{9,10},{10,... | collective-permute-start | bytes 172040 | tf_op jit(solution)/shard_map/ppermute | solution.py:62
  14.4 0.6 %collective-permute-start.4 = (bf16[8,3584]{1,0:T(8,128)(2,1)S(1)}, bf16[8,3584]{1,0:T(8,128)(2,1)S(1)}, u32[]{:S(2)}, u32[]{:S(2)}) collective-permute-start(bf16[8,3584]{1,0:T(8,128)(2,1)S(1)} %get-tuple-element.44.refs_0_), channel_id=1, source_target_pairs={{0,1},{1,0},{2,3},{3,2},{4,5},{5,4},{6,7},{7,6},{8,9},{9,8},{10,11... | collective-permute-start | bytes 172040 | tf_op jit(solution)/shard_map/ppermute | solution.py:62
  15.1 0.5 gather_fusion
  16.1 0.6 gather_fusion.1
  17.2 2.2 %collective-permute-done.3.refs_2_ = bf16[8,3584]{1,0:T(8,128)(2,1)S(1)} collective-permute-done((bf16[8,3584]{1,0:T(8,128)(2,1)S(1)}, bf16[8,3584]{1,0:T(8,128)(2,1)S(1)}, u32[]{:S(2)}, u32[]{:S(2)}) %collective-permute-start.3) | collective-permute-done | bytes 57376 | tf_op jit(solution)/shard_map/ppermute | solution.py:62
  19.8 1.0 %collective-permute-start.5 = (bf16[24,3584]{1,0:T(8,128)(2,1)S(1)}, bf16[24,3584]{1,0:T(8,128)(2,1)S(1)}, u32[]{:S(2)}, u32[]{:S(2)}) collective-permute-start(bf16[24,3584]{1,0:T(8,128)(2,1)S(1)} %get-tuple-element.46), channel_id=1, source_target_pairs={{0,16},{4,12},{8,24},{12,4},{16,0},{20,28},{24,8},{28,20},{1,17},{... | collective-permute-start | bytes 516104 | tf_op jit(solution)/shard_map/ppermute | solution.py:47
  20.8 1.2 %collective-permute-start.6 = (bf16[24,3584]{1,0:T(8,128)(2,1)S(1)}, bf16[24,3584]{1,0:T(8,128)(2,1)S(1)}, u32[]{:S(2)}, u32[]{:S(2)}) collective-permute-start(bf16[24,3584]{1,0:T(8,128)(2,1)S(1)} %get-tuple-element.47), channel_id=1, source_target_pairs={{0,24},{4,28},{8,16},{12,20},{16,8},{20,12},{24,0},{28,4},{1,25},{... | collective-permute-start | bytes 516104 | tf_op jit(solution)/shard_map/ppermute | solution.py:47
  22.1 1.4 %collective-permute-start.7 = (bf16[24,3584]{1,0:T(8,128)(2,1)S(1)}, bf16[24,3584]{1,0:T(8,128)(2,1)S(1)}, u32[]{:S(2)}, u32[]{:S(2)}) collective-permute-start(bf16[24,3584]{1,0:T(8,128)(2,1)S(1)} %get-tuple-element.48), channel_id=1, source_target_pairs={{0,8},{4,20},{8,0},{12,28},{16,24},{20,4},{24,16},{28,12},{1,9},{5... | collective-permute-start | bytes 516104 | tf_op jit(solution)/shard_map/ppermute | solution.py:47
  23.5 5.8 %collective-permute-done.5 = bf16[24,3584]{1,0:T(8,128)(2,1)S(1)} collective-permute-done((bf16[24,3584]{1,0:T(8,128)(2,1)S(1)}, bf16[24,3584]{1,0:T(8,128)(2,1)S(1)}, u32[]{:S(2)}, u32[]{:S(2)}) %collective-permute-start.5) | collective-permute-done | bytes 172064 | tf_op jit(solution)/shard_map/ppermute | solution.py:47
  29.3 0.6 %collective-permute-start.10 = (bf16[24,3584]{1,0:T(8,128)(2,1)S(1)}, bf16[24,3584]{1,0:T(8,128)(2,1)S(1)}, u32[]{:S(2)}, u32[]{:S(2)}) collective-permute-start(bf16[24,3584]{1,0:T(8,128)(2,1)S(1)} %collective-permute-done.6), channel_id=1, source_target_pairs={{0,4},{4,0},{8,12},{12,8},{16,20},{20,16},{24,28},{28,24},{1,5},{5... | collective-permute-start | bytes 516104 | tf_op jit(solution)/shard_map/ppermute | solution.py:52
  30.1 0.5 collective-permute-start.11
  31.0 0.7 %collective-permute-done.11 = bf16[24,3584]{1,0:T(8,128)(2,1)S(1)} collective-permute-done((bf16[24,3584]{1,0:T(8,128)(2,1)S(1)}, bf16[24,3584]{1,0:T(8,128)(2,1)S(1)}, u32[]{:S(2)}, u32[]{:S(2)}) %collective-permute-start.11) | collective-permute-done | bytes 172064 | tf_op jit(solution)/shard_map/ppermute | solution.py:52
  31.7 3.1 %expert.1 = (f32[24,3584]{1,0:T(8,128)S(1)}, f32[24,3584]{1,0:T(8,128)S(1)}, f32[24,3584]{1,0:T(8,128)S(1)}, f32[24,3584]{1,0:T(8,128)S(1)}, bf16[24,3584]{1,0:T...) custom-call(bf16[192,3584]{1,0:T(8,128)(2,1)S(1)} %constant_dynamic-updat, ...), custom_call_target="tpu_custom_call" | custom-call | flops 2818572288 | bytes 14680064 | tf_op jit(solution)/shard_map/expert/pallas_call | solution.py:294
  34.8 0.4 collective-permute-start.17
  36.3 1.0 %collective-permute-start.18 = (bf16[24,3584]{1,0:T(8,128)(2,1)S(1)}, bf16[24,3584]{1,0:T(8,128)(2,1)S(1)}, u32[]{:S(2)}, u32[]{:S(2)}) collective-permute-start(bf16[24,3584]{1,0:T(8,128)(2,1)S(1)} %add_convert_fusion), channel_id=1, source_target_pairs={{0,16},{4,12},{8,24},{12,4},{16,0},{20,28},{24,8},{28,20},{1,17},{... | collective-permute-start | bytes 516104 | tf_op jit(solution)/shard_map/ppermute | solution.py:47
  37.3 1.6 %collective-permute-start.16 = (bf16[24,3584]{1,0:T(8,128)(2,1)S(1)}, bf16[24,3584]{1,0:T(8,128)(2,1)S(1)}, u32[]{:S(2)}, u32[]{:S(2)}) collective-permute-start(bf16[24,3584]{1,0:T(8,128)(2,1)S(1)} %add_convert_fusion.1), channel_id=1, source_target_pairs={{0,24},{4,28},{8,16},{12,20},{16,8},{20,12},{24,0},{28,4},{1,25},{... | collective-permute-start | bytes 516104 | tf_op jit(solution)/shard_map/ppermute | solution.py:47
  38.9 1.1 %collective-permute-start.14 = (bf16[24,3584]{1,0:T(8,128)(2,1)S(1)}, bf16[24,3584]{1,0:T(8,128)(2,1)S(1)}, u32[]{:S(2)}, u32[]{:S(2)}) collective-permute-start(bf16[24,3584]{1,0:T(8,128)(2,1)S(1)} %add_convert_fusion.2), channel_id=1, source_target_pairs={{0,8},{4,20},{8,0},{12,28},{16,24},{20,4},{24,16},{28,12},{1,9},{5... | collective-permute-start | bytes 516104 | tf_op jit(solution)/shard_map/ppermute | solution.py:47
  40.1 5.7 %collective-permute-done.18.refs_3_ = bf16[24,3584]{1,0:T(8,128)(2,1)S(1)} collective-permute-done((bf16[24,3584]{1,0:T(8,128)(2,1)S(1)}, bf16[24,3584]{1,0:T(8,128)(2,1)S(1)}, u32[]{:S(2)}, u32[]{:S(2)}) %collective-permute-start.18) | collective-permute-done | bytes 172064 | tf_op jit(solution)/shard_map/ppermute | solution.py:47
  45.8 0.9 %collective-permute-done.14.refs_1_ = bf16[24,3584]{1,0:T(8,128)(2,1)S(1)} collective-permute-done((bf16[24,3584]{1,0:T(8,128)(2,1)S(1)}, bf16[24,3584]{1,0:T(8,128)(2,1)S(1)}, u32[]{:S(2)}, u32[]{:S(2)}) %collective-permute-start.14) | collective-permute-done | bytes 172064 | tf_op jit(solution)/shard_map/ppermute | solution.py:47
  46.7 0.4 combine.1
  47.1 2.8 %collective-permute-start.19 = (bf16[8,3584]{1,0:T(8,128)(2,1)S(1)}, bf16[8,3584]{1,0:T(8,128)(2,1)S(1)}, u32[]{:S(2)}, u32[]{:S(2)}) collective-permute-start(bf16[8,3584]{1,0:T(8,128)(2,1)S(1)} %get-tuple-element.58), channel_id=1, source_target_pairs={{0,3},{1,2},{2,1},{3,0},{4,6},{5,7},{6,4},{7,5},{8,11},{9,10},{10,... | collective-permute-start | bytes 172040 | tf_op jit(solution)/shard_map/ppermute | solution.py:62
  49.9 1.7 %collective-permute-start.21 = (bf16[8,3584]{1,0:T(8,128)(2,1)S(1)}, bf16[8,3584]{1,0:T(8,128)(2,1)S(1)}, u32[]{:S(2)}, u32[]{:S(2)}) collective-permute-start(bf16[8,3584]{1,0:T(8,128)(2,1)S(1)} %get-tuple-element.60), channel_id=1, source_target_pairs={{0,2},{1,3},{2,0},{3,1},{4,7},{5,6},{6,5},{7,4},{8,10},{9,11},{10,... | collective-permute-start | bytes 172040 | tf_op jit(solution)/shard_map/ppermute | solution.py:62
  51.6 1.9 %collective-permute-done.19 = bf16[8,3584]{1,0:T(8,128)(2,1)S(1)} collective-permute-done((bf16[8,3584]{1,0:T(8,128)(2,1)S(1)}, bf16[8,3584]{1,0:T(8,128)(2,1)S(1)}, u32[]{:S(2)}, u32[]{:S(2)}) %collective-permute-start.19) | collective-permute-done | bytes 57376 | tf_op jit(solution)/shard_map/ppermute | solution.py:62
  53.5 0.6 %collective-permute-done.20 = bf16[8,3584]{1,0:T(8,128)(2,1)S(1)} collective-permute-done((bf16[8,3584]{1,0:T(8,128)(2,1)S(1)}, bf16[8,3584]{1,0:T(8,128)(2,1)S(1)}, u32[]{:S(2)}, u32[]{:S(2)}) %collective-permute-start.20) | collective-permute-done | bytes 57376 | tf_op jit(solution)/shard_map/ppermute | solution.py:62
  54.1 0.8 %collective-permute-done.21 = bf16[8,3584]{1,0:T(8,128)(2,1)S(1)} collective-permute-done((bf16[8,3584]{1,0:T(8,128)(2,1)S(1)}, bf16[8,3584]{1,0:T(8,128)(2,1)S(1)}, u32[]{:S(2)}, u32[]{:S(2)}) %collective-permute-start.21) | collective-permute-done | bytes 57376 | tf_op jit(solution)/shard_map/ppermute | solution.py:62
  55.0 0.7 %add_convert_fusion.4 = bf16[8,3584]{1,0:T(8,128)(2,1)} fusion(bf16[8,3584]{1,0:T(8,128)(2,1)S(1)} %collective-permute-done.21, bf16[8,3584]{1,0:T(8,128)(2,1)S(1)} %collective-permute-done.20, f32[8,3584]{1,0:T(8,128)S(1)} %get-tuple-element.57, bf16[8,3584]{1,0:T(8,128)(2,1)S(1)} %collective-permute-done.19), kind=kLoop, calls=%fused_computation.6 | loop fusion | flops 200704 | bytes 344064 | tf_op jit(solution)/shard_map/convert_element_type | solution.py:413
  (86 shorter events, 3.4 us)
Async XLA Ops:
  1.2 4.2 %copy-start.1 = (bf16[8,3584]{1,0:T(8,128)(2,1)S(1)}, bf16[8,3584]{1,0:T(8,128)(2,1)}, u32[]{:S(2)}) copy-start(bf16[8,3584]{1,0:T(8,128)(2,1)} %queries_ref.1) | copy-start | bytes 172036
  1.2 4.2 %copy-start.2 = (bf16[8,1024]{1,0:T(8,128)(2,1)S(1)}, bf16[8,1024]{1,0:T(8,128)(2,1)}, u32[]{:S(2)}) copy-start(bf16[8,1024]{1,0:T(8,128)(2,1)} %fresh_ref.1) | copy-start | bytes 49156
  1.3 7.2 %copy-start.6 = (bf16[8,3584]{1,0:T(8,128)(2,1)S(1)}, bf16[8,3584]{1,0:T(8,128)(2,1)}, u32[]{:S(2)}) copy-start(bf16[8,3584]{1,0:T(8,128)(2,1)} %resid_ref.1) | copy-start | bytes 172036
  1.3 7.2 %copy-start.7 = (bf16[3584]{0:T(1024)(128)(2,1)S(1)}, bf16[3584]{0:T(1024)(128)(2,1)}, u32[]{:S(2)}) copy-start(bf16[3584]{0:T(1024)(128)(2,1)} %gain_ref.1) | copy-start | bytes 21508
  1.9 6.6 %collective-permute-start = (bf16[64,1024]{1,0:T(8,128)(2,1)S(1)}, bf16[64,1024]{1,0:T(8,128)(2,1)S(1)}, u32[]{:S(2)}, u32[]{:S(2)}) collective-permute-start(bf16[64,1024]{1,0:T(8,128)(2,1)S(1)} %bitcast.35), channel_id=1, source_target_pairs={{4,8},{8,4},{12,16},{16,12},{20,24},{24,20},{28,0},{0,28},{5,9},{9... | collective-permute-start | bytes 393224 | tf_op jit(solution)/shard_map/ppermute | solution.py:38
  5.3 3.2 %collective-permute-start.1 = (bf16[64,1024]{1,0:T(8,128)(2,1)S(1)}, bf16[64,1024]{1,0:T(8,128)(2,1)S(1)}, u32[]{:S(2)}, u32[]{:S(2)}) collective-permute-start(bf16[64,1024]{1,0:T(8,128)(2,1)S(1)} %bitcast.34), channel_id=1, source_target_pairs={{0,4},{4,0},{8,12},{12,8},{16,20},{20,16},{24,28},{28,24},{1,5},{5... | collective-permute-start | bytes 393224 | tf_op jit(solution)/shard_map/ppermute | solution.py:38
  8.5 6.5 %copy-start.9 = (s32[32,8]{0,1:T(8,128)S(1)}, s32[32,8]{0,1:T(8,128)}, u32[]{:S(2)}) copy-start(s32[32,8]{0,1:T(8,128)} %param.23) | copy-start | bytes 3076
  8.5 7.5 %copy-start.10 = (f32[32,8]{0,1:T(8,128)S(1)}, f32[32,8]{0,1:T(8,128)}, u32[]{:S(2)}) copy-start(f32[32,8]{0,1:T(8,128)} %param.24) | copy-start | bytes 3076
  9.2 8.0 %collective-permute-start.2 = (bf16[8,3584]{1,0:T(8,128)(2,1)S(1)}, bf16[8,3584]{1,0:T(8,128)(2,1)S(1)}, u32[]{:S(2)}, u32[]{:S(2)}) collective-permute-start(bf16[8,3584]{1,0:T(8,128)(2,1)S(1)} %get-tuple-element.44.refs_0_), channel_id=1, source_target_pairs={{0,3},{1,2},{2,1},{3,0},{4,6},{5,7},{6,4},{7,5},{8,11},{9,10},{10,... | collective-permute-start | bytes 172040 | tf_op jit(solution)/shard_map/ppermute | solution.py:62
  14.4 5.1 %collective-permute-start.3 = (bf16[8,3584]{1,0:T(8,128)(2,1)S(1)}, bf16[8,3584]{1,0:T(8,128)(2,1)S(1)}, u32[]{:S(2)}, u32[]{:S(2)}) collective-permute-start(bf16[8,3584]{1,0:T(8,128)(2,1)S(1)} %get-tuple-element.44.refs_0_), channel_id=1, source_target_pairs={{0,2},{1,3},{2,0},{3,1},{4,7},{5,6},{6,5},{7,4},{8,10},{9,11},{10,... | collective-permute-start | bytes 172040 | tf_op jit(solution)/shard_map/ppermute | solution.py:62
  14.4 5.1 %collective-permute-start.4 = (bf16[8,3584]{1,0:T(8,128)(2,1)S(1)}, bf16[8,3584]{1,0:T(8,128)(2,1)S(1)}, u32[]{:S(2)}, u32[]{:S(2)}) collective-permute-start(bf16[8,3584]{1,0:T(8,128)(2,1)S(1)} %get-tuple-element.44.refs_0_), channel_id=1, source_target_pairs={{0,1},{1,0},{2,3},{3,2},{4,5},{5,4},{6,7},{7,6},{8,9},{9,8},{10,11... | collective-permute-start | bytes 172040 | tf_op jit(solution)/shard_map/ppermute | solution.py:62
  16.8 14.8 %slice-start = ((s8[7340032]{0:T(1024)(128)(4,1)}), s8[4194304]{0:T(1024)(128)(4,1)S(1)}, s32[]{:S(2)}) async-start(s8[7340032]{0:T(1024)(128)(4,1)} %bitcast.25), calls=%async_computation | async-start | bytes 8388608
  16.8 14.8 %slice-start.2 = ((s8[7340032]{0:T(1024)(128)(4,1)}), s8[4194304]{0:T(1024)(128)(4,1)S(1)}, s32[]{:S(2)}) async-start(s8[7340032]{0:T(1024)(128)(4,1)} %bitcast.28), calls=%async_computation.2 | async-start | bytes 8388608
  16.9 14.7 %slice-start.1 = ((s8[7340032]{0:T(1024)(128)(4,1)}), s8[3145728]{0:T(1024)(128)(4,1)S(1)}, s32[]{:S(2)}) async-start(s8[7340032]{0:T(1024)(128)(4,1)} %bitcast.25), calls=%async_computation.1 | async-start | bytes 6291456
  17.0 14.7 %slice-start.3 = ((s8[7340032]{0:T(1024)(128)(4,1)}), s8[3145728]{0:T(1024)(128)(4,1)S(1)}, s32[]{:S(2)}) async-start(s8[7340032]{0:T(1024)(128)(4,1)} %bitcast.28), calls=%async_computation.3 | async-start | bytes 6291456
  19.8 9.5 %collective-permute-start.5 = (bf16[24,3584]{1,0:T(8,128)(2,1)S(1)}, bf16[24,3584]{1,0:T(8,128)(2,1)S(1)}, u32[]{:S(2)}, u32[]{:S(2)}) collective-permute-start(bf16[24,3584]{1,0:T(8,128)(2,1)S(1)} %get-tuple-element.46), channel_id=1, source_target_pairs={{0,16},{4,12},{8,24},{12,4},{16,0},{20,28},{24,8},{28,20},{1,17},{... | collective-permute-start | bytes 516104 | tf_op jit(solution)/shard_map/ppermute | solution.py:47
  20.8 9.8 %collective-permute-start.8 = (bf16[24,3584]{1,0:T(8,128)(2,1)S(1)}, bf16[24,3584]{1,0:T(8,128)(2,1)S(1)}, u32[]{:S(2)}, u32[]{:S(2)}) collective-permute-start(bf16[24,3584]{1,0:T(8,128)(2,1)S(1)} %get-tuple-element.45), channel_id=1, source_target_pairs={{0,4},{4,0},{8,12},{12,8},{16,20},{20,16},{24,28},{28,24},{1,5},{5... | collective-permute-start | bytes 516104 | tf_op jit(solution)/shard_map/ppermute | solution.py:52
  20.8 8.5 %collective-permute-start.6 = (bf16[24,3584]{1,0:T(8,128)(2,1)S(1)}, bf16[24,3584]{1,0:T(8,128)(2,1)S(1)}, u32[]{:S(2)}, u32[]{:S(2)}) collective-permute-start(bf16[24,3584]{1,0:T(8,128)(2,1)S(1)} %get-tuple-element.47), channel_id=1, source_target_pairs={{0,24},{4,28},{8,16},{12,20},{16,8},{20,12},{24,0},{28,4},{1,25},{... | collective-permute-start | bytes 516104 | tf_op jit(solution)/shard_map/ppermute | solution.py:47
  22.1 8.0 %collective-permute-start.7 = (bf16[24,3584]{1,0:T(8,128)(2,1)S(1)}, bf16[24,3584]{1,0:T(8,128)(2,1)S(1)}, u32[]{:S(2)}, u32[]{:S(2)}) collective-permute-start(bf16[24,3584]{1,0:T(8,128)(2,1)S(1)} %get-tuple-element.48), channel_id=1, source_target_pairs={{0,8},{4,20},{8,0},{12,28},{16,24},{20,4},{24,16},{28,12},{1,9},{5... | collective-permute-start | bytes 516104 | tf_op jit(solution)/shard_map/ppermute | solution.py:47
  29.3 1.4 %collective-permute-start.9 = (bf16[24,3584]{1,0:T(8,128)(2,1)S(1)}, bf16[24,3584]{1,0:T(8,128)(2,1)S(1)}, u32[]{:S(2)}, u32[]{:S(2)}) collective-permute-start(bf16[24,3584]{1,0:T(8,128)(2,1)S(1)} %collective-permute-done.5), channel_id=1, source_target_pairs={{0,4},{4,0},{8,12},{12,8},{16,20},{20,16},{24,28},{28,24},{1,5},{5... | collective-permute-start | bytes 516104 | tf_op jit(solution)/shard_map/ppermute | solution.py:52
  29.3 1.6 %collective-permute-start.10 = (bf16[24,3584]{1,0:T(8,128)(2,1)S(1)}, bf16[24,3584]{1,0:T(8,128)(2,1)S(1)}, u32[]{:S(2)}, u32[]{:S(2)}) collective-permute-start(bf16[24,3584]{1,0:T(8,128)(2,1)S(1)} %collective-permute-done.6), channel_id=1, source_target_pairs={{0,4},{4,0},{8,12},{12,8},{16,20},{20,16},{24,28},{28,24},{1,5},{5... | collective-permute-start | bytes 516104 | tf_op jit(solution)/shard_map/ppermute | solution.py:52
  30.1 1.6 %collective-permute-start.11 = (bf16[24,3584]{1,0:T(8,128)(2,1)S(1)}, bf16[24,3584]{1,0:T(8,128)(2,1)S(1)}, u32[]{:S(2)}, u32[]{:S(2)}) collective-permute-start(bf16[24,3584]{1,0:T(8,128)(2,1)S(1)} %collective-permute-done.7), channel_id=1, source_target_pairs={{0,4},{4,0},{8,12},{12,8},{16,20},{20,16},{24,28},{28,24},{1,5},{5... | collective-permute-start | bytes 516104 | tf_op jit(solution)/shard_map/ppermute | solution.py:52
  34.8 1.5 %collective-permute-start.17 = (bf16[24,3584]{1,0:T(8,128)(2,1)S(1)}, bf16[24,3584]{1,0:T(8,128)(2,1)S(1)}, u32[]{:S(2)}, u32[]{:S(2)}) collective-permute-start(bf16[24,3584]{1,0:T(8,128)(2,1)S(1)} %get-tuple-element.56), channel_id=1, source_target_pairs={{0,4},{4,0},{8,12},{12,8},{16,20},{20,16},{24,28},{28,24},{1,5},{5... | collective-permute-start | bytes 516104 | tf_op jit(solution)/shard_map/ppermute | solution.py:52
  35.2 2.0 %collective-permute-start.15 = (bf16[24,3584]{1,0:T(8,128)(2,1)S(1)}, bf16[24,3584]{1,0:T(8,128)(2,1)S(1)}, u32[]{:S(2)}, u32[]{:S(2)}) collective-permute-start(bf16[24,3584]{1,0:T(8,128)(2,1)S(1)} %get-tuple-element.54), channel_id=1, source_target_pairs={{0,4},{4,0},{8,12},{12,8},{16,20},{20,16},{24,28},{28,24},{1,5},{5... | collective-permute-start | bytes 516104 | tf_op jit(solution)/shard_map/ppermute | solution.py:52
  35.4 3.5 %collective-permute-start.13 = (bf16[24,3584]{1,0:T(8,128)(2,1)S(1)}, bf16[24,3584]{1,0:T(8,128)(2,1)S(1)}, u32[]{:S(2)}, u32[]{:S(2)}) collective-permute-start(bf16[24,3584]{1,0:T(8,128)(2,1)S(1)} %get-tuple-element.52), channel_id=1, source_target_pairs={{0,4},{4,0},{8,12},{12,8},{16,20},{20,16},{24,28},{28,24},{1,5},{5... | collective-permute-start | bytes 516104 | tf_op jit(solution)/shard_map/ppermute | solution.py:52
  35.8 4.3 %collective-permute-start.12 = (bf16[24,3584]{1,0:T(8,128)(2,1)S(1)}, bf16[24,3584]{1,0:T(8,128)(2,1)S(1)}, u32[]{:S(2)}, u32[]{:S(2)}) collective-permute-start(bf16[24,3584]{1,0:T(8,128)(2,1)S(1)} %get-tuple-element.50), channel_id=1, source_target_pairs={{0,4},{4,0},{8,12},{12,8},{16,20},{20,16},{24,28},{28,24},{1,5},{5... | collective-permute-start | bytes 516104 | tf_op jit(solution)/shard_map/ppermute | solution.py:52
  36.3 9.5 %collective-permute-start.18 = (bf16[24,3584]{1,0:T(8,128)(2,1)S(1)}, bf16[24,3584]{1,0:T(8,128)(2,1)S(1)}, u32[]{:S(2)}, u32[]{:S(2)}) collective-permute-start(bf16[24,3584]{1,0:T(8,128)(2,1)S(1)} %add_convert_fusion), channel_id=1, source_target_pairs={{0,16},{4,12},{8,24},{12,4},{16,0},{20,28},{24,8},{28,20},{1,17},{... | collective-permute-start | bytes 516104 | tf_op jit(solution)/shard_map/ppermute | solution.py:47
  37.3 8.5 %collective-permute-start.16 = (bf16[24,3584]{1,0:T(8,128)(2,1)S(1)}, bf16[24,3584]{1,0:T(8,128)(2,1)S(1)}, u32[]{:S(2)}, u32[]{:S(2)}) collective-permute-start(bf16[24,3584]{1,0:T(8,128)(2,1)S(1)} %add_convert_fusion.1), channel_id=1, source_target_pairs={{0,24},{4,28},{8,16},{12,20},{16,8},{20,12},{24,0},{28,4},{1,25},{... | collective-permute-start | bytes 516104 | tf_op jit(solution)/shard_map/ppermute | solution.py:47
  38.9 7.8 %collective-permute-start.14 = (bf16[24,3584]{1,0:T(8,128)(2,1)S(1)}, bf16[24,3584]{1,0:T(8,128)(2,1)S(1)}, u32[]{:S(2)}, u32[]{:S(2)}) collective-permute-start(bf16[24,3584]{1,0:T(8,128)(2,1)S(1)} %add_convert_fusion.2), channel_id=1, source_target_pairs={{0,8},{4,20},{8,0},{12,28},{16,24},{20,4},{24,16},{28,12},{1,9},{5... | collective-permute-start | bytes 516104 | tf_op jit(solution)/shard_map/ppermute | solution.py:47
  47.1 6.4 %collective-permute-start.19 = (bf16[8,3584]{1,0:T(8,128)(2,1)S(1)}, bf16[8,3584]{1,0:T(8,128)(2,1)S(1)}, u32[]{:S(2)}, u32[]{:S(2)}) collective-permute-start(bf16[8,3584]{1,0:T(8,128)(2,1)S(1)} %get-tuple-element.58), channel_id=1, source_target_pairs={{0,3},{1,2},{2,1},{3,0},{4,6},{5,7},{6,4},{7,5},{8,11},{9,10},{10,... | collective-permute-start | bytes 172040 | tf_op jit(solution)/shard_map/ppermute | solution.py:62
  49.9 4.2 %collective-permute-start.20 = (bf16[8,3584]{1,0:T(8,128)(2,1)S(1)}, bf16[8,3584]{1,0:T(8,128)(2,1)S(1)}, u32[]{:S(2)}, u32[]{:S(2)}) collective-permute-start(bf16[8,3584]{1,0:T(8,128)(2,1)S(1)} %get-tuple-element.59), channel_id=1, source_target_pairs={{0,1},{1,0},{2,3},{3,2},{4,5},{5,4},{6,7},{7,6},{8,9},{9,8},{10,11... | collective-permute-start | bytes 172040 | tf_op jit(solution)/shard_map/ppermute | solution.py:62
  49.9 5.1 %collective-permute-start.21 = (bf16[8,3584]{1,0:T(8,128)(2,1)S(1)}, bf16[8,3584]{1,0:T(8,128)(2,1)S(1)}, u32[]{:S(2)}, u32[]{:S(2)}) collective-permute-start(bf16[8,3584]{1,0:T(8,128)(2,1)S(1)} %get-tuple-element.60), channel_id=1, source_target_pairs={{0,2},{1,3},{2,0},{3,1},{4,7},{5,6},{6,5},{7,4},{8,10},{9,11},{10,... | collective-permute-start | bytes 172040 | tf_op jit(solution)/shard_map/ppermute | solution.py:62
  (7 other events, 23.2 us)
